TPU v7x, 512 devices: a whole 4x4x16 slice. The times are simulated.
512 devices in a mesh: dp: 128 (over z, y, core), mp: 4 (over x).
Axes of the slice: x: 4, y: 4, z: 16, core: 2. Of those that a mesh axis runs over, the one named last changes fastest.
Arguments:
- x_work: bfloat16 [49152, 1280], P('dp', 'mp'), may hold values from -14 to 14
- norm_gain: bfloat16 [1280], P('mp'), may hold values from 0.099609375 to 1.8984375
- w_qkv: bfloat16 [1280, 1920], P(None, 'mp'), may hold values from -0.2934839 to 0.2934839
- w_out: bfloat16 [640, 1280], P('mp'), may hold values from -0.9373467 to 0.9373467
- cot_owned: bfloat16 [90112, 1280], P('dp', 'mp'), may hold values from -10.5 to 10.5
- counts: int32 [128], replicated, may hold values from 1 to 11, as said below
Outputs:
- y_owned: bfloat16 [90112, 1280], P('dp', 'mp')
- x_grad: bfloat16 [49152, 1280], P('dp', 'mp')
- qkv_grad: float32 [1280, 1920], P(None, 'mp')
- out_grad: float32 [640, 1280], P('mp')
- gain_grad: float32 [1280], P('mp')
Inputs may be any that keep to these rules, and one draw needn't show every extreme that they name: Live slots of an owner are its first counts[o] slots; with P[o] = starts[o] - o * 6, every P[o] lies in 0 .. 5 and P[0] = 0; the counts sum to 768.
All inputs are finite; a program needn't handle non-finite values.
Results may differ from a plain program's by a relative error of at most 0.0077.
Values may be sent and summed in bfloat16 or wider, within the bound.
No kernel may reach another device: no remote copies, remote signals or barrier semaphores. Data moves between devices by JAX's collectives and lax.ppermute only.
A program may use at most 64 MiB of HBM per device.

v0:
```python
import jax
import jax.numpy as jnp
from jax import lax
from jax.sharding import PartitionSpec as P

HD = 80
WIN = 64


epsilon = 1e-06


def passed_along(shard, axis, by):
    devices = lax.axis_size(axis)
    pairs = [(i, i + by) for i in range(devices) if 0 <= i + by < devices]
    return lax.ppermute(shard, axis, pairs)


def split_heads(packed, window_count, heads_here):
    grid = packed.reshape(window_count, WIN, heads_here, 3, HD)
    return (grid[:, :, :, 0], grid[:, :, :, 1], grid[:, :, :, 2])


def shards(x_work, norm_gain, w_qkv, w_out, cot_owned, counts):
    my_rank = lax.axis_index("dp")
    mp_index = lax.axis_index("mp")
    row_count, feat_width = x_work.shape
    window_count = row_count // WIN
    slot_count = cot_owned.shape[0] // WIN
    heads_here = w_qkv.shape[1] // (3 * HD)
    count_ends = jnp.cumsum(counts)
    my_start = count_ends[my_rank] - counts[my_rank]
    drift = my_start - my_rank * window_count
    kept_slots = window_count - drift
    cot_windows = cot_owned.reshape(slot_count, WIN, feat_width)
    send_cot = lax.dynamic_slice_in_dim(cot_windows, kept_slots, window_count - 1, 0)
    got_cot = passed_along(send_cot, "dp", 1)
    turns = jnp.arange(window_count, dtype=jnp.int32)
    own_pick = jnp.clip(turns - drift, 0, slot_count - 1)
    near_pick = jnp.clip(turns, 0, window_count - 2)
    cot_work = jnp.where((turns < drift)[:, None, None], got_cot[near_pick], cot_windows[own_pick])
    cot_work = cot_work.reshape(row_count, feat_width)
    x_full, gain_full = (
        lax.all_gather(x_work, "mp", axis=1, tiled=True),
        lax.all_gather(norm_gain, "mp", axis=0, tiled=True),
    )
    x_float = x_full.astype(jnp.float32)
    inverse_rms = lax.rsqrt(jnp.mean(x_float * x_float, axis=1, keepdims=True) + epsilon)
    x_hat = x_float * inverse_rms
    normed = (x_hat * gain_full.astype(jnp.float32)).astype(jnp.bfloat16)
    packed = jnp.dot(normed, w_qkv, preferred_element_type=jnp.float32).astype(jnp.bfloat16)
    queries, key_heads, value_heads = split_heads(packed, window_count, heads_here)
    scores = jnp.einsum(
        "wqhd,wkhd->whqk", queries, key_heads, preferred_element_type=jnp.float32
    ) * HD ** (-0.5)
    probabilities = jax.nn.softmax(scores, axis=-1)
    weights = probabilities.astype(jnp.bfloat16)
    mixed_heads = jnp.einsum(
        "whqk,wkhd->wqhd", weights, value_heads, preferred_element_type=jnp.float32
    )
    mixed_heads = mixed_heads.astype(jnp.bfloat16).reshape(row_count, heads_here * HD)
    branch_part = jnp.dot(mixed_heads, w_out, preferred_element_type=jnp.float32)
    branch = lax.psum_scatter(branch_part, "mp", scatter_dimension=1, tiled=True)
    y_work = (x_work.astype(jnp.float32) + branch).astype(jnp.bfloat16)
    y_windows = y_work.reshape(window_count, WIN, feat_width)
    got_rows = passed_along(y_windows[: window_count - 1], "dp", -1)
    slot_ids = jnp.arange(slot_count, dtype=jnp.int32)
    local_pick = jnp.clip(slot_ids + drift, 0, window_count - 1)
    far_pick = jnp.clip(slot_ids - kept_slots, 0, window_count - 2)
    y_owned = jnp.where(
        (slot_ids < kept_slots)[:, None, None], y_windows[local_pick], got_rows[far_pick]
    )
    y_owned = jnp.where(
        (slot_ids < counts[my_rank])[:, None, None], y_owned, jnp.zeros((), jnp.bfloat16)
    )
    y_owned = y_owned.reshape(slot_count * WIN, feat_width)
    cot_full = lax.all_gather(cot_work, "mp", axis=1, tiled=True)
    out_grad = jnp.dot(mixed_heads.T, cot_full, preferred_element_type=jnp.float32)
    grad_mixed = jnp.dot(cot_full, w_out.T, preferred_element_type=jnp.float32).astype(jnp.bfloat16)
    grad_mixed = grad_mixed.reshape(window_count, WIN, heads_here, HD)
    grad_weights = jnp.einsum(
        "wqhd,wkhd->whqk", grad_mixed, value_heads, preferred_element_type=jnp.float32
    )
    grad_values = jnp.einsum(
        "whqk,wqhd->wkhd", weights, grad_mixed, preferred_element_type=jnp.float32
    )
    grad_scores = (
        probabilities
        * (grad_weights - jnp.sum(grad_weights * probabilities, axis=-1, keepdims=True))
        * HD ** (-0.5)
    )
    grad_query = jnp.einsum("whqk,wkhd->wqhd", grad_scores, key_heads.astype(jnp.float32))
    grad_keys = jnp.einsum("whqk,wqhd->wkhd", grad_scores, queries.astype(jnp.float32))
    grad_packed = jnp.stack([grad_query, grad_keys, grad_values], axis=3)
    grad_packed = grad_packed.reshape(row_count, heads_here * 3 * HD).astype(jnp.bfloat16)
    qkv_grad = jnp.dot(normed.T, grad_packed, preferred_element_type=jnp.float32)
    normed_part = jnp.dot(grad_packed, w_qkv.T, preferred_element_type=jnp.float32)
    grad_normed = lax.psum_scatter(normed_part, "mp", scatter_dimension=1, tiled=True)
    x_slice = lax.dynamic_slice_in_dim(x_hat, mp_index * feat_width, feat_width, 1)
    scaled = grad_normed * norm_gain.astype(jnp.float32)
    row_total = lax.psum(jnp.sum(scaled * x_slice, axis=1), "mp")
    row_dot = row_total[:, None] / x_full.shape[1]
    x_grad = (cot_work.astype(jnp.float32) + inverse_rms * (scaled - x_slice * row_dot)).astype(
        jnp.bfloat16
    )
    gain_part = jnp.sum(grad_normed * x_slice, axis=0)
    qkv_grad, out_grad, gain_grad = lax.psum((qkv_grad, out_grad, gain_part), "dp")
    return (y_owned, x_grad, qkv_grad, out_grad, gain_grad)


def solution(mesh):
    return jax.shard_map(
        shards,
        mesh=mesh,
        in_specs=(P("dp", "mp"), P("mp"), P(None, "mp"), P("mp", None), P("dp", "mp"), P()),
        out_specs=(P("dp", "mp"), P("dp", "mp"), P(None, "mp"), P("mp", None), P("mp")),
        check_vma=False,
    )
```

profile of v0, /device:TPU:1, one launch (start us, length us, event | category | flops | bytes accessed | tf_op | source)
XLA Modules:
  0.0 470.7 jit_solution(3209574865920395613)
XLA Ops:
  8.1 1.4 dynamic-slice.1
  10.1 0.9 dynamic-update-slice
  11.0 9.3 %all-reduce = bf16[1280]{0:T(1024)(128)(2,1)S(1)} all-reduce(bf16[1280]{0:T(1024)(128)(2,1)S(1)} %dynamic-update-slice), channel_id=1, replica_groups=mesh['dp'=128,'mp'=4] {'mp'}, use_global_device_ids=true, to_apply=%add | all-reduce | flops 1280 | bytes 5120
  20.3 12.4 %all_gather.9 = bf16[384,1280]{0,1:T(8,128)(2,1)S(1)} all-gather(bf16[384,320]{0,1:T(8,128)(2,1)} %param.6), channel_id=1, replica_groups=mesh['dp'=128,'mp'=4] {'mp'}, dimensions={1}, use_global_device_ids=true | all-gather | bytes 1228800 | tf_op jit(solution)/shard_map/all_gather | solution.py:44
  32.9 1.6 convolution_convert_fusion
  34.5 1.6 reshape.186
  36.1 1.0 fusion.35
  37.1 1.2 copy.43
  38.3 1.2 copy.45
  39.6 0.9 copy.44
  40.5 1.2 fusion.36
  42.6 1.9 fusion.41
  44.9 0.6 dynamic_slice.13
  45.5 0.5 constant_dynamic-slice_fusion.1
  47.3 0.3 copy.28
  47.7 7.3 %collective-permute-start.1 = (bf16[5,64,320]{2,1,0:T(8,128)(2,1)S(1)}, bf16[5,64,320]{2,1,0:T(8,128)(2,1)S(1)}, u32[]{:S(2)}, u32[]{:S(2)}) collective-permute-start(bf16[5,64,320]{2,1,0:T(8,128)(2,1)S(1)} %constant_dynamic-slice_fusion), channel_id=1, source_target_pairs={{0,4},{4,8},{8,12},{12,16},{16,20},{20,24},{24,28},{28,32},{32,36}... | collective-permute-start | bytes 614408 | tf_op jit(solution)/shard_map/ppermute | solution.py:16
  55.1 0.6 gather_fusion.3
  56.1 2.1 collective-permute-done.1
  58.1 0.6 gather_fusion.2
  59.0 14.6 %all_gather.11 = bf16[384,1280]{0,1:T(8,128)(2,1)S(1)} all-gather(bf16[384,320]{0,1:T(8,128)(2,1)S(1)} %broadcast_select_fusion), channel_id=1, replica_groups=mesh['dp'=128,'mp'=4] {'mp'}, dimensions={1}, use_global_device_ids=true | all-gather | bytes 1228800 | tf_op jit(solution)/shard_map/all_gather | solution.py:77
  73.6 2.0 convolution_convert_fusion.5
  75.6 1.8 reshape.187
  77.5 1.8 copy.32
  79.3 1.3 fusion.7
  80.6 1.5 multiply_reduce_fusion.2
  82.8 1.4 copy.35
  84.1 2.5 convert_element_type.56
  86.6 3.2 fusion.42
  90.1 1.4 convert_multiply_fusion
  91.5 1.4 fusion.43
  92.9 2.4 fusion.9
  95.3 0.7 iota_compare_fusion.2
  96.2 1.1 add_convert_fusion.1
  97.3 0.9 copy.27
  98.2 4.2 collective-permute-start
  102.6 1.5 gather_fusion
  104.1 5.7 %collective-permute-done = bf16[5,64,320]{2,1,0:T(8,128)(2,1)} collective-permute-done((bf16[5,64,320]{2,1,0:T(8,128)(2,1)}, bf16[5,64,320]{2,1,0:T(8,128)(2,1)}, u32[]{:S(2)}, u32[]{:S(2)}) %collective-permute-start) | collective-permute-done | bytes 204832 | tf_op jit(solution)/shard_map/ppermute | solution.py:16
  109.8 2.4 gather_fusion.1
  112.2 2.3 fusion.8
  114.5 2.2 copy.36
  116.7 18.1 %reduce-scatter.5.cloned.1.call-done = f32[384,320]{0,1:T(8,128)} async-done(((f32[384,1280]{0,1:T(8,128)}), f32[384,320]{0,1:T(8,128)}) %reduce-scatter.5.cloned.1.call-update) | async-done | bytes 491536 | tf_op jit(solution)/shard_map/reduce_scatter | solution.py:98
  134.8 1.2 multiply_reduce_fusion
  136.0 248.7 %psum.31 = f32[320]{0:T(512)} all-reduce(f32[320]{0:T(512)S(1)} %get-tuple-element.10), channel_id=1, replica_groups=mesh['dp'=128,'mp'=4] {'dp'}, use_global_device_ids=true, to_apply=%region_12.13 | all-reduce | flops 320 | bytes 2560 | tf_op jit(solution)/shard_map/psum | solution.py:107
  384.7 7.0 %psum.28 = f32[384]{0:T(512)S(1)} all-reduce(f32[384]{0:T(512)S(1)} %get-tuple-element.11), channel_id=1, replica_groups=mesh['dp'=128,'mp'=4] {'mp'}, use_global_device_ids=true, to_apply=%region_8.9 | all-reduce | flops 384 | bytes 3072 | tf_op jit(solution)/shard_map/psum | solution.py:101
  391.7 1.9 add_convert_fusion
  393.6 65.4 %all-reduce.4.cloned.1.call-done = (f32[1280,480]{0,1:T(8,128)}, f32[160,1280]{1,0:T(8,128)}) async-done(((f32[1280,480]{0,1:T(8,128)}, f32[160,1280]{1,0:T(8,128)}), (f32[1280,480]{0,1:T(8,128)}, f32[160,1280]{1,0:T(8,128)})) %all-reduce.4.cloned.1.call-update) | async-done | bytes 3276816 | tf_op jit(solution)/shard_map/psum | solution.py:107
  459.0 3.4 copy.49
  462.4 0.9 copy.50
  (80 shorter events, 3.6 us)
Async XLA Ops:
  8.0 24.9 %copy-start = (bf16[1280,480]{0,1:T(8,128)(2,1)S(1)}, bf16[1280,480]{0,1:T(8,128)(2,1)}, u32[]{:S(2)}) copy-start(bf16[1280,480]{0,1:T(8,128)(2,1)} %param.8) | copy-start | bytes 3686404
  8.0 88.2 %reduce-scatter.3.cloned.1.call-start = ((), (), s32[]{:S(2)}) async-start(), calls=%async_computation.2 | async-start | bytes 2457600 | tf_op jit(solution)/shard_map/reduce_scatter | solution.py:63
  38.3 3.4 copy-start.11
  39.6 2.2 copy-start.9
  39.6 3.0 copy-start.5
  41.7 0.8 copy-start.15
  41.7 2.8 copy-start.17
  42.6 2.0 copy-start.3
  42.6 2.0 copy-start.14
  42.6 4.7 copy-start.8
  44.6 90.2 %reduce-scatter.5.cloned.1.call-start = ((), (), s32[]{:S(2)}) async-start(), calls=%async_computation.3 | async-start | bytes 2457600 | tf_op jit(solution)/shard_map/reduce_scatter | solution.py:98
  47.7 10.5 %collective-permute-start.1 = (bf16[5,64,320]{2,1,0:T(8,128)(2,1)S(1)}, bf16[5,64,320]{2,1,0:T(8,128)(2,1)S(1)}, u32[]{:S(2)}, u32[]{:S(2)}) collective-permute-start(bf16[5,64,320]{2,1,0:T(8,128)(2,1)S(1)} %constant_dynamic-slice_fusion), channel_id=1, source_target_pairs={{0,4},{4,8},{8,12},{12,16},{16,20},{20,24},{24,28},{28,32},{32,36}... | collective-permute-start | bytes 614408 | tf_op jit(solution)/shard_map/ppermute | solution.py:16
  59.0 20.3 %copy-start.18 = (f32[6,2,64]{2,1,0:T(2,128)S(1)}, f32[6,2,64]{2,1,0:T(2,128)}, u32[]{:S(2)}) copy-start(f32[6,2,64]{2,1,0:T(2,128)} %copy-done.17) | copy-start | bytes 9220
  79.3 2.8 copy-start.12
  79.3 2.8 copy-start.16
  80.6 1.7 copy-start.10
  86.6 3.3 copy-start.13
  89.8 369.2 %all-reduce.4.cloned.1.call-start = ((), (), s32[]{:S(2)}) async-start(), calls=%async_computation.4 | async-start | bytes 6553600 | tf_op jit(solution)/shard_map/psum | solution.py:107
  90.1 1.4 copy-start.4
  90.1 2.8 copy-start.2
  95.3 0.9 copy-start.6
  98.2 11.7 %collective-permute-start = (bf16[5,64,320]{2,1,0:T(8,128)(2,1)}, bf16[5,64,320]{2,1,0:T(8,128)(2,1)}, u32[]{:S(2)}, u32[]{:S(2)}) collective-permute-start(bf16[5,64,320]{2,1,0:T(8,128)(2,1)} %bitcast.11), channel_id=1, source_target_pairs={{4,0},{8,4},{12,8},{16,12},{20,16},{24,20},{28,24},{32,28},{36,32}... | collective-permute-start | bytes 614408 | tf_op jit(solution)/shard_map/ppermute | solution.py:16
  104.1 30.7 %copy-start.1 = (f32[384,1280]{0,1:T(8,128)S(1)}, f32[384,1280]{0,1:T(8,128)}, u32[]{:S(2)}) copy-start(f32[384,1280]{0,1:T(8,128)} %convert_multiply_fusion) | copy-start | bytes 5898244
  459.0 3.4 copy-start.7
Sparse Core Ops, SparseCore 0:
  44.7 44.9 reduce-scatter.2
  92.6 42.1 reduce-scatter.4
Sparse Core Ops, SparseCore 1:
  95.4 363.5 all-reduce.3
where the time goes:
time: 472 us; the launch traced here: 471 us
  blocking collectives  292 us (62%)
  waiting for transfers between devices  91.4 us (19%)
  local copies, waits for them, and re-layouts  31.4 us (7%)
  between operations  17.8 us (4%)
  matrix products  17.3 us (4%)
  starting transfers between devices  11.7 us (2%)
  other arithmetic  9.24 us (2%)
    psum x1, blocking collectives, shards(): lax.psum((qkv_grad, out_grad, gain_part), 'dp')  249 us
    psum x1, waiting for transfers between devices, shards(): lax.psum((qkv_grad, out_grad, gain_part), 'dp')  65.4 us
    reduce_scatter x1, waiting for transfers between devices, shards(): lax.psum_scatter(normed_part, 'mp', scatter_dimension=1, tiled=True)  18.1 us
    all_gather x1, blocking collectives, shards(): cot_full = lax.all_gather(cot_work, 'mp', axis=1, tiled=True)  14.6 us
    unnamed x48, local copies, waits for them, and re-layouts  12.6 us
    all_gather x1, blocking collectives, shards(): lax.all_gather(x_work, 'mp', axis=1, tiled=True)  12.4 us
    ppermute x2, starting transfers between devices, passed_along(): return lax.ppermute(shard, axis, pairs)  11.5 us
  transfers between devices with their start and end apart: 5, of which 4 were waited for; matrix products, arithmetic and copies ran while one was open for 8% of the time, Pallas kernels for 0%

commit v1 on v0

v1 whole, which is shorter than its diff:
```python
import jax
import jax.numpy as jnp
from jax import lax
from jax.experimental import pallas as pl
from jax.experimental.pallas import tpu as pltpu
from jax.sharding import Mesh, PartitionSpec as P

HD = 80
WIN = 64
W_DEV = 6
epsilon = 1e-06

F32 = jnp.float32
BF16 = jnp.bfloat16
DP = ("zh", "zl", "y", "c")

FEAT = 1280
ROWS = 384
FX = 320
QKV = 480
ATT = 160
HEADS = 2
SLOTS = 704
PASS = 320
GROWS = 336

HALF = 25600
Y_LANES = 6400
Z_LANES = 1664
TILE = 128

VMEM = pl.BlockSpec(memory_space=pltpu.VMEM)


def call(kernel, out_shapes, scratch=(), vmem_mib=24, flops=1000000):
    return pl.pallas_call(
        kernel,
        out_shape=out_shapes,
        scratch_shapes=list(scratch),
        compiler_params=pltpu.CompilerParams(vmem_limit_bytes=vmem_mib * 1024 * 1024),
        cost_estimate=pl.CostEstimate(flops=flops, bytes_accessed=1000000, transcendentals=0),
    )


def struct(shape, dtype):
    return jax.ShapeDtypeStruct(shape, dtype)


def drift_of(counts_row, rank):
    owners = lax.broadcasted_iota(jnp.int32, counts_row.shape, 1)
    before = jnp.sum(jnp.where(owners < rank, counts_row, 0), axis=1, keepdims=True)
    return before - rank * W_DEV


def one_hot(rows, cols, shift):
    r = lax.broadcasted_iota(jnp.int32, (rows, cols), 0)
    c = lax.broadcasted_iota(jnp.int32, (rows, cols), 1)
    return jnp.where(r == c + shift, 1.0, 0.0).astype(BF16)


def dot(a, b, dims):
    return lax.dot_general(a, b, ((dims[:1], dims[1:]), ((), ())), preferred_element_type=F32)


def route_send(counts_ref, cot_ref, send_ref):
    rank = lax.axis_index(DP)
    drift = drift_of(counts_ref[...], rank)
    pick = one_hot(SLOTS, PASS, (W_DEV - drift) * WIN)
    send_ref[...] = dot(cot_ref[...], pick, (1, 0)).astype(BF16)


def route_in(counts_ref, gain_ref, cot_ref, got_ref, out_ref):
    rank = lax.axis_index(DP)
    drift = drift_of(counts_ref[...], rank) * WIN
    own = dot(cot_ref[:, :ROWS], one_hot(ROWS, ROWS, -drift), (1, 0))
    col = lax.broadcasted_iota(jnp.int32, (PASS, ROWS), 1)
    row = lax.broadcasted_iota(jnp.int32, (PASS, ROWS), 0)
    near = jnp.where((row == col) & (col < drift), 1.0, 0.0).astype(BF16)
    out_ref[:FX, :] = (own + dot(got_ref[...], near, (1, 0))).astype(BF16)
    out_ref[FX:, :] = jnp.zeros((GROWS - FX, ROWS), BF16)
    out_ref[FX:, :FX] = jnp.broadcast_to(gain_ref[...], (GROWS - FX, FX))


def block(x_ref, g_ref, wq_ref, wo_ref, mp_ref, send_ref, keep_ref, gcol, nrm, gt, pk, gm, mx, gp, part, dsum):
    core = lax.axis_index("c")
    r_i = lax.broadcasted_iota(jnp.int32, (FX, ROWS), 0)
    c_i = lax.broadcasted_iota(jnp.int32, (FX, ROWS), 1)
    for j in range(4):
        gt[FX * j:FX * (j + 1), :] = g_ref[j, :FX, :]
        row = g_ref[j, FX:GROWS, :].astype(F32)[:1, :]
        gcol[FX * j:FX * (j + 1), :] = jnp.sum(jnp.where(r_i == c_i, row, 0.0), axis=1, keepdims=True)
    total = jnp.zeros((8, ROWS), F32)
    for i in range(16):
        x = x_ref[80 * i:80 * (i + 1), :].astype(F32)
        total += jnp.sum((x * x).reshape(10, 8, ROWS), axis=0)
    rms = lax.rsqrt(jnp.sum(total, axis=0, keepdims=True) / FEAT + epsilon)
    for i in range(16):
        s = slice(80 * i, 80 * (i + 1))
        nrm[s, :] = ((x_ref[s, :].astype(F32) * rms) * gcol[s, :]).astype(BF16)
    pk[...] = dot(wq_ref[...], nrm[...], (1, 0)).astype(BF16)
    gm[...] = dot(wo_ref[...], gt[...], (1, 0)).astype(BF16)
    qi = lax.broadcasted_iota(jnp.int32, (128, 128), 0)
    ki = lax.broadcasted_iota(jnp.int32, (128, 128), 1)
    same = (qi < WIN) == (ki < WIN)
    scale = HD ** (-0.5)
    for h in range(HEADS):
        for p in range(3):
            c = slice(128 * p, 128 * (p + 1))
            b = 3 * HD * h
            q, k, v = (pk[b + HD * t:b + HD * (t + 1), c] for t in range(3))
            g = gm[HD * h:HD * (h + 1), c]
            scores = jnp.where(same, dot(q, k, (0, 0)) * scale, -jnp.inf)
            e = jnp.exp(scores - jnp.max(scores, axis=1, keepdims=True))
            probs = e / jnp.sum(e, axis=1, keepdims=True)
            weights = probs.astype(BF16)
            mx[HD * h:HD * (h + 1), c] = dot(v, weights, (1, 1)).astype(BF16)
            dw = dot(g, v, (0, 0))
            ds = probs * (dw - jnp.sum(dw * probs, axis=1, keepdims=True)) * scale
            ds = ds.astype(BF16)
            gp[b:b + HD, c] = dot(k, ds, (1, 1)).astype(BF16)
            gp[b + HD:b + 2 * HD, c] = dot(q, ds, (1, 0)).astype(BF16)
            gp[b + 2 * HD:b + 3 * HD, c] = dot(g, weights, (1, 0)).astype(BF16)
    dsum[:QKV, :] = dot(gp[...], nrm[...], (1, 1))
    dsum[QKV:, :] = dot(mx[...], gt[...], (1, 1))
    for i in range(20):
        c = slice(FEAT * i, FEAT * (i + 1))
        keep_ref[:, c] = dsum[pl.ds(pl.multiple_of(core * 320 + 16 * i, 16), 16), :]
        send_ref[:, c] = dsum[pl.ds(pl.multiple_of((1 - core) * 320 + 16 * i, 16), 16), :].astype(BF16)
    part[...] = dot(wo_ref[...], mx[...], (0, 0))
    for i in range(20):
        j, o = divmod(64 * i, FX)
        mp_ref[j, o:o + 64, :] = part[64 * i:64 * (i + 1), :].astype(BF16)
    part[...] = dot(wq_ref[...], gp[...], (0, 0))
    row_dot = jnp.zeros((8, ROWS), F32)
    tile_row = lax.broadcasted_iota(jnp.int32, (16, TILE), 0)
    gain_tile = jnp.zeros((16, TILE), F32)
    for i in range(10):
        s = slice(128 * i, 128 * (i + 1))
        t = part[s, :] * (x_ref[s, :].astype(F32) * rms)
        row_dot += jnp.sum((t * gcol[s, :]).reshape(16, 8, ROWS), axis=0)
        lanes = t[:, :128] + t[:, 128:256] + t[:, 256:]
        line = jnp.sum(lanes.T, axis=0, keepdims=True)
        gain_tile = jnp.where(tile_row == i, line, gain_tile)
    gain_tile = gain_tile.astype(BF16)
    send_ref[:, HALF:] = gain_tile
    keep_ref[:, HALF:] = gain_tile.astype(F32)
    mean = jnp.sum(row_dot, axis=0, keepdims=True) / FEAT
    for i in range(20):
        s = slice(64 * i, 64 * (i + 1))
        j, o = divmod(64 * i, FX)
        z = rms * (part[s, :] * gcol[s, :] - (x_ref[s, :].astype(F32) * rms) * mean)
        mp_ref[j, FX + o:FX + o + 64, :] = z.astype(BF16)


def core_sum(keep_ref, got_ref, out_ref):
    gain = (keep_ref[:, HALF:] + got_ref[:, HALF:].astype(F32)).astype(BF16)
    for b in range(4):
        s = slice(Y_LANES * b, Y_LANES * (b + 1))
        out_ref[b, :, :Y_LANES] = (keep_ref[:, s] + got_ref[:, s].astype(F32)).astype(BF16)
        out_ref[b, :, Y_LANES:] = gain


def sum_of_four(ref, s):
    a, b, c, d = (ref[i, :, s].astype(F32) for i in range(4))
    return (a + b) + (c + d)


def y_sum(got_ref, out_ref):
    gain = sum_of_four(got_ref, slice(Y_LANES, Y_LANES + TILE)).astype(BF16)
    for b in range(4):
        lo, hi = Z_LANES * b, min(Z_LANES * (b + 1), Y_LANES)
        out_ref[b, :, :hi - lo] = sum_of_four(got_ref, slice(lo, hi)).astype(BF16)
        if hi - lo < Z_LANES:
            out_ref[b, :, hi - lo:Z_LANES] = jnp.zeros((16, Z_LANES - (hi - lo)), BF16)
        out_ref[b, :, Z_LANES:] = gain


def zl_sum(got_ref, out_ref):
    out_ref[...] = sum_of_four(got_ref, slice(None)).astype(BF16)


def zh_sum(got_ref, out_ref, gain_ref):
    out_ref[...] = sum_of_four(got_ref, slice(0, Z_LANES)).astype(BF16)
    gain_ref[...] = sum_of_four(got_ref, slice(Z_LANES, Z_LANES + TILE))


def z_pack(got_ref, out_ref):
    for b in range(4):
        lo, hi = Z_LANES * b, min(Z_LANES * (b + 1), Y_LANES)
        out_ref[:, lo:hi] = got_ref[b, :, :hi - lo]


def weight_out(own_ref, other_ref, qkv_ref, out_ref):
    core = lax.axis_index("c")

    def rows(first, second):
        for i in range(40):
            ref = first if i < 20 else second
            b, o = divmod(i % 20, 5)
            tile = ref[b, :, FEAT * o:FEAT * (o + 1)].astype(F32)
            if i < 30:
                qkv_ref[16 * i:16 * (i + 1), :] = tile
            else:
                out_ref[16 * (i - 30):16 * (i - 29), :] = tile

    @pl.when(core == 0)
    def _():
        rows(own_ref, other_ref)

    @pl.when(core == 1)
    def _():
        rows(other_ref, own_ref)


def gain_out(a_ref, b_ref, c_ref, d_ref, out_ref):
    mp = lax.axis_index("x")
    tile = (a_ref[...] + b_ref[...]) + (c_ref[...] + d_ref[...])
    line = jnp.concatenate([tile[i:i + 1, :] for i in range(10)], axis=1)
    out = jnp.zeros((1, FX), F32)
    for j in range(4):
        out = jnp.where(mp == j, line[:, FX * j:FX * (j + 1)], out)
    out_ref[...] = out


def heads_sum(got_ref, x_ref, cot_ref, y_ref, send_ref, grad_ref):
    for i in range(5):
        s = slice(64 * i, 64 * (i + 1))
        t = slice(FX + 64 * i, FX + 64 * (i + 1))
        a, b, c, d = (got_ref[j, s, :].astype(F32) for j in range(4))
        y = (x_ref[s, :].astype(F32) + ((a + b) + (c + d))).astype(BF16)
        y_ref[s, :] = y
        send_ref[s, :] = y[:, :PASS]
        a, b, c, d = (got_ref[j, t, :].astype(F32) for j in range(4))
        grad_ref[s, :] = (cot_ref[s, :].astype(F32) + ((a + b) + (c + d))).astype(BF16)


def route_out(counts_ref, y_ref, got_ref, out_ref):
    rank = lax.axis_index(DP)
    counts = counts_ref[...]
    owners = lax.broadcasted_iota(jnp.int32, counts.shape, 1)
    live = jnp.sum(jnp.where(owners == rank, counts, 0), axis=1, keepdims=True) * WIN
    drift = drift_of(counts, rank) * WIN
    kept = W_DEV * WIN - drift
    r = lax.broadcasted_iota(jnp.int32, (ROWS, SLOTS), 0)
    c = lax.broadcasted_iota(jnp.int32, (ROWS, SLOTS), 1)
    own = jnp.where((r == c + drift) & (c < live), 1.0, 0.0).astype(BF16)
    r, c = r[:PASS], c[:PASS]
    far = jnp.where((r == c - kept) & (c < live), 1.0, 0.0).astype(BF16)
    out_ref[...] = (dot(y_ref[...], own, (1, 0)) + dot(got_ref[...], far, (1, 0))).astype(BF16)


def shards(x_work, norm_gain, w_qkv, w_out, cot_owned, counts):
    xt, cot, wq = x_work.T, cot_owned.T, w_qkv.T
    counts = counts.reshape(1, -1)
    gain = norm_gain.reshape(1, -1)
    up = [(i, i + 1) for i in range(127)]
    down = [(i + 1, i) for i in range(127)]
    cores = [(0, 1), (1, 0)]

    send = call(route_send, struct((FX, PASS), BF16))(counts, cot)
    got = lax.ppermute(send, DP, up)
    x_full = lax.all_gather(xt, "x", axis=0, tiled=True)
    cot_work = call(route_in, struct((GROWS, ROWS), BF16))(counts, gain, cot, got)
    g_full = lax.all_gather(cot_work, "x", axis=0)

    heads, send, keep = call(
        block,
        (
            struct((4, 2 * FX, ROWS), BF16),
            struct((16, HALF + TILE), BF16),
            struct((16, HALF + TILE), F32),
        ),
        scratch=(
            pltpu.VMEM((FEAT, 1), F32),
            pltpu.VMEM((FEAT, ROWS), BF16),
            pltpu.VMEM((FEAT, ROWS), BF16),
            pltpu.VMEM((QKV, ROWS), BF16),
            pltpu.VMEM((ATT, ROWS), BF16),
            pltpu.VMEM((ATT, ROWS), BF16),
            pltpu.VMEM((QKV, ROWS), BF16),
            pltpu.VMEM((FEAT, ROWS), F32),
            pltpu.VMEM((QKV + ATT, FEAT), F32),
        ),
        vmem_mib=48,
        flops=2000000000,
    )(x_full, g_full, wq, w_out)

    heads = lax.all_to_all(heads, "x", 0, 0)

    got = lax.ppermute(send, "c", cores)
    parts = call(core_sum, struct((4, 16, Y_LANES + TILE), BF16))(keep, got)
    parts = lax.all_to_all(parts, "y", 0, 0)
    parts = call(y_sum, struct((4, 16, Z_LANES + TILE), BF16))(parts)
    parts = lax.all_to_all(parts, "zl", 0, 0)
    part = call(zl_sum, struct((16, Z_LANES + TILE), BF16))(parts)
    parts = lax.all_gather(part, "zh", axis=0)
    part, gain_own = call(zh_sum, (struct((16, Z_LANES), BF16), struct((16, TILE), F32)))(parts)
    gain_got = [lax.ppermute(gain_own, "x", [(i, (i + k) % 4) for i in range(4)]) for k in (1, 2, 3)]
    parts = lax.all_gather(part, "zl", axis=0)
    part = call(z_pack, struct((16, Y_LANES), BF16))(parts)
    own = lax.all_gather(part, "y", axis=0)
    other = lax.ppermute(own, "c", cores)
    qkv_grad, out_grad = call(weight_out, (struct((QKV, FEAT), F32), struct((ATT, FEAT), F32)))(own, other)
    gain_grad = call(gain_out, struct((1, FX), F32))(gain_own, *gain_got)

    y_work, send, x_grad = call(
        heads_sum,
        (struct((FX, ROWS), BF16), struct((FX, PASS), BF16), struct((FX, ROWS), BF16)),
    )(heads, xt, cot_work)
    got = lax.ppermute(send, DP, down)
    y_owned = call(route_out, struct((FX, SLOTS), BF16))(counts, y_work, got)
    return (y_owned.T, x_grad.T, qkv_grad.T, out_grad, gain_grad.reshape(FX))


def solution(mesh):
    fine = Mesh(mesh.devices.reshape(4, 4, 4, 2, 4), DP + ("x",))
    return jax.shard_map(
        shards,
        mesh=fine,
        in_specs=(P(DP, "x"), P("x"), P(None, "x"), P("x", None), P(DP, "x"), P()),
        out_specs=(P(DP, "x"), P(DP, "x"), P(None, "x"), P("x", None), P("x")),
        check_vma=False,
    )
```

time: 472 us -> 161 us (0.34)
  blocking collectives: 292 us -> 93.6 us
  waiting for transfers between devices: 91.4 us -> 3.49 us
  starting transfers between devices: 11.7 us -> 42.6 us
  local copies, waits for them, and re-layouts: 31.4 us -> 2.38 us
  matrix products: 17.3 us -> 0 us
  between operations: 17.8 us -> 0.77 us
  Pallas kernels: 0 us -> 15.9 us
  other arithmetic: 9.24 us -> 0.6 us
    psum x2 -> x0, blocking collectives: 256 us -> none  [the longest x1 249 us: shards(): lax.psum((qkv_grad, out_grad, gain_part), 'dp')]
    psum x1 -> x0, waiting for transfers between devices: 65.4 us -> none  [shards(): lax.psum((qkv_grad, out_grad, gain_part), 'dp')]
    all_gather x2 -> x5, blocking collectives: 27 us -> 70.8 us  [the longest x1 23 us: shards(): parts = lax.all_gather(part, 'zh', axis=0)]
    ppermute x2 -> x7, starting transfers between devices: 11.5 us -> 38.7 us  [the longest x1 13.3 us: shards(): other = lax.ppermute(own, 'c', cores)]
    all_to_all x0 -> x2, blocking collectives: none -> 22.8 us  [the longest x1 14.7 us: shards(): parts = lax.all_to_all(parts, 'y', 0, 0)]
    reduce_scatter x2 -> x0, waiting for transfers between devices: 18.1 us -> none  [the longest x1 18.1 us: shards(): lax.psum_scatter(normed_part, 'mp', scatter_dimension=1, tiled=True)]
    dot_general x11 -> x0, matrix products: 16 us -> none  [the longest x1 3.18 us: shards(): jnp.dot(grad_packed, w_qkv.T, preferred_element_type=jnp.float32)]
    pallas_call x0 -> x12, Pallas kernels: none -> 15.9 us  [the longest x1 8.73 us: shards(): call(block, (struct((4, 2 * FX, ROWS), BF16), struct((16, HALF + TILE), B...]
  transfers between devices with their start and end apart: 5 -> 8, of which waited for: 4 -> 2; matrix products, arithmetic and copies ran while one was open for 8% -> 1% of each run, Pallas kernels for 0% -> 2%
where the time goes in v1:
time: 161 us; the launch traced here: 159 us
  blocking collectives  93.6 us (58%)
  starting transfers between devices  42.6 us (26%)
  Pallas kernels  15.9 us (10%)
  waiting for transfers between devices  3.49 us (2%)
  local copies, waits for them, and re-layouts  2.38 us (1%)
    all_gather x1, blocking collectives, shards(): parts = lax.all_gather(part, 'zh', axis=0)  23 us
    all_to_all x1, blocking collectives, shards(): parts = lax.all_to_all(parts, 'y', 0, 0)  14.7 us
    all_gather x1, blocking collectives, shards(): x_full = lax.all_gather(xt, 'x', axis=0, tiled=True)  13.6 us
    ppermute x1, starting transfers between devices, shards(): other = lax.ppermute(own, 'c', cores)  13.3 us
    all_gather x1, blocking collectives, shards(): g_full = lax.all_gather(cot_work, 'x', axis=0)  12.3 us
    all_gather x1, blocking collectives, shards(): parts = lax.all_gather(part, 'zl', axis=0)  11.2 us
    all_gather x1, blocking collectives, shards(): own = lax.all_gather(part, 'y', axis=0)  10.8 us
    ppermute x1, starting transfers between devices, shards(): got = lax.ppermute(send, 'c', cores)  9.61 us
  transfers between devices with their start and end apart: 8, of which 2 were waited for; matrix products, arithmetic and copies ran while one was open for 1% of the time, Pallas kernels for 2%

profile of v1, /device:TPU:1, one launch (start us, length us, event | category | flops | bytes accessed | tf_op | source)
XLA Modules:
  0.0 159.4 jit_solution(17017703737530700385)
XLA Ops:
  0.6 0.0 copy-start
  0.6 1.0 copy-done
  1.7 0.0 copy-start.2
  1.7 0.7 copy-done.2
  2.3 0.0 copy-start.4
  2.3 0.0 copy-start.5
  2.3 0.5 shard_map.101
  2.8 4.6 %collective-permute-start = (bf16[320,320]{1,0:T(8,128)(2,1)S(1)}, bf16[320,320]{1,0:T(8,128)(2,1)S(1)}, u32[]{:S(2)}, u32[]{:S(2)}) collective-permute-start(bf16[320,320]{1,0:T(8,128)(2,1)S(1)} %shard_map.101), channel_id=1, source_target_pairs={{0,4},{4,8},{8,12},{12,16},{16,20},{20,24},{24,28},{28,32},{32,36}... | collective-permute-start | bytes 614408 | tf_op jit(solution)/shard_map/ppermute | solution.py:261
  7.5 0.7 reshape.20.gain_ref
  8.1 13.6 %all_gather.27.x_ref = bf16[1280,384]{1,0:T(8,128)(2,1)S(1)} all-gather(bf16[320,384]{1,0:T(8,128)(2,1)} %bitcast.16), channel_id=1, replica_groups=mesh['zh'=4,'zl'=4,'y'=4,'c'=2,'x'=4] {'x'}, dimensions={0}, use_global_device_ids=true | all-gather | bytes 1228800 | tf_op jit(solution)/shard_map/all_gather | solution.py:262
  21.7 0.0 collective-permute-done.got_ref
  21.7 0.5 shard_map.102.cot_ref
  22.3 12.3 %all-gather = bf16[1344,384]{1,0:T(8,128)(2,1)S(1)} all-gather(bf16[336,384]{1,0:T(8,128)(2,1)S(1)} %shard_map.102.cot_ref), channel_id=2, replica_groups=mesh['zh'=4,'zl'=4,'y'=4,'c'=2,'x'=4] {'x'}, dimensions={0}, use_global_device_ids=true | all-gather | bytes 1290240 | tf_op jit(solution)/shard_map/all_gather | solution.py:264
  34.5 0.0 copy-done.4
  34.5 0.0 copy-done.5
  34.6 8.7 %shard_map.103 = (bf16[4,640,384]{2,1,0:T(8,128)(2,1)}, bf16[16,25728]{1,0:T(8,128)(2,1)S(1)}, f32[16,25728]{1,0:T(8,128)S(1)}) custom-call(bf16[1280,384]{1,0:T(8,128)(2,1)S(1)} %all_gather.27.x_ref, bf16[4,336,384]{2,1,0:T(8,128)(2,1)S(1)} %bitcast.15, bf16[480,1280]{1,0:T(8,128)(2,1)S(1)} %bitcast.23, bf16[160,1280]{1,0:T(8,128)(2,1)S(1)} %copy-done.5), custom_call_target="tpu_custom_call" | custom-call | flops 2000000000 | bytes 1000000 | tf_op jit(solution)/shard_map/pallas_call | solution.py:266
  43.3 9.6 %collective-permute-start.2 = (bf16[16,25728]{1,0:T(8,128)(2,1)S(1)}, bf16[16,25728]{1,0:T(8,128)(2,1)S(1)}, u32[]{:S(2)}, u32[]{:S(2)}) collective-permute-start(bf16[16,25728]{1,0:T(8,128)(2,1)S(1)} %get-tuple-element.20), channel_id=1, source_target_pairs={{0,4},{4,0},{1,5},{5,1},{2,6},{6,2},{3,7},{7,3},{8,12},{12,8},{9,1... | collective-permute-start | bytes 2469896 | tf_op jit(solution)/shard_map/ppermute | solution.py:290
  52.9 1.9 %collective-permute-done.2.got_ref = bf16[16,25728]{1,0:T(8,128)(2,1)S(1)} collective-permute-done((bf16[16,25728]{1,0:T(8,128)(2,1)S(1)}, bf16[16,25728]{1,0:T(8,128)(2,1)S(1)}, u32[]{:S(2)}, u32[]{:S(2)}) %collective-permute-start.2) | collective-permute-done | bytes 823328 | tf_op jit(solution)/shard_map/ppermute | solution.py:290
  54.8 0.2 shard_map.106
  55.0 14.7 %all_to_all.15.got_ref = bf16[4,16,6528]{2,1,0:T(8,128)(2,1)S(1)} all-to-all(bf16[4,16,6528]{2,1,0:T(8,128)(2,1)S(1)} %shard_map.106), channel_id=1, replica_groups=mesh['zh'=4,'zl'=4,'y'=4,'c'=2,'x'=4] {'y'}, dimensions={0} | all-to-all | bytes 1671168 | tf_op jit(solution)/shard_map/all_to_all | solution.py:292
  69.7 0.1 shard_map.107
  69.8 8.1 %all_to_all.16.got_ref = bf16[4,16,1792]{2,1,0:T(8,128)(2,1)S(1)} all-to-all(bf16[4,16,1792]{2,1,0:T(8,128)(2,1)S(1)} %shard_map.107), channel_id=1, replica_groups=mesh['zh'=4,'zl'=4,'y'=4,'c'=2,'x'=4] {'zl'}, dimensions={0} | all-to-all | bytes 458752 | tf_op jit(solution)/shard_map/all_to_all | solution.py:294
  78.0 3.9 %all-to-all-start = ((bf16[4,640,384]{2,1,0:T(8,128)(2,1)}), bf16[4,640,384]{2,1,0:T(8,128)(2,1)S(1)}, u32[]{:S(2)}, u32[]{:S(2)}) async-start(bf16[4,640,384]{2,1,0:T(8,128)(2,1)} %get-tuple-element.15), calls=%async_computation | async-start | bytes 3932160 | tf_op jit(solution)/shard_map/all_to_all | solution.py:288
  81.9 0.0 copy-start.1
  81.9 23.0 %all-gather.1 = bf16[64,1792]{1,0:T(8,128)(2,1)S(1)} all-gather(bf16[16,1792]{1,0:T(8,128)(2,1)S(1)} %shard_map.108), channel_id=3, replica_groups=mesh['zh'=4,'zl'=4,'y'=4,'c'=2,'x'=4] {'zh'}, dimensions={0}, use_global_device_ids=true | all-gather | bytes 286720 | tf_op jit(solution)/shard_map/all_gather | solution.py:296
  104.9 11.2 %all-gather.2 = bf16[64,1664]{1,0:T(8,128)(2,1)S(1)} all-gather(bf16[16,1664]{1,0:T(8,128)(2,1)S(1)} %get-tuple-element.21), channel_id=4, replica_groups=mesh['zh'=4,'zl'=4,'y'=4,'c'=2,'x'=4] {'zl'}, dimensions={0}, use_global_device_ids=true | all-gather | bytes 266240 | tf_op jit(solution)/shard_map/all_gather | solution.py:299
  116.1 0.0 copy-start.3
  116.1 10.8 %all-gather.3 = bf16[64,6400]{1,0:T(8,128)(2,1)S(1)} all-gather(bf16[16,6400]{1,0:T(8,128)(2,1)S(1)} %shard_map.110), channel_id=5, replica_groups=mesh['zh'=4,'zl'=4,'y'=4,'c'=2,'x'=4] {'y'}, dimensions={0}, use_global_device_ids=true | all-gather | bytes 1024000 | tf_op jit(solution)/shard_map/all_gather | solution.py:301
  126.9 13.3 %collective-permute-start.3 = (bf16[4,16,6400]{2,1,0:T(8,128)(2,1)S(1)}, bf16[4,16,6400]{2,1,0:T(8,128)(2,1)}, u32[]{:S(2)}, u32[]{:S(2)}) collective-permute-start(bf16[4,16,6400]{2,1,0:T(8,128)(2,1)S(1)} %bitcast.11), channel_id=1, source_target_pairs={{0,4},{4,0},{1,5},{5,1},{2,6},{6,2},{3,7},{7,3},{8,12},{12,8},{9,1... | collective-permute-start | bytes 2457608 | tf_op jit(solution)/shard_map/ppermute | solution.py:302
  140.2 0.0 all-to-all-done.got_ref
  140.2 0.0 copy-done.1
  140.3 0.9 shard_map.104
  141.1 1.9 %collective-permute-start.1 = (bf16[320,320]{1,0:T(8,128)(2,1)S(1)}, bf16[320,320]{1,0:T(8,128)(2,1)S(1)}, u32[]{:S(2)}, u32[]{:S(2)}) collective-permute-start(bf16[320,320]{1,0:T(8,128)(2,1)S(1)} %get-tuple-element.17), channel_id=1, source_target_pairs={{4,0},{8,4},{12,8},{16,12},{20,16},{24,20},{28,24},{32,28},{36,32}... | collective-permute-start | bytes 614408 | tf_op jit(solution)/shard_map/ppermute | solution.py:310
  143.0 4.3 %collective-permute-start.6 = (f32[16,128]{1,0:T(8,128)S(1)}, f32[16,128]{1,0:T(8,128)S(1)}, u32[]{:S(2)}, u32[]{:S(2)}) collective-permute-start(f32[16,128]{1,0:T(8,128)S(1)} %get-tuple-element.24.a_ref), channel_id=1, source_target_pairs={{0,3},{1,0},{2,1},{3,2},{4,7},{5,4},{6,5},{7,6},{8,11},{9,8},{10,9... | collective-permute-start | bytes 24584 | tf_op jit(solution)/shard_map/ppermute | solution.py:298
  147.4 2.5 %collective-permute-start.5 = (f32[16,128]{1,0:T(8,128)S(1)}, f32[16,128]{1,0:T(8,128)S(1)}, u32[]{:S(2)}, u32[]{:S(2)}) collective-permute-start(f32[16,128]{1,0:T(8,128)S(1)} %get-tuple-element.24.a_ref), channel_id=1, source_target_pairs={{0,2},{1,3},{2,0},{3,1},{4,6},{5,7},{6,4},{7,5},{8,10},{9,11},{10,... | collective-permute-start | bytes 24584 | tf_op jit(solution)/shard_map/ppermute | solution.py:298
  149.9 2.5 %collective-permute-start.4 = (f32[16,128]{1,0:T(8,128)S(1)}, f32[16,128]{1,0:T(8,128)S(1)}, u32[]{:S(2)}, u32[]{:S(2)}) collective-permute-start(f32[16,128]{1,0:T(8,128)S(1)} %get-tuple-element.24.a_ref), channel_id=1, source_target_pairs={{0,1},{1,2},{2,3},{3,0},{4,5},{5,6},{6,7},{7,4},{8,9},{9,10},{10,1... | collective-permute-start | bytes 24584 | tf_op jit(solution)/shard_map/ppermute | solution.py:298
  152.4 0.0 collective-permute-done.1.got_ref
  152.4 0.0 copy-done.3
  152.4 1.6 shard_map.105
  153.9 0.0 collective-permute-done.6.d_ref
  153.9 0.0 collective-permute-done.5.c_ref
  153.9 1.5 collective-permute-done.4.b_ref
  155.5 0.3 shard_map.112
  155.8 0.6 reduce
  156.4 0.0 collective-permute-done.3.other_ref
  156.4 3.1 %shard_map.111 = (f32[480,1280]{1,0:T(8,128)}, f32[160,1280]{1,0:T(8,128)}) custom-call(bf16[4,16,6400]{2,1,0:T(8,128)(2,1)S(1)} %bitcast.12, bf16[4,16,6400]{2,1,0:T(8,128)(2,1)} %collective-permute-done.3.other_ref), custom_call_target="tpu_custom_call" | custom-call | flops 1000000 | bytes 1000000 | tf_op jit(solution)/shard_map/pallas_call | solution.py:303
  (3 shorter events, 0.1 us)
Async XLA Ops:
  0.6 1.0 copy-start
  1.7 0.7 copy-start.2
  2.3 32.2 %copy-start.4 = (bf16[1280,480]{0,1:T(8,128)(2,1)S(1)}, bf16[1280,480]{0,1:T(8,128)(2,1)}, u32[]{:S(2)}) copy-start(bf16[1280,480]{0,1:T(8,128)(2,1)} %param.8) | copy-start | bytes 3686404
  2.3 32.2 %copy-start.5 = (bf16[160,1280]{1,0:T(8,128)(2,1)S(1)}, bf16[160,1280]{1,0:T(8,128)(2,1)}, u32[]{:S(2)}) copy-start(bf16[160,1280]{1,0:T(8,128)(2,1)} %wo_ref.1) | copy-start | bytes 1228804
  2.8 18.9 %collective-permute-start = (bf16[320,320]{1,0:T(8,128)(2,1)S(1)}, bf16[320,320]{1,0:T(8,128)(2,1)S(1)}, u32[]{:S(2)}, u32[]{:S(2)}) collective-permute-start(bf16[320,320]{1,0:T(8,128)(2,1)S(1)} %shard_map.101), channel_id=1, source_target_pairs={{0,4},{4,8},{8,12},{12,16},{16,20},{20,24},{24,28},{28,32},{32,36}... | collective-permute-start | bytes 614408 | tf_op jit(solution)/shard_map/ppermute | solution.py:261
  43.3 11.6 %collective-permute-start.2 = (bf16[16,25728]{1,0:T(8,128)(2,1)S(1)}, bf16[16,25728]{1,0:T(8,128)(2,1)S(1)}, u32[]{:S(2)}, u32[]{:S(2)}) collective-permute-start(bf16[16,25728]{1,0:T(8,128)(2,1)S(1)} %get-tuple-element.20), channel_id=1, source_target_pairs={{0,4},{4,0},{1,5},{5,1},{2,6},{6,2},{3,7},{7,3},{8,12},{12,8},{9,1... | collective-permute-start | bytes 2469896 | tf_op jit(solution)/shard_map/ppermute | solution.py:290
  78.0 62.3 %all-to-all-start = ((bf16[4,640,384]{2,1,0:T(8,128)(2,1)}), bf16[4,640,384]{2,1,0:T(8,128)(2,1)S(1)}, u32[]{:S(2)}, u32[]{:S(2)}) async-start(bf16[4,640,384]{2,1,0:T(8,128)(2,1)} %get-tuple-element.15), calls=%async_computation | async-start | bytes 3932160 | tf_op jit(solution)/shard_map/all_to_all | solution.py:288
  81.9 58.4 %copy-start.1 = (bf16[384,320]{0,1:T(8,128)(2,1)S(1)}, bf16[384,320]{0,1:T(8,128)(2,1)}, u32[]{:S(2)}) copy-start(bf16[384,320]{0,1:T(8,128)(2,1)} %param.6) | copy-start | bytes 737284
  116.1 36.2 %copy-start.3 = (s32[128]{0:T(128)S(1)}, s32[128]{0:T(128)}, u32[]{:S(2)}) copy-start(s32[128]{0:T(128)} %param.11) | copy-start | bytes 1540
  126.9 29.4 %collective-permute-start.3 = (bf16[4,16,6400]{2,1,0:T(8,128)(2,1)S(1)}, bf16[4,16,6400]{2,1,0:T(8,128)(2,1)}, u32[]{:S(2)}, u32[]{:S(2)}) collective-permute-start(bf16[4,16,6400]{2,1,0:T(8,128)(2,1)S(1)} %bitcast.11), channel_id=1, source_target_pairs={{0,4},{4,0},{1,5},{5,1},{2,6},{6,2},{3,7},{7,3},{8,12},{12,8},{9,1... | collective-permute-start | bytes 2457608 | tf_op jit(solution)/shard_map/ppermute | solution.py:302
  141.1 11.2 %collective-permute-start.1 = (bf16[320,320]{1,0:T(8,128)(2,1)S(1)}, bf16[320,320]{1,0:T(8,128)(2,1)S(1)}, u32[]{:S(2)}, u32[]{:S(2)}) collective-permute-start(bf16[320,320]{1,0:T(8,128)(2,1)S(1)} %get-tuple-element.17), channel_id=1, source_target_pairs={{4,0},{8,4},{12,8},{16,12},{20,16},{24,20},{28,24},{32,28},{36,32}... | collective-permute-start | bytes 614408 | tf_op jit(solution)/shard_map/ppermute | solution.py:310
  143.0 10.9 %collective-permute-start.6 = (f32[16,128]{1,0:T(8,128)S(1)}, f32[16,128]{1,0:T(8,128)S(1)}, u32[]{:S(2)}, u32[]{:S(2)}) collective-permute-start(f32[16,128]{1,0:T(8,128)S(1)} %get-tuple-element.24.a_ref), channel_id=1, source_target_pairs={{0,3},{1,0},{2,1},{3,2},{4,7},{5,4},{6,5},{7,6},{8,11},{9,8},{10,9... | collective-permute-start | bytes 24584 | tf_op jit(solution)/shard_map/ppermute | solution.py:298
  147.4 6.6 %collective-permute-start.5 = (f32[16,128]{1,0:T(8,128)S(1)}, f32[16,128]{1,0:T(8,128)S(1)}, u32[]{:S(2)}, u32[]{:S(2)}) collective-permute-start(f32[16,128]{1,0:T(8,128)S(1)} %get-tuple-element.24.a_ref), channel_id=1, source_target_pairs={{0,2},{1,3},{2,0},{3,1},{4,6},{5,7},{6,4},{7,5},{8,10},{9,11},{10,... | collective-permute-start | bytes 24584 | tf_op jit(solution)/shard_map/ppermute | solution.py:298
  149.9 5.6 %collective-permute-start.4 = (f32[16,128]{1,0:T(8,128)S(1)}, f32[16,128]{1,0:T(8,128)S(1)}, u32[]{:S(2)}, u32[]{:S(2)}) collective-permute-start(f32[16,128]{1,0:T(8,128)S(1)} %get-tuple-element.24.a_ref), channel_id=1, source_target_pairs={{0,1},{1,2},{2,3},{3,0},{4,5},{5,6},{6,7},{7,4},{8,9},{9,10},{10,1... | collective-permute-start | bytes 24584 | tf_op jit(solution)/shard_map/ppermute | solution.py:298

commit v2 on v1

v2 whole, which is shorter than its diff:
```python
import jax
import jax.numpy as jnp
from jax import lax
from jax.experimental import pallas as pl
from jax.experimental.pallas import tpu as pltpu
from jax.sharding import Mesh, PartitionSpec as P

HD = 80
WIN = 64
W_DEV = 6
epsilon = 1e-06

F32 = jnp.float32
BF16 = jnp.bfloat16
DP = ("zh", "zl", "y", "c")

FEAT = 1280
ROWS = 384
FX = 320
QKV = 480
ATT = 160
HEADS = 2
SLOTS = 704
PASS = 320
GROWS = 336

HALF = 25600
Y_LANES = 6400
Z_LANES = 1664
TILE = 128

VMEM = pl.BlockSpec(memory_space=pltpu.VMEM)
ANY = pl.BlockSpec(memory_space=pl.ANY)
HBM = pl.BlockSpec(memory_space=pltpu.HBM)


def call(kernel, out_shapes, ins=None, outs=None, aliases=None, scratch=(), vmem_mib=24, flops=1000000):
    specs = {}
    if ins is not None:
        specs["in_specs"] = ins
    if outs is not None:
        specs["out_specs"] = outs
    return pl.pallas_call(
        kernel,
        out_shape=out_shapes,
        scratch_shapes=list(scratch),
        input_output_aliases=aliases or {},
        compiler_params=pltpu.CompilerParams(vmem_limit_bytes=vmem_mib * 1024 * 1024),
        cost_estimate=pl.CostEstimate(flops=flops, bytes_accessed=1000000, transcendentals=0),
        **specs,
    )


def struct(shape, dtype):
    return jax.ShapeDtypeStruct(shape, dtype)


def drift_of(counts_row, rank):
    owners = lax.broadcasted_iota(jnp.int32, counts_row.shape, 1)
    before = jnp.sum(jnp.where(owners < rank, counts_row, 0), axis=1, keepdims=True)
    return before - rank * W_DEV


def one_hot(rows, cols, shift):
    r = lax.broadcasted_iota(jnp.int32, (rows, cols), 0)
    c = lax.broadcasted_iota(jnp.int32, (rows, cols), 1)
    return jnp.where(r == c + shift, 1.0, 0.0).astype(BF16)


def dot(a, b, dims):
    return lax.dot_general(a, b, ((dims[:1], dims[1:]), ((), ())), preferred_element_type=F32)


def enter(counts_hbm, cot_hbm, send_ref, counts, cot, sems):
    copies = [
        pltpu.make_async_copy(counts_hbm, counts, sems.at[0]),
        pltpu.make_async_copy(cot_hbm, cot, sems.at[1]),
    ]
    for copy in copies:
        copy.start()
    for copy in copies:
        copy.wait()
    drift = drift_of(counts[...], lax.axis_index(DP))
    pick = one_hot(SLOTS, PASS, (W_DEV - drift) * WIN)
    send_ref[...] = dot(cot[...], pick, (1, 0)).astype(BF16)


def route_in(counts_ref, gain_ref, cot_ref, got_ref, out_ref):
    drift = drift_of(counts_ref[...], lax.axis_index(DP)) * WIN
    own = dot(cot_ref[:, :ROWS], one_hot(ROWS, ROWS, -drift), (1, 0))
    col = lax.broadcasted_iota(jnp.int32, (PASS, ROWS), 1)
    row = lax.broadcasted_iota(jnp.int32, (PASS, ROWS), 0)
    near = jnp.where((row == col) & (col < drift), 1.0, 0.0).astype(BF16)
    out_ref[:FX, :] = (own + dot(got_ref[...], near, (1, 0))).astype(BF16)
    out_ref[FX:, :] = jnp.zeros((GROWS - FX, ROWS), BF16)
    out_ref[FX:, :FX] = jnp.broadcast_to(gain_ref[...], (GROWS - FX, FX))


def x_rows(x_ref, i):
    return x_ref[80 * i:80 * (i + 1), :]


def pairs():
    return [(3 * h + p, h, slice(128 * p, 128 * (p + 1)), 3 * HD * h) for h in range(HEADS) for p in range(3)]


def block(x_ref, g_ref, wq_ref, wo_ref, send_ref, keep_ref, gp_ref, mx_ref, gcol_ref, rms_ref, gt, nrm, pk, gm, dsum):
    core = lax.axis_index("c")
    r_i = lax.broadcasted_iota(jnp.int32, (FX, ROWS), 0)
    c_i = lax.broadcasted_iota(jnp.int32, (FX, ROWS), 1)
    total = jnp.zeros((8, ROWS), F32)
    for i in range(16):
        x = x_rows(x_ref, i).astype(F32)
        total += jnp.sum((x * x).reshape(10, 8, ROWS), axis=0)
    rms = lax.rsqrt(jnp.sum(total, axis=0, keepdims=True) / FEAT + epsilon)
    rms_ref[...] = rms
    for j in range(4):
        gt[FX * j:FX * (j + 1), :] = g_ref[j, :FX, :]
        row = g_ref[j, FX:, :].astype(F32)[:1, :]
        gcol_ref[FX * j:FX * (j + 1), :] = jnp.sum(jnp.where(r_i == c_i, row, 0.0), axis=1, keepdims=True)
    for i in range(16):
        s = slice(80 * i, 80 * (i + 1))
        nrm[s, :] = ((x_rows(x_ref, i).astype(F32) * rms) * gcol_ref[s, :]).astype(BF16)
    pk[...] = dot(wq_ref[...], nrm[...], (1, 0)).astype(BF16)
    gm[...] = dot(wo_ref[...], gt[...], (1, 0)).astype(BF16)
    qi = lax.broadcasted_iota(jnp.int32, (128, 128), 0)
    ki = lax.broadcasted_iota(jnp.int32, (128, 128), 1)
    same = (qi < WIN) == (ki < WIN)
    scores = [
        jnp.where(same, dot(pk[b:b + HD, c], pk[b + HD:b + 2 * HD, c], (0, 0)) * HD ** (-0.5), -jnp.inf)
        for _, _, c, b in pairs()
    ]
    dws = [dot(gm[HD * h:HD * (h + 1), c], pk[b + 2 * HD:b + 3 * HD, c], (0, 0)) for _, h, c, b in pairs()]
    exps = [jnp.exp(s - jnp.max(s, axis=1, keepdims=True)) for s in scores]
    probs = [e / jnp.sum(e, axis=1, keepdims=True) for e in exps]
    weights = [p.astype(BF16) for p in probs]
    dss = [
        (p * (dw - jnp.sum(dw * p, axis=1, keepdims=True)) * HD ** (-0.5)).astype(BF16)
        for p, dw in zip(probs, dws)
    ]
    for n, h, c, b in pairs():
        mx_ref[HD * h:HD * (h + 1), c] = dot(pk[b + 2 * HD:b + 3 * HD, c], weights[n], (1, 1)).astype(BF16)
        gp_ref[b:b + HD, c] = dot(pk[b + HD:b + 2 * HD, c], dss[n], (1, 1)).astype(BF16)
        gp_ref[b + HD:b + 2 * HD, c] = dot(pk[b:b + HD, c], dss[n], (1, 0)).astype(BF16)
        gp_ref[b + 2 * HD:b + 3 * HD, c] = dot(gm[HD * h:HD * (h + 1), c], weights[n], (1, 0)).astype(BF16)
    dsum[:QKV, :] = dot(gp_ref[...], nrm[...], (1, 1))
    dsum[QKV:, :] = dot(mx_ref[...], gt[...], (1, 1))
    for i in range(20):
        c = slice(FEAT * i, FEAT * (i + 1))
        keep_ref[:, c] = dsum[pl.ds(pl.multiple_of(core * 320 + 16 * i, 16), 16), :]
        send_ref[:, c] = dsum[pl.ds(pl.multiple_of((1 - core) * 320 + 16 * i, 16), 16), :].astype(BF16)
    total = jnp.zeros((8, FEAT), F32)
    for i in range(30):
        s = slice(16 * i, 16 * (i + 1))
        total += jnp.sum((wq_ref[s, :].astype(F32) * dsum[s, :]).reshape(2, 8, FEAT), axis=0)
    line = jnp.sum(total, axis=0, keepdims=True)
    tile_row = lax.broadcasted_iota(jnp.int32, (16, TILE), 0)
    tile = jnp.zeros((16, TILE), F32)
    for i in range(10):
        tile = jnp.where(tile_row == i, line[:, TILE * i:TILE * (i + 1)], tile)
    tile = tile.astype(BF16)
    send_ref[:, HALF:] = tile
    keep_ref[:, HALF:] = tile.astype(F32)


def head_shares(gp_ref, mx_ref, x_ref, wq_ref, wo_ref, gcol_ref, rms_ref, heads_ref, part, out, sems):
    rms = rms_ref[...]
    part[...] = dot(wo_ref[...], mx_ref[...], (0, 0))
    for j in range(4):
        out[j, :FX, :] = part[FX * j:FX * (j + 1), :].astype(BF16)
    part[...] = dot(wq_ref[...], gp_ref[...], (0, 0))
    row_dot = jnp.zeros((8, ROWS), F32)
    for i in range(16):
        s = slice(80 * i, 80 * (i + 1))
        x = x_rows(x_ref, i).astype(F32)
        row_dot += jnp.sum(((part[s, :] * gcol_ref[s, :]) * (x * rms)).reshape(10, 8, ROWS), axis=0)
    mean = jnp.sum(row_dot, axis=0, keepdims=True) / FEAT
    copies = []
    for j in range(4):
        for i in range(4):
            s = slice(FX * j + 80 * i, FX * j + 80 * (i + 1))
            x = x_rows(x_ref, 4 * j + i).astype(F32)
            z = rms * (part[s, :] * gcol_ref[s, :] - (x * rms) * mean)
            out[j, FX + 80 * i:FX + 80 * (i + 1), :] = z.astype(BF16)
        copies.append(pltpu.make_async_copy(out.at[j], heads_ref.at[j, pl.ds(0, 2 * FX)], sems.at[j]))
        copies[j].start()
    for copy in copies:
        copy.wait()


def core_sum(keep_ref, got_ref, heads_ref, out_ref):
    gain = (keep_ref[:, HALF:] + got_ref[:, HALF:].astype(F32)).astype(BF16)
    for b in range(4):
        s = slice(Y_LANES * b, Y_LANES * (b + 1))
        out_ref[b, :, :Y_LANES] = (keep_ref[:, s] + got_ref[:, s].astype(F32)).astype(BF16)
        out_ref[b, :, Y_LANES:] = gain


def sum_of_four(ref, s):
    a, b, c, d = (ref[i, :, s].astype(F32) for i in range(4))
    return (a + b) + (c + d)


def y_sum(got_ref, out_ref):
    gain = sum_of_four(got_ref, slice(Y_LANES, Y_LANES + TILE)).astype(BF16)
    for b in range(4):
        lo, hi = Z_LANES * b, min(Z_LANES * (b + 1), Y_LANES)
        out_ref[b, :, :hi - lo] = sum_of_four(got_ref, slice(lo, hi)).astype(BF16)
        if hi - lo < Z_LANES:
            out_ref[b, :, hi - lo:Z_LANES] = jnp.zeros((16, Z_LANES - (hi - lo)), BF16)
        out_ref[b, :, Z_LANES:] = gain


def zl_sum(got_ref, out_ref):
    out_ref[...] = sum_of_four(got_ref, slice(None)).astype(BF16)


def pair_sum(own_ref, got_ref, out_ref):
    out_ref[...] = (own_ref[...].astype(F32) + got_ref[...].astype(F32)).astype(BF16)


def zh_sum(own_ref, got_ref, heads_in, out_ref, heads_ref, lines, sems):
    total = own_ref[...].astype(F32) + got_ref[...].astype(F32)
    out_ref[...] = total[:, :Z_LANES].astype(BF16)
    tile = total[:, Z_LANES:]
    line = jnp.concatenate([tile[i:i + 1, :] for i in range(10)], axis=1)
    row = lax.broadcasted_iota(jnp.int32, (16, FX), 0)
    copies = []
    for j in range(4):
        chunk = line[:, FX * j:FX * (j + 1)]
        high = chunk.astype(BF16).astype(F32)
        lines[j] = jnp.zeros((16, ROWS), BF16)
        lines[j, :, :FX] = jnp.where(row == 0, high, jnp.where(row == 1, chunk - high, 0.0)).astype(BF16)
        copies.append(pltpu.make_async_copy(lines.at[j], heads_ref.at[j, pl.ds(2 * FX, 16)], sems.at[j]))
        copies[j].start()
    for copy in copies:
        copy.wait()


def z_pack(got_ref, out_ref):
    for b in range(4):
        lo, hi = Z_LANES * b, min(Z_LANES * (b + 1), Y_LANES)
        out_ref[:, lo:hi] = got_ref[b, :, :hi - lo]


def weight_rows(ref, half, qkv_ref, out_ref, buf, sems):
    for b in range(4):
        for o in range(5):
            i = 5 * b + o
            buf[16 * i:16 * (i + 1), :] = ref[b, :, FEAT * o:FEAT * (o + 1)].astype(F32)
        chunk = buf.at[pl.ds(80 * b, 80)]

        @pl.when(half == 0)
        def _():
            pltpu.make_async_copy(chunk, qkv_ref.at[pl.ds(80 * b, 80)], sems.at[b]).start()

        @pl.when(half == 1)
        def _():
            target = qkv_ref.at[pl.ds(320 + 80 * b, 80)] if b < 2 else out_ref.at[pl.ds(80 * (b - 2), 80)]
            pltpu.make_async_copy(chunk, target, sems.at[b]).start()

    for b in range(4):
        chunk = buf.at[pl.ds(80 * b, 80)]
        pltpu.make_async_copy(chunk, qkv_ref.at[pl.ds(0, 80)], sems.at[b]).wait()


def weight_own(ref, qkv_ref, out_ref, buf, sems):
    weight_rows(ref, lax.axis_index("c"), qkv_ref, out_ref, buf, sems)


def weight_other(ref, qkv_in, out_in, qkv_ref, out_ref, buf, sems):
    weight_rows(ref, 1 - lax.axis_index("c"), qkv_ref, out_ref, buf, sems)


def heads_sum(got_ref, x_ref, cot_ref, gain_ref, y_ref, send_ref, grad_ref, gain_grad_ref):
    for i in range(5):
        s = slice(64 * i, 64 * (i + 1))
        t = slice(FX + 64 * i, FX + 64 * (i + 1))
        a, b, c, d = (got_ref[j, s, :].astype(F32) for j in range(4))
        y = (x_ref[s, :].astype(F32) + ((a + b) + (c + d))).astype(BF16)
        y_ref[s, :] = y
        send_ref[s, :] = y[:, :PASS]
        a, b, c, d = (got_ref[j, t, :].astype(F32) for j in range(4))
        grad_ref[s, :] = (cot_ref[s, :].astype(F32) + ((a + b) + (c + d))).astype(BF16)
    a, b, c, d = (got_ref[j, 2 * FX:, :].astype(F32) for j in range(4))
    line = jnp.sum((a + b) + (c + d), axis=0, keepdims=True)
    gain_grad_ref[...] = (line[:, :FX] / gain_ref[...].astype(F32)).reshape(FX)


def route_out(counts_ref, y_ref, got_ref, out_ref):
    rank = lax.axis_index(DP)
    counts = counts_ref[...]
    owners = lax.broadcasted_iota(jnp.int32, counts.shape, 1)
    live = jnp.sum(jnp.where(owners == rank, counts, 0), axis=1, keepdims=True) * WIN
    drift = drift_of(counts, rank) * WIN
    kept = W_DEV * WIN - drift
    r = lax.broadcasted_iota(jnp.int32, (ROWS, SLOTS), 0)
    c = lax.broadcasted_iota(jnp.int32, (ROWS, SLOTS), 1)
    own = jnp.where((r == c + drift) & (c < live), 1.0, 0.0).astype(BF16)
    r, c = r[:PASS], c[:PASS]
    far = jnp.where((r == c - kept) & (c < live), 1.0, 0.0).astype(BF16)
    out_ref[...] = (dot(y_ref[...], own, (1, 0)) + dot(got_ref[...], far, (1, 0))).astype(BF16)


def shards(x_work, norm_gain, w_qkv, w_out, cot_owned, counts):
    xt, cot, wq = x_work.T, cot_owned.T, w_qkv.T
    counts = counts.reshape(1, -1)
    gain = norm_gain.reshape(1, -1)
    up = [(i, i + 1) for i in range(127)]
    down = [(i + 1, i) for i in range(127)]
    cores = [(0, 1), (1, 0)]

    send = call(
        enter,
        struct((FX, PASS), BF16),
        ins=(HBM, HBM),
        scratch=(pltpu.VMEM((1, 128), jnp.int32), pltpu.VMEM((FX, SLOTS), BF16), pltpu.SemaphoreType.DMA((2,))),
    )(counts, cot)
    got = lax.ppermute(send, DP, up)
    x_full = lax.all_gather(xt, "x", axis=0, tiled=True)
    cot_work = call(route_in, struct((GROWS, ROWS), BF16))(counts, gain, cot, got)
    g_full = lax.all_gather(cot_work, "x", axis=0)

    send, keep, gp, mx, gcol, rms = call(
        block,
        (
            struct((16, HALF + TILE), BF16),
            struct((16, HALF + TILE), F32),
            struct((QKV, ROWS), BF16),
            struct((ATT, ROWS), BF16),
            struct((FEAT, 1), F32),
            struct((1, ROWS), F32),
        ),
        scratch=(
            pltpu.VMEM((FEAT, ROWS), BF16),
            pltpu.VMEM((FEAT, ROWS), BF16),
            pltpu.VMEM((QKV, ROWS), BF16),
            pltpu.VMEM((ATT, ROWS), BF16),
            pltpu.VMEM((QKV + ATT, FEAT), F32),
        ),
        vmem_mib=40,
        flops=1500000000,
    )(x_full, g_full, wq, w_out)

    got = lax.ppermute(send, "c", cores)
    heads_shape = struct((4, 2 * FX + 16, ROWS), BF16)
    heads = call(
        head_shares,
        heads_shape,
        outs=HBM,
        scratch=(
            pltpu.VMEM((FEAT, ROWS), F32),
            pltpu.VMEM((4, 2 * FX, ROWS), BF16),
            pltpu.SemaphoreType.DMA((4,)),
        ),
        vmem_mib=40,
        flops=700000000,
    )(gp, mx, x_full, wq, w_out, gcol, rms)

    parts = call(core_sum, struct((4, 16, Y_LANES + TILE), BF16), ins=(VMEM, VMEM, HBM))(keep, got, heads)
    parts = lax.all_to_all(parts, "y", 0, 0)
    parts = call(y_sum, struct((4, 16, Z_LANES + TILE), BF16))(parts)
    parts = lax.all_to_all(parts, "zl", 0, 0)
    part = call(zl_sum, struct((16, Z_LANES + TILE), BF16))(parts)
    got = lax.ppermute(part, "zh", [(0, 1), (1, 0), (2, 3), (3, 2)])
    part = call(pair_sum, struct((16, Z_LANES + TILE), BF16))(part, got)
    got = lax.ppermute(part, "zh", [(1, 2), (2, 1), (3, 0), (0, 3)])
    part, heads = call(
        zh_sum,
        (struct((16, Z_LANES), BF16), heads_shape),
        ins=(VMEM, VMEM, HBM),
        outs=(VMEM, HBM),
        aliases={2: 1},
        scratch=(pltpu.VMEM((4, 16, ROWS), BF16), pltpu.SemaphoreType.DMA((4,))),
    )(part, got, heads)
    heads = lax.all_to_all(heads, "x", 0, 0)
    parts = lax.all_gather(part, "zl", axis=0)
    part = call(z_pack, struct((16, Y_LANES), BF16))(parts)
    own = lax.all_gather(part, "y", axis=0)
    other = lax.ppermute(own, "c", cores)
    weight_shapes = (struct((QKV, FEAT), F32), struct((ATT, FEAT), F32))
    weight_scratch = (pltpu.VMEM((320, FEAT), F32), pltpu.SemaphoreType.DMA((4,)))
    weights = call(weight_own, weight_shapes, outs=(ANY, ANY), scratch=weight_scratch)(own)
    qkv_grad, out_grad = call(
        weight_other,
        weight_shapes,
        ins=(VMEM, ANY, ANY),
        outs=(ANY, ANY),
        aliases={1: 0, 2: 1},
        scratch=weight_scratch,
    )(other, *weights)

    y_work, send, x_grad, gain_grad = call(
        heads_sum,
        (
            struct((FX, ROWS), BF16),
            struct((FX, PASS), BF16),
            struct((FX, ROWS), BF16),
            struct((FX,), F32),
        ),
    )(heads, xt, cot_work, gain)
    got = lax.ppermute(send, DP, down)
    y_owned = call(route_out, struct((FX, SLOTS), BF16))(counts, y_work, got)
    return (y_owned.T, x_grad.T, qkv_grad.T, out_grad, gain_grad)


def solution(mesh):
    fine = Mesh(mesh.devices.reshape(4, 4, 4, 2, 4), DP + ("x",))
    return jax.shard_map(
        shards,
        mesh=fine,
        in_specs=(P(DP, "x"), P("x"), P(None, "x"), P("x", None), P(DP, "x"), P()),
        out_specs=(P(DP, "x"), P(DP, "x"), P(None, "x"), P("x", None), P("x")),
        check_vma=False,
    )
```

time: 161 us -> 146 us (0.907)
  blocking collectives: 93.6 us -> 74.7 us
  starting transfers between devices: 42.6 us -> 47.3 us
  waiting for transfers between devices: 3.49 us -> 5.22 us
    all_gather x1 -> x0, blocking collectives: 23 us -> none  [shards(): parts = lax.all_gather(part, 'zh', axis=0)]
    ppermute x3 -> x2, starting transfers between devices: 9.3 us -> 16.2 us  [the longest x1 8.11 us: shards(): got = lax.ppermute(part, 'zh', [(1, 2), (2, 1), (3, 0), (0, 3)])]
    ppermute x1, starting transfers between devices: 13.3 us -> 10.4 us  [shards(): other = lax.ppermute(own, 'c', cores)]
    all_gather x1, blocking collectives: 11.2 us -> 13.9 us  [shards(): parts = lax.all_gather(part, 'zl', axis=0)]
    ppermute x1, waiting for transfers between devices: 0.01 us -> 1.96 us  [shards(): got = lax.ppermute(send, DP, down)]
    ppermute x1, waiting for transfers between devices: 1.94 us -> 0.01 us  [shards(): got = lax.ppermute(send, 'c', cores)]
    ppermute x3 -> x2, waiting for transfers between devices: 1.54 us -> 3.25 us  [the longest x1 1.69 us: shards(): got = lax.ppermute(part, 'zh', [(1, 2), (2, 1), (3, 0), (0, 3)])]
    pallas_call x6 -> x8, Pallas kernels: 12.8 us -> 12.4 us  [the longest x1 4.03 us: shards(): call(block, (struct((16, HALF + TILE), BF16), struct((16, HALF + TILE), F...]
  transfers between devices with their start and end apart: 8 -> 7, of which waited for: 2 -> 3; matrix products, arithmetic and copies ran while one was open for 1% -> 0% of each run, Pallas kernels for 2% -> 5%
where the time goes in v2:
time: 146 us
  blocking collectives  74.7 us (51%)
  starting transfers between devices  47.3 us (32%)
  Pallas kernels  15.5 us (11%)
  waiting for transfers between devices  5.22 us (4%)
  local copies, waits for them, and re-layouts  2.38 us (2%)
    all_to_all x1, blocking collectives, shards(): parts = lax.all_to_all(parts, 'y', 0, 0)  15.4 us
    all_gather x1, blocking collectives, shards(): parts = lax.all_gather(part, 'zl', axis=0)  13.9 us
    all_gather x1, blocking collectives, shards(): x_full = lax.all_gather(xt, 'x', axis=0, tiled=True)  13.6 us
    all_gather x1, blocking collectives, shards(): g_full = lax.all_gather(cot_work, 'x', axis=0)  12.3 us
    all_gather x1, blocking collectives, shards(): own = lax.all_gather(part, 'y', axis=0)  11.4 us
    ppermute x1, starting transfers between devices, shards(): other = lax.ppermute(own, 'c', cores)  10.4 us
    ppermute x1, starting transfers between devices, shards(): got = lax.ppermute(send, 'c', cores)  9.61 us
    all_to_all x1, blocking collectives, shards(): parts = lax.all_to_all(parts, 'zl', 0, 0)  8.16 us
  transfers between devices with their start and end apart: 7, of which 3 were waited for; matrix products, arithmetic and copies ran while one was open for 0% of the time, Pallas kernels for 5%

profile of v2, /device:TPU:1, one launch (start us, length us, event | category | flops | bytes accessed | tf_op | source)
XLA Modules:
  0.0 145.8 jit_solution(15933185467324567202)
XLA Ops:
  0.6 0.0 copy-start
  0.6 1.0 copy-done
  1.7 0.0 copy-start.4
  1.7 0.7 copy-done.4
  2.3 0.0 copy-start.1
  2.3 0.0 copy-start.3
  2.3 0.9 shard_map.101
  3.2 4.6 %collective-permute-start = (bf16[320,320]{1,0:T(8,128)(2,1)S(1)}, bf16[320,320]{1,0:T(8,128)(2,1)S(1)}, u32[]{:S(2)}, u32[]{:S(2)}) collective-permute-start(bf16[320,320]{1,0:T(8,128)(2,1)S(1)} %shard_map.101), channel_id=1, source_target_pairs={{0,4},{4,8},{8,12},{12,16},{16,20},{20,24},{24,28},{28,32},{32,36}... | collective-permute-start | bytes 614408 | tf_op jit(solution)/shard_map/ppermute | solution.py:319
  7.8 0.7 reshape.17.gain_ref
  8.5 13.6 %all_gather.21.x_ref = bf16[1280,384]{1,0:T(8,128)(2,1)S(1)} all-gather(bf16[320,384]{1,0:T(8,128)(2,1)} %bitcast.17), channel_id=1, replica_groups=mesh['zh'=4,'zl'=4,'y'=4,'c'=2,'x'=4] {'x'}, dimensions={0}, use_global_device_ids=true | all-gather | bytes 1228800 | tf_op jit(solution)/shard_map/all_gather | solution.py:320
  22.1 0.0 collective-permute-done.got_ref
  22.1 0.5 shard_map.102.cot_ref
  22.6 12.3 %all-gather = bf16[1344,384]{1,0:T(8,128)(2,1)S(1)} all-gather(bf16[336,384]{1,0:T(8,128)(2,1)S(1)} %shard_map.102.cot_ref), channel_id=2, replica_groups=mesh['zh'=4,'zl'=4,'y'=4,'c'=2,'x'=4] {'x'}, dimensions={0}, use_global_device_ids=true | all-gather | bytes 1290240 | tf_op jit(solution)/shard_map/all_gather | solution.py:322
  34.9 0.0 copy-done.1
  34.9 0.0 copy-done.3
  34.9 4.0 %shard_map.103 = (bf16[16,25728]{1,0:T(8,128)(2,1)S(1)}, f32[16,25728]{1,0:T(8,128)S(1)}, bf16[480,384]{1,0:T(8,128)(2,1)S(1)}, bf16[160,384]{1,0:T(8,128)(2,1)S...) custom-call(bf16[1280,384]{1,0:T(8,128)(2,1)S(1)} %all_gather.21.x_ref, bf16[4,336,384]{2,1,0:T(8,128)(2,1)S(1)} %bitcast.16, ...), custom_call_target="tpu_custom_call" | custom-call | flops 1500000000 | bytes 1000000 | tf_op jit(solution)/shard_map/pallas_call | solution.py:324
  38.9 9.6 %collective-permute-start.1 = (bf16[16,25728]{1,0:T(8,128)(2,1)S(1)}, bf16[16,25728]{1,0:T(8,128)(2,1)S(1)}, u32[]{:S(2)}, u32[]{:S(2)}) collective-permute-start(bf16[16,25728]{1,0:T(8,128)(2,1)S(1)} %get-tuple-element.22), channel_id=1, source_target_pairs={{0,4},{4,0},{1,5},{5,1},{2,6},{6,2},{3,7},{7,3},{8,12},{12,8},{9,1... | collective-permute-start | bytes 2469896 | tf_op jit(solution)/shard_map/ppermute | solution.py:345
  48.5 3.0 %shard_map.104.heads_ref.heads_in = bf16[4,656,384]{2,1,0:T(8,128)(2,1)} custom-call(bf16[480,384]{1,0:T(8,128)(2,1)S(1)} %get-tuple-element.23.gp_ref, bf16[160,384]{1,0:T(8,128)(2,1)S(1)} %get-tuple-element.24.mx_ref, bf16[1280,384]{1,0:T(8,128)(2,1)S(1)} %all_gather.21.x_ref, bf16[480,1280]{1,0:T(8,128)(2,1)S(1)} %bitcast.15, ...), custom_call_target="tpu_custom_call" | custom-call | flops 700000000 | bytes 1000000 | tf_op jit(solution)/shard_map/pallas_call | solution.py:347
  51.5 0.0 collective-permute-done.1.got_ref
  51.5 0.2 shard_map.105
  51.7 15.4 %all_to_all.15.got_ref = bf16[4,16,6528]{2,1,0:T(8,128)(2,1)S(1)} all-to-all(bf16[4,16,6528]{2,1,0:T(8,128)(2,1)S(1)} %shard_map.105), channel_id=1, replica_groups=mesh['zh'=4,'zl'=4,'y'=4,'c'=2,'x'=4] {'y'}, dimensions={0} | all-to-all | bytes 1671168 | tf_op jit(solution)/shard_map/all_to_all | solution.py:361
  67.1 0.1 shard_map.106
  67.2 8.2 %all_to_all.16.got_ref = bf16[4,16,1792]{2,1,0:T(8,128)(2,1)S(1)} all-to-all(bf16[4,16,1792]{2,1,0:T(8,128)(2,1)S(1)} %shard_map.106), channel_id=1, replica_groups=mesh['zh'=4,'zl'=4,'y'=4,'c'=2,'x'=4] {'zl'}, dimensions={0} | all-to-all | bytes 458752 | tf_op jit(solution)/shard_map/all_to_all | solution.py:363
  75.4 8.1 %collective-permute-start.2 = (bf16[16,1792]{1,0:T(8,128)(2,1)S(1)}, bf16[16,1792]{1,0:T(8,128)(2,1)S(1)}, u32[]{:S(2)}, u32[]{:S(2)}) collective-permute-start(bf16[16,1792]{1,0:T(8,128)(2,1)S(1)} %shard_map.107.own_ref), channel_id=1, source_target_pairs={{0,128},{128,0},{256,384},{384,256},{1,129},{129,1},{257,385},{385... | collective-permute-start | bytes 172040 | tf_op jit(solution)/shard_map/ppermute | solution.py:365
  83.5 1.6 %collective-permute-done.2.got_ref = bf16[16,1792]{1,0:T(8,128)(2,1)S(1)} collective-permute-done((bf16[16,1792]{1,0:T(8,128)(2,1)S(1)}, bf16[16,1792]{1,0:T(8,128)(2,1)S(1)}, u32[]{:S(2)}, u32[]{:S(2)}) %collective-permute-start.2) | collective-permute-done | bytes 57376 | tf_op jit(solution)/shard_map/ppermute | solution.py:365
  85.1 8.1 %collective-permute-start.3 = (bf16[16,1792]{1,0:T(8,128)(2,1)S(1)}, bf16[16,1792]{1,0:T(8,128)(2,1)S(1)}, u32[]{:S(2)}, u32[]{:S(2)}) collective-permute-start(bf16[16,1792]{1,0:T(8,128)(2,1)S(1)} %shard_map.108.own_ref), channel_id=1, source_target_pairs={{128,256},{256,128},{384,0},{0,384},{129,257},{257,129},{385,1},{1... | collective-permute-start | bytes 172040 | tf_op jit(solution)/shard_map/ppermute | solution.py:367
  93.2 1.7 %collective-permute-done.3.got_ref = bf16[16,1792]{1,0:T(8,128)(2,1)S(1)} collective-permute-done((bf16[16,1792]{1,0:T(8,128)(2,1)S(1)}, bf16[16,1792]{1,0:T(8,128)(2,1)S(1)}, u32[]{:S(2)}, u32[]{:S(2)}) %collective-permute-start.3) | collective-permute-done | bytes 57376 | tf_op jit(solution)/shard_map/ppermute | solution.py:367
  94.9 0.7 shard_map.109
  95.6 0.0 copy-start.2
  95.7 4.5 %all-to-all-start.2 = ((bf16[4,656,384]{2,1,0:T(8,128)(2,1)}), bf16[4,656,384]{2,1,0:T(8,128)(2,1)S(1)}, u32[]{:S(2)}, u32[]{:S(2)}) async-start(bf16[4,656,384]{2,1,0:T(8,128)(2,1)} %get-tuple-element.27), calls=%async_computation.2 | async-start | bytes 4030464 | tf_op jit(solution)/shard_map/all_to_all | solution.py:376
  100.2 13.9 %all-gather.1 = bf16[64,1664]{1,0:T(8,128)(2,1)S(1)} all-gather(bf16[16,1664]{1,0:T(8,128)(2,1)S(1)} %get-tuple-element.31), channel_id=3, replica_groups=mesh['zh'=4,'zl'=4,'y'=4,'c'=2,'x'=4] {'zl'}, dimensions={0}, use_global_device_ids=true | all-gather | bytes 266240 | tf_op jit(solution)/shard_map/all_gather | solution.py:377
  114.1 11.4 %all-gather.2 = bf16[64,6400]{1,0:T(8,128)(2,1)S(1)} all-gather(bf16[16,6400]{1,0:T(8,128)(2,1)S(1)} %shard_map.112), channel_id=4, replica_groups=mesh['zh'=4,'zl'=4,'y'=4,'c'=2,'x'=4] {'y'}, dimensions={0}, use_global_device_ids=true | all-gather | bytes 1024000 | tf_op jit(solution)/shard_map/all_gather | solution.py:379
  125.5 10.4 %collective-permute-start.5 = (bf16[4,16,6400]{2,1,0:T(8,128)(2,1)S(1)}, bf16[4,16,6400]{2,1,0:T(8,128)(2,1)}, u32[]{:S(2)}, u32[]{:S(2)}) collective-permute-start(bf16[4,16,6400]{2,1,0:T(8,128)(2,1)S(1)} %bitcast.10), channel_id=1, source_target_pairs={{0,4},{4,0},{1,5},{5,1},{2,6},{6,2},{3,7},{7,3},{8,12},{12,8},{9,1... | collective-permute-start | bytes 2457608 | tf_op jit(solution)/shard_map/ppermute | solution.py:380
  135.9 0.0 all-to-all-done.2.got_ref
  135.9 0.0 copy-done.2
  135.9 0.9 shard_map.110
  136.8 1.9 %collective-permute-start.4 = (bf16[320,320]{1,0:T(8,128)(2,1)S(1)}, bf16[320,320]{1,0:T(8,128)(2,1)S(1)}, u32[]{:S(2)}, u32[]{:S(2)}) collective-permute-start(bf16[320,320]{1,0:T(8,128)(2,1)S(1)} %get-tuple-element.29), channel_id=1, source_target_pairs={{4,0},{8,4},{12,8},{16,12},{20,16},{24,20},{28,24},{32,28},{36,32}... | collective-permute-start | bytes 614408 | tf_op jit(solution)/shard_map/ppermute | solution.py:402
  138.7 1.2 shard_map.113
  139.9 0.0 collective-permute-done.5.ref
  139.9 0.0 copy-start.5
  140.0 2.4 %shard_map.114 = (f32[480,1280]{1,0:T(8,128)}, f32[160,1280]{1,0:T(8,128)}) custom-call(bf16[4,16,6400]{2,1,0:T(8,128)(2,1)} %collective-permute-done.5.ref, f32[480,1280]{1,0:T(8,128)} %get-tuple-element.32.qkv_in, f32[160,1280]{1,0:T(8,128)} %get-tuple-element.33.out_in), custom_call_target="tpu_custom_call", output_to_operand_aliasing={{0}: (1, {}), {1}: (2, {})} | custom-call | flops 1000000 | bytes 1000000 | tf_op jit(solution)/shard_map/pallas_call | solution.py:384
  142.3 2.0 %collective-permute-done.4.got_ref = bf16[320,320]{1,0:T(8,128)(2,1)S(1)} collective-permute-done((bf16[320,320]{1,0:T(8,128)(2,1)S(1)}, bf16[320,320]{1,0:T(8,128)(2,1)S(1)}, u32[]{:S(2)}, u32[]{:S(2)}) %collective-permute-start.4) | collective-permute-done | bytes 204832 | tf_op jit(solution)/shard_map/ppermute | solution.py:402
  144.3 0.0 copy-done.5
  144.3 1.5 %shard_map.111 = bf16[320,704]{1,0:T(8,128)(2,1)} custom-call(s32[1,128]{1,0:T(1,128)S(1)} %bitcast.22, bf16[320,384]{1,0:T(8,128)(2,1)S(1)} %get-tuple-element.28.y_ref, bf16[320,320]{1,0:T(8,128)(2,1)S(1)} %collective-permute-done.4.got_ref), custom_call_target="tpu_custom_call" | custom-call | flops 1000000 | bytes 1000000 | tf_op jit(solution)/shard_map/pallas_call | solution.py:403
  (3 shorter events, 0.1 us)
Async XLA Ops:
  0.6 1.0 copy-start
  1.7 0.7 copy-start.4
  2.3 32.6 %copy-start.1 = (bf16[1280,480]{0,1:T(8,128)(2,1)S(1)}, bf16[1280,480]{0,1:T(8,128)(2,1)}, u32[]{:S(2)}) copy-start(bf16[1280,480]{0,1:T(8,128)(2,1)} %param.8) | copy-start | bytes 3686404
  2.3 32.6 %copy-start.3 = (bf16[160,1280]{1,0:T(8,128)(2,1)S(1)}, bf16[160,1280]{1,0:T(8,128)(2,1)}, u32[]{:S(2)}) copy-start(bf16[160,1280]{1,0:T(8,128)(2,1)} %wo_ref.3) | copy-start | bytes 1228804
  3.2 18.9 %collective-permute-start = (bf16[320,320]{1,0:T(8,128)(2,1)S(1)}, bf16[320,320]{1,0:T(8,128)(2,1)S(1)}, u32[]{:S(2)}, u32[]{:S(2)}) collective-permute-start(bf16[320,320]{1,0:T(8,128)(2,1)S(1)} %shard_map.101), channel_id=1, source_target_pairs={{0,4},{4,8},{8,12},{12,16},{16,20},{20,24},{24,28},{28,32},{32,36}... | collective-permute-start | bytes 614408 | tf_op jit(solution)/shard_map/ppermute | solution.py:319
  38.9 12.6 %collective-permute-start.1 = (bf16[16,25728]{1,0:T(8,128)(2,1)S(1)}, bf16[16,25728]{1,0:T(8,128)(2,1)S(1)}, u32[]{:S(2)}, u32[]{:S(2)}) collective-permute-start(bf16[16,25728]{1,0:T(8,128)(2,1)S(1)} %get-tuple-element.22), channel_id=1, source_target_pairs={{0,4},{4,0},{1,5},{5,1},{2,6},{6,2},{3,7},{7,3},{8,12},{12,8},{9,1... | collective-permute-start | bytes 2469896 | tf_op jit(solution)/shard_map/ppermute | solution.py:345
  75.4 9.7 %collective-permute-start.2 = (bf16[16,1792]{1,0:T(8,128)(2,1)S(1)}, bf16[16,1792]{1,0:T(8,128)(2,1)S(1)}, u32[]{:S(2)}, u32[]{:S(2)}) collective-permute-start(bf16[16,1792]{1,0:T(8,128)(2,1)S(1)} %shard_map.107.own_ref), channel_id=1, source_target_pairs={{0,128},{128,0},{256,384},{384,256},{1,129},{129,1},{257,385},{385... | collective-permute-start | bytes 172040 | tf_op jit(solution)/shard_map/ppermute | solution.py:365
  85.1 9.8 %collective-permute-start.3 = (bf16[16,1792]{1,0:T(8,128)(2,1)S(1)}, bf16[16,1792]{1,0:T(8,128)(2,1)S(1)}, u32[]{:S(2)}, u32[]{:S(2)}) collective-permute-start(bf16[16,1792]{1,0:T(8,128)(2,1)S(1)} %shard_map.108.own_ref), channel_id=1, source_target_pairs={{128,256},{256,128},{384,0},{0,384},{129,257},{257,129},{385,1},{1... | collective-permute-start | bytes 172040 | tf_op jit(solution)/shard_map/ppermute | solution.py:367
  95.6 40.3 %copy-start.2 = (bf16[384,320]{0,1:T(8,128)(2,1)S(1)}, bf16[384,320]{0,1:T(8,128)(2,1)}, u32[]{:S(2)}) copy-start(bf16[384,320]{0,1:T(8,128)(2,1)} %param.6) | copy-start | bytes 737284
  95.7 40.3 %all-to-all-start.2 = ((bf16[4,656,384]{2,1,0:T(8,128)(2,1)}), bf16[4,656,384]{2,1,0:T(8,128)(2,1)S(1)}, u32[]{:S(2)}, u32[]{:S(2)}) async-start(bf16[4,656,384]{2,1,0:T(8,128)(2,1)} %get-tuple-element.27), calls=%async_computation.2 | async-start | bytes 4030464 | tf_op jit(solution)/shard_map/all_to_all | solution.py:376
  125.5 14.5 %collective-permute-start.5 = (bf16[4,16,6400]{2,1,0:T(8,128)(2,1)S(1)}, bf16[4,16,6400]{2,1,0:T(8,128)(2,1)}, u32[]{:S(2)}, u32[]{:S(2)}) collective-permute-start(bf16[4,16,6400]{2,1,0:T(8,128)(2,1)S(1)} %bitcast.10), channel_id=1, source_target_pairs={{0,4},{4,0},{1,5},{5,1},{2,6},{6,2},{3,7},{7,3},{8,12},{12,8},{9,1... | collective-permute-start | bytes 2457608 | tf_op jit(solution)/shard_map/ppermute | solution.py:380
  136.8 7.5 %collective-permute-start.4 = (bf16[320,320]{1,0:T(8,128)(2,1)S(1)}, bf16[320,320]{1,0:T(8,128)(2,1)S(1)}, u32[]{:S(2)}, u32[]{:S(2)}) collective-permute-start(bf16[320,320]{1,0:T(8,128)(2,1)S(1)} %get-tuple-element.29), channel_id=1, source_target_pairs={{4,0},{8,4},{12,8},{16,12},{20,16},{24,20},{28,24},{32,28},{36,32}... | collective-permute-start | bytes 614408 | tf_op jit(solution)/shard_map/ppermute | solution.py:402
  139.9 4.3 %copy-start.5 = (s32[128]{0:T(128)S(1)}, s32[128]{0:T(128)}, u32[]{:S(2)}) copy-start(s32[128]{0:T(128)} %param.11) | copy-start | bytes 1540

commit v3 on v2

--- a/solution.py
+++ b/solution.py
@@ -188,7 +188,7 @@
         copy.wait()
 
 
-def core_sum(keep_ref, got_ref, heads_ref, out_ref):
+def core_sum(keep_ref, got_ref, out_ref):
     gain = (keep_ref[:, HALF:] + got_ref[:, HALF:].astype(F32)).astype(BF16)
     for b in range(4):
         s = slice(Y_LANES * b, Y_LANES * (b + 1))
@@ -215,14 +215,18 @@
     out_ref[...] = sum_of_four(got_ref, slice(None)).astype(BF16)
 
 
-def pair_sum(own_ref, got_ref, out_ref):
+def pair_sum(own_ref, got_ref, heads_ref, out_ref):
     out_ref[...] = (own_ref[...].astype(F32) + got_ref[...].astype(F32)).astype(BF16)
 
 
-def zh_sum(own_ref, got_ref, heads_in, out_ref, heads_ref, lines, sems):
+def zh_sum(own_ref, got_ref, out_ref, tile_ref):
     total = own_ref[...].astype(F32) + got_ref[...].astype(F32)
     out_ref[...] = total[:, :Z_LANES].astype(BF16)
-    tile = total[:, Z_LANES:]
+    tile_ref[...] = total[:, Z_LANES:]
+
+
+def gain_lines(tile_ref, heads_in, heads_ref, lines, sems):
+    tile = tile_ref[...]
     line = jnp.concatenate([tile[i:i + 1, :] for i in range(10)], axis=1)
     row = lax.broadcasted_iota(jnp.int32, (16, FX), 0)
     copies = []
@@ -237,39 +241,64 @@
         copy.wait()
 
 
-def z_pack(got_ref, out_ref):
-    for b in range(4):
-        lo, hi = Z_LANES * b, min(Z_LANES * (b + 1), Y_LANES)
-        out_ref[:, lo:hi] = got_ref[b, :, :hi - lo]
-
-
-def weight_rows(ref, half, qkv_ref, out_ref, buf, sems):
-    for b in range(4):
+def z_pair(own_ref, got_ref, out_ref):
+    first = lax.axis_index("zl") < 2
+
+    @pl.when(first)
+    def _():
+        out_ref[0] = own_ref[...]
+        out_ref[1] = got_ref[...]
+
+    @pl.when(jnp.logical_not(first))
+    def _():
+        out_ref[0] = got_ref[...]
+        out_ref[1] = own_ref[...]
+
+
+def z_pack(own_ref, got_ref, out_ref):
+    zl = lax.axis_index("zl")
+    outer = (zl == 0) | (zl == 3)
+
+    def place(outer_ref, inner_ref):
+        for n, shard in enumerate((outer_ref.at[0], inner_ref.at[0], inner_ref.at[1], outer_ref.at[1])):
+            lo, hi = Z_LANES * n, min(Z_LANES * (n + 1), Y_LANES)
+            out_ref[:, lo:hi] = shard[:, :hi - lo]
+
+    @pl.when(outer)
+    def _():
+        place(own_ref, got_ref)
+
+    @pl.when(jnp.logical_not(outer))
+    def _():
+        place(got_ref, own_ref)
+
+
+def weights_out(own_ref, other_any, qkv_ref, out_ref, other, buf, sems):
+    core = lax.axis_index("c")
+    loads = [pltpu.make_async_copy(other_any.at[b], other.at[b], sems.at[8 + b]) for b in range(4)]
+    for load in loads:
+        load.start()
+    for n in range(8):
+        b = n % 4
+        if n >= 4:
+            loads[b].wait()
+        ref, half = (own_ref, core) if n < 4 else (other, 1 - core)
         for o in range(5):
-            i = 5 * b + o
-            buf[16 * i:16 * (i + 1), :] = ref[b, :, FEAT * o:FEAT * (o + 1)].astype(F32)
-        chunk = buf.at[pl.ds(80 * b, 80)]
+            row = 80 * n + 16 * o
+            buf[row:row + 16, :] = ref[b, :, FEAT * o:FEAT * (o + 1)].astype(F32)
+        chunk = buf.at[pl.ds(80 * n, 80)]
 
         @pl.when(half == 0)
         def _():
-            pltpu.make_async_copy(chunk, qkv_ref.at[pl.ds(80 * b, 80)], sems.at[b]).start()
+            pltpu.make_async_copy(chunk, qkv_ref.at[pl.ds(80 * b, 80)], sems.at[n]).start()
 
         @pl.when(half == 1)
         def _():
             target = qkv_ref.at[pl.ds(320 + 80 * b, 80)] if b < 2 else out_ref.at[pl.ds(80 * (b - 2), 80)]
-            pltpu.make_async_copy(chunk, target, sems.at[b]).start()
-
-    for b in range(4):
-        chunk = buf.at[pl.ds(80 * b, 80)]
-        pltpu.make_async_copy(chunk, qkv_ref.at[pl.ds(0, 80)], sems.at[b]).wait()
-
-
-def weight_own(ref, qkv_ref, out_ref, buf, sems):
-    weight_rows(ref, lax.axis_index("c"), qkv_ref, out_ref, buf, sems)
-
-
-def weight_other(ref, qkv_in, out_in, qkv_ref, out_ref, buf, sems):
-    weight_rows(ref, 1 - lax.axis_index("c"), qkv_ref, out_ref, buf, sems)
+            pltpu.make_async_copy(chunk, target, sems.at[n]).start()
+
+    for n in range(8):
+        pltpu.make_async_copy(buf.at[pl.ds(80 * n, 80)], qkv_ref.at[pl.ds(0, 80)], sems.at[n]).wait()
 
 
 def heads_sum(got_ref, x_ref, cot_ref, gain_ref, y_ref, send_ref, grad_ref, gain_grad_ref):
@@ -357,38 +386,41 @@
         flops=700000000,
     )(gp, mx, x_full, wq, w_out, gcol, rms)
 
-    parts = call(core_sum, struct((4, 16, Y_LANES + TILE), BF16), ins=(VMEM, VMEM, HBM))(keep, got, heads)
+    parts = call(core_sum, struct((4, 16, Y_LANES + TILE), BF16))(keep, got)
     parts = lax.all_to_all(parts, "y", 0, 0)
     parts = call(y_sum, struct((4, 16, Z_LANES + TILE), BF16))(parts)
     parts = lax.all_to_all(parts, "zl", 0, 0)
     part = call(zl_sum, struct((16, Z_LANES + TILE), BF16))(parts)
     got = lax.ppermute(part, "zh", [(0, 1), (1, 0), (2, 3), (3, 2)])
-    part = call(pair_sum, struct((16, Z_LANES + TILE), BF16))(part, got)
+    part = call(pair_sum, struct((16, Z_LANES + TILE), BF16), ins=(VMEM, VMEM, HBM))(part, got, heads)
     got = lax.ppermute(part, "zh", [(1, 2), (2, 1), (3, 0), (0, 3)])
-    part, heads = call(
-        zh_sum,
-        (struct((16, Z_LANES), BF16), heads_shape),
-        ins=(VMEM, VMEM, HBM),
-        outs=(VMEM, HBM),
-        aliases={2: 1},
+    part, tile = call(zh_sum, (struct((16, Z_LANES), BF16), struct((16, TILE), F32)))(part, got)
+    got = lax.ppermute(part, "zl", [(0, 3), (3, 0), (1, 2), (2, 1)])
+    heads = call(
+        gain_lines,
+        heads_shape,
+        ins=(VMEM, HBM),
+        outs=HBM,
+        aliases={1: 0},
         scratch=(pltpu.VMEM((4, 16, ROWS), BF16), pltpu.SemaphoreType.DMA((4,))),
-    )(part, got, heads)
+    )(tile, heads)
     heads = lax.all_to_all(heads, "x", 0, 0)
-    parts = lax.all_gather(part, "zl", axis=0)
-    part = call(z_pack, struct((16, Y_LANES), BF16))(parts)
+    pair = call(z_pair, struct((2, 16, Z_LANES), BF16), flops=30000000000)(part, got)
+    got = lax.ppermute(pair, "zl", [(0, 1), (1, 0), (2, 3), (3, 2)])
+    part = call(z_pack, struct((16, Y_LANES), BF16))(pair, got)
     own = lax.all_gather(part, "y", axis=0)
     other = lax.ppermute(own, "c", cores)
-    weight_shapes = (struct((QKV, FEAT), F32), struct((ATT, FEAT), F32))
-    weight_scratch = (pltpu.VMEM((320, FEAT), F32), pltpu.SemaphoreType.DMA((4,)))
-    weights = call(weight_own, weight_shapes, outs=(ANY, ANY), scratch=weight_scratch)(own)
     qkv_grad, out_grad = call(
-        weight_other,
-        weight_shapes,
-        ins=(VMEM, ANY, ANY),
+        weights_out,
+        (struct((QKV, FEAT), F32), struct((ATT, FEAT), F32)),
+        ins=(VMEM, ANY),
         outs=(ANY, ANY),
-        aliases={1: 0, 2: 1},
-        scratch=weight_scratch,
-    )(other, *weights)
+        scratch=(
+            pltpu.VMEM((4, 16, Y_LANES), BF16),
+            pltpu.VMEM((QKV + ATT, FEAT), F32),
+            pltpu.SemaphoreType.DMA((12,)),
+        ),
+    )(own, other)
 
     y_work, send, x_grad, gain_grad = call(
         heads_sum,

time: 146 us -> 143 us (0.979)
  blocking collectives: 74.7 us -> 60.9 us
  starting transfers between devices: 47.3 us -> 53 us
  waiting for transfers between devices: 5.22 us -> 10.6 us
    all_gather x1 -> x0, blocking collectives: 13.9 us -> none  [shards(): parts = lax.all_gather(part, 'zl', axis=0)]
    ppermute x0 -> x2, starting transfers between devices: none -> 7.8 us  [the longest x1 5.74 us: shards(): got = lax.ppermute(part, 'zl', [(0, 3), (3, 0), (1, 2), (2, 1)])]
    ppermute x0 -> x2, waiting for transfers between devices: none -> 3.52 us  [the longest x1 3.52 us: shards(): got = lax.ppermute(pair, 'zl', [(0, 1), (1, 0), (2, 3), (3, 2)])]
    ppermute x1, waiting for transfers between devices: 0.01 us -> 1.94 us  [shards(): got = lax.ppermute(send, 'c', cores)]
    ppermute x1, waiting for transfers between devices: 1.56 us -> 0.01 us  [shards(): got = lax.ppermute(part, 'zh', [(0, 1), (1, 0), (2, 3), (3, 2)])]
    ppermute x1, starting transfers between devices: 8.11 us -> 6.64 us  [shards(): got = lax.ppermute(part, 'zh', [(1, 2), (2, 1), (3, 0), (0, 3)])]
    pallas_call x6 -> x7, Pallas kernels: 4.55 us -> 3.74 us  [the longest x1 2.74 us: shards(): call(weights_out, (struct((QKV, FEAT), F32), struct((ATT, FEAT), F32)), i...]
  transfers between devices with their start and end apart: 7 -> 9, of which waited for: 3 -> 4; matrix products, arithmetic and copies ran while one was open for 0% -> 0% of each run, Pallas kernels for 5% -> 5%
where the time goes in v3:
time: 143 us; the launch traced here: 142 us
  blocking collectives  60.9 us (43%)
  starting transfers between devices  53 us (37%)
  Pallas kernels  14.6 us (10%)
  waiting for transfers between devices  10.6 us (7%)
  local copies, waits for them, and re-layouts  2.38 us (2%)
    all_to_all x1, blocking collectives, shards(): parts = lax.all_to_all(parts, 'y', 0, 0)  14.7 us
    all_gather x1, blocking collectives, shards(): x_full = lax.all_gather(xt, 'x', axis=0, tiled=True)  13.6 us
    all_gather x1, blocking collectives, shards(): g_full = lax.all_gather(cot_work, 'x', axis=0)  12.3 us
    all_gather x1, blocking collectives, shards(): own = lax.all_gather(part, 'y', axis=0)  12.3 us
    ppermute x1, starting transfers between devices, shards(): got = lax.ppermute(send, 'c', cores)  9.61 us
    ppermute x1, starting transfers between devices, shards(): other = lax.ppermute(own, 'c', cores)  9.51 us
    ppermute x1, starting transfers between devices, shards(): got = lax.ppermute(part, 'zh', [(0, 1), (1, 0), (2, 3), (3, 2)])  8.69 us
    all_to_all x1, blocking collectives, shards(): parts = lax.all_to_all(parts, 'zl', 0, 0)  8.15 us
  transfers between devices with their start and end apart: 9, of which 4 were waited for; matrix products, arithmetic and copies ran while one was open for 0% of the time, Pallas kernels for 5%

profile of v3, /device:TPU:1, one launch (start us, length us, event | category | flops | bytes accessed | tf_op | source)
XLA Modules:
  0.0 142.3 jit_solution(465386384188029443)
XLA Ops:
  0.6 0.0 copy-start
  0.6 1.0 copy-done
  1.7 0.0 copy-start.4
  1.7 0.7 copy-done.4
  2.3 0.0 copy-start.1
  2.3 0.0 copy-start.3
  2.3 0.9 shard_map.101
  3.2 4.6 %collective-permute-start = (bf16[320,320]{1,0:T(8,128)(2,1)S(1)}, bf16[320,320]{1,0:T(8,128)(2,1)S(1)}, u32[]{:S(2)}, u32[]{:S(2)}) collective-permute-start(bf16[320,320]{1,0:T(8,128)(2,1)S(1)} %shard_map.101), channel_id=1, source_target_pairs={{0,4},{4,8},{8,12},{12,16},{16,20},{20,24},{24,28},{28,32},{32,36}... | collective-permute-start | bytes 614408 | tf_op jit(solution)/shard_map/ppermute | solution.py:348
  7.8 0.7 reshape.17.gain_ref
  8.5 13.6 %all_gather.15.x_ref = bf16[1280,384]{1,0:T(8,128)(2,1)S(1)} all-gather(bf16[320,384]{1,0:T(8,128)(2,1)} %bitcast.16), channel_id=1, replica_groups=mesh['zh'=4,'zl'=4,'y'=4,'c'=2,'x'=4] {'x'}, dimensions={0}, use_global_device_ids=true | all-gather | bytes 1228800 | tf_op jit(solution)/shard_map/all_gather | solution.py:349
  22.1 0.0 collective-permute-done.got_ref
  22.1 0.5 shard_map.102.cot_ref
  22.6 12.3 %all-gather = bf16[1344,384]{1,0:T(8,128)(2,1)S(1)} all-gather(bf16[336,384]{1,0:T(8,128)(2,1)S(1)} %shard_map.102.cot_ref), channel_id=2, replica_groups=mesh['zh'=4,'zl'=4,'y'=4,'c'=2,'x'=4] {'x'}, dimensions={0}, use_global_device_ids=true | all-gather | bytes 1290240 | tf_op jit(solution)/shard_map/all_gather | solution.py:351
  34.9 0.0 copy-done.1
  34.9 0.0 copy-done.3
  34.9 4.0 %shard_map.103 = (bf16[16,25728]{1,0:T(8,128)(2,1)S(1)}, f32[16,25728]{1,0:T(8,128)S(1)}, bf16[480,384]{1,0:T(8,128)(2,1)S(1)}, bf16[160,384]{1,0:T(8,128)(2,1)S...) custom-call(bf16[1280,384]{1,0:T(8,128)(2,1)S(1)} %all_gather.15.x_ref, bf16[4,336,384]{2,1,0:T(8,128)(2,1)S(1)} %bitcast.15, ...), custom_call_target="tpu_custom_call" | custom-call | flops 1500000000 | bytes 1000000 | tf_op jit(solution)/shard_map/pallas_call | solution.py:353
  38.9 9.6 %collective-permute-start.1 = (bf16[16,25728]{1,0:T(8,128)(2,1)S(1)}, bf16[16,25728]{1,0:T(8,128)(2,1)S(1)}, u32[]{:S(2)}, u32[]{:S(2)}) collective-permute-start(bf16[16,25728]{1,0:T(8,128)(2,1)S(1)} %get-tuple-element.20), channel_id=1, source_target_pairs={{0,4},{4,0},{1,5},{5,1},{2,6},{6,2},{3,7},{7,3},{8,12},{12,8},{9,1... | collective-permute-start | bytes 2469896 | tf_op jit(solution)/shard_map/ppermute | solution.py:374
  48.5 1.9 %collective-permute-done.1.got_ref = bf16[16,25728]{1,0:T(8,128)(2,1)S(1)} collective-permute-done((bf16[16,25728]{1,0:T(8,128)(2,1)S(1)}, bf16[16,25728]{1,0:T(8,128)(2,1)S(1)}, u32[]{:S(2)}, u32[]{:S(2)}) %collective-permute-start.1) | collective-permute-done | bytes 823328 | tf_op jit(solution)/shard_map/ppermute | solution.py:374
  50.4 0.2 shard_map.104
  50.6 14.7 %all_to_all.15.got_ref = bf16[4,16,6528]{2,1,0:T(8,128)(2,1)S(1)} all-to-all(bf16[4,16,6528]{2,1,0:T(8,128)(2,1)S(1)} %shard_map.104), channel_id=1, replica_groups=mesh['zh'=4,'zl'=4,'y'=4,'c'=2,'x'=4] {'y'}, dimensions={0} | all-to-all | bytes 1671168 | tf_op jit(solution)/shard_map/all_to_all | solution.py:390
  65.3 0.1 shard_map.105
  65.4 8.1 %all_to_all.16.got_ref = bf16[4,16,1792]{2,1,0:T(8,128)(2,1)S(1)} all-to-all(bf16[4,16,1792]{2,1,0:T(8,128)(2,1)S(1)} %shard_map.105), channel_id=1, replica_groups=mesh['zh'=4,'zl'=4,'y'=4,'c'=2,'x'=4] {'zl'}, dimensions={0} | all-to-all | bytes 458752 | tf_op jit(solution)/shard_map/all_to_all | solution.py:392
  73.6 8.7 %collective-permute-start.2 = (bf16[16,1792]{1,0:T(8,128)(2,1)S(1)}, bf16[16,1792]{1,0:T(8,128)(2,1)S(1)}, u32[]{:S(2)}, u32[]{:S(2)}) collective-permute-start(bf16[16,1792]{1,0:T(8,128)(2,1)S(1)} %shard_map.106.own_ref), channel_id=1, source_target_pairs={{0,128},{128,0},{256,384},{384,256},{1,129},{129,1},{257,385},{385... | collective-permute-start | bytes 172040 | tf_op jit(solution)/shard_map/ppermute | solution.py:394
  82.3 3.0 %shard_map.107.heads_ref.heads_in = bf16[4,656,384]{2,1,0:T(8,128)(2,1)} custom-call(bf16[480,384]{1,0:T(8,128)(2,1)S(1)} %get-tuple-element.21.gp_ref, bf16[160,384]{1,0:T(8,128)(2,1)S(1)} %get-tuple-element.22.mx_ref, bf16[1280,384]{1,0:T(8,128)(2,1)S(1)} %all_gather.15.x_ref, bf16[480,1280]{1,0:T(8,128)(2,1)S(1)} %bitcast.14, ...), custom_call_target="tpu_custom_call" | custom-call | flops 700000000 | bytes 1000000 | tf_op jit(solution)/shard_map/pallas_call | solution.py:376
  85.3 0.0 collective-permute-done.2.got_ref
  85.3 6.6 %collective-permute-start.3 = (bf16[16,1792]{1,0:T(8,128)(2,1)S(1)}, bf16[16,1792]{1,0:T(8,128)(2,1)S(1)}, u32[]{:S(2)}, u32[]{:S(2)}) collective-permute-start(bf16[16,1792]{1,0:T(8,128)(2,1)S(1)} %shard_map.108.own_ref), channel_id=1, source_target_pairs={{128,256},{256,128},{384,0},{0,384},{129,257},{257,129},{385,1},{1... | collective-permute-start | bytes 172040 | tf_op jit(solution)/shard_map/ppermute | solution.py:396
  92.0 2.2 %collective-permute-done.3.got_ref = bf16[16,1792]{1,0:T(8,128)(2,1)S(1)} collective-permute-done((bf16[16,1792]{1,0:T(8,128)(2,1)S(1)}, bf16[16,1792]{1,0:T(8,128)(2,1)S(1)}, u32[]{:S(2)}, u32[]{:S(2)}) %collective-permute-start.3) | collective-permute-done | bytes 57376 | tf_op jit(solution)/shard_map/ppermute | solution.py:396
  94.2 5.7 %collective-permute-start.5 = (bf16[16,1664]{1,0:T(8,128)(2,1)S(1)}, bf16[16,1664]{1,0:T(8,128)(2,1)S(1)}, u32[]{:S(2)}, u32[]{:S(2)}) collective-permute-start(bf16[16,1664]{1,0:T(8,128)(2,1)S(1)} %get-tuple-element.29.own_ref), channel_id=1, source_target_pairs={{0,96},{96,0},{32,64},{64,32},{1,97},{97,1},{33,65},{65,33},{2,98}... | collective-permute-start | bytes 159752 | tf_op jit(solution)/shard_map/ppermute | solution.py:398
  100.0 0.7 shard_map.110
  100.7 4.3 %all-to-all-start.2 = ((bf16[4,656,384]{2,1,0:T(8,128)(2,1)}), bf16[4,656,384]{2,1,0:T(8,128)(2,1)S(1)}, u32[]{:S(2)}, u32[]{:S(2)}) async-start(bf16[4,656,384]{2,1,0:T(8,128)(2,1)} %shard_map.110), calls=%async_computation.2 | async-start | bytes 4030464 | tf_op jit(solution)/shard_map/all_to_all | solution.py:407
  105.0 0.0 copy-start.2
  105.0 0.0 collective-permute-done.5.got_ref
  105.0 2.1 %collective-permute-start.6 = (bf16[2,16,1664]{2,1,0:T(8,128)(2,1)S(1)}, bf16[2,16,1664]{2,1,0:T(8,128)(2,1)S(1)}, u32[]{:S(2)}, u32[]{:S(2)}) collective-permute-start(bf16[2,16,1664]{2,1,0:T(8,128)(2,1)S(1)} %shard_map.113.own_ref), channel_id=1, source_target_pairs={{0,32},{32,0},{64,96},{96,64},{1,33},{33,1},{65,97},{97,65},{2,34}... | collective-permute-start | bytes 319496 | tf_op jit(solution)/shard_map/ppermute | solution.py:409
  107.1 3.5 %collective-permute-done.6.got_ref = bf16[2,16,1664]{2,1,0:T(8,128)(2,1)S(1)} collective-permute-done((bf16[2,16,1664]{2,1,0:T(8,128)(2,1)S(1)}, bf16[2,16,1664]{2,1,0:T(8,128)(2,1)S(1)}, u32[]{:S(2)}, u32[]{:S(2)}) %collective-permute-start.6) | collective-permute-done | bytes 106528 | tf_op jit(solution)/shard_map/ppermute | solution.py:409
  110.6 12.3 %all-gather.1 = bf16[64,6400]{1,0:T(8,128)(2,1)S(1)} all-gather(bf16[16,6400]{1,0:T(8,128)(2,1)S(1)} %shard_map.114), channel_id=3, replica_groups=mesh['zh'=4,'zl'=4,'y'=4,'c'=2,'x'=4] {'y'}, dimensions={0}, use_global_device_ids=true | all-gather | bytes 1024000 | tf_op jit(solution)/shard_map/all_gather | solution.py:411
  122.9 0.0 copy-start.5
  122.9 9.5 %collective-permute-start.7 = (bf16[4,16,6400]{2,1,0:T(8,128)(2,1)S(1)}, bf16[4,16,6400]{2,1,0:T(8,128)(2,1)}, u32[]{:S(2)}, u32[]{:S(2)}) collective-permute-start(bf16[4,16,6400]{2,1,0:T(8,128)(2,1)S(1)} %bitcast.9), channel_id=1, source_target_pairs={{0,4},{4,0},{1,5},{5,1},{2,6},{6,2},{3,7},{7,3},{8,12},{12,8},{9,1... | collective-permute-start | bytes 2457608 | tf_op jit(solution)/shard_map/ppermute | solution.py:412
  132.4 0.0 all-to-all-done.2.got_ref
  132.4 0.0 copy-done.2
  132.4 0.9 shard_map.111
  133.3 1.9 %collective-permute-start.4 = (bf16[320,320]{1,0:T(8,128)(2,1)S(1)}, bf16[320,320]{1,0:T(8,128)(2,1)S(1)}, u32[]{:S(2)}, u32[]{:S(2)}) collective-permute-start(bf16[320,320]{1,0:T(8,128)(2,1)S(1)} %get-tuple-element.27), channel_id=1, source_target_pairs={{4,0},{8,4},{12,8},{16,12},{20,16},{24,20},{28,24},{32,28},{36,32}... | collective-permute-start | bytes 614408 | tf_op jit(solution)/shard_map/ppermute | solution.py:434
  135.2 0.0 collective-permute-done.7.other_any
  135.2 2.7 %shard_map.115 = (f32[480,1280]{1,0:T(8,128)}, f32[160,1280]{1,0:T(8,128)}) custom-call(bf16[4,16,6400]{2,1,0:T(8,128)(2,1)S(1)} %bitcast.10, bf16[4,16,6400]{2,1,0:T(8,128)(2,1)} %collective-permute-done.7.other_any), custom_call_target="tpu_custom_call" | custom-call | flops 1000000 | bytes 1000000 | tf_op jit(solution)/shard_map/pallas_call | solution.py:413
  138.0 2.8 %collective-permute-done.4.got_ref = bf16[320,320]{1,0:T(8,128)(2,1)S(1)} collective-permute-done((bf16[320,320]{1,0:T(8,128)(2,1)S(1)}, bf16[320,320]{1,0:T(8,128)(2,1)S(1)}, u32[]{:S(2)}, u32[]{:S(2)}) %collective-permute-start.4) | collective-permute-done | bytes 204832 | tf_op jit(solution)/shard_map/ppermute | solution.py:434
  140.8 0.0 copy-done.5
  140.8 1.5 %shard_map.112 = bf16[320,704]{1,0:T(8,128)(2,1)} custom-call(s32[1,128]{1,0:T(1,128)S(1)} %bitcast.20, bf16[320,384]{1,0:T(8,128)(2,1)S(1)} %get-tuple-element.26.y_ref, bf16[320,320]{1,0:T(8,128)(2,1)S(1)} %collective-permute-done.4.got_ref), custom_call_target="tpu_custom_call" | custom-call | flops 1000000 | bytes 1000000 | tf_op jit(solution)/shard_map/pallas_call | solution.py:435
  (5 shorter events, 0.1 us)
Async XLA Ops:
  0.6 1.0 copy-start
  1.7 0.7 copy-start.4
  2.3 32.6 %copy-start.1 = (bf16[1280,480]{0,1:T(8,128)(2,1)S(1)}, bf16[1280,480]{0,1:T(8,128)(2,1)}, u32[]{:S(2)}) copy-start(bf16[1280,480]{0,1:T(8,128)(2,1)} %param.8) | copy-start | bytes 3686404
  2.3 32.6 %copy-start.3 = (bf16[160,1280]{1,0:T(8,128)(2,1)S(1)}, bf16[160,1280]{1,0:T(8,128)(2,1)}, u32[]{:S(2)}) copy-start(bf16[160,1280]{1,0:T(8,128)(2,1)} %wo_ref.3) | copy-start | bytes 1228804
  3.2 18.9 %collective-permute-start = (bf16[320,320]{1,0:T(8,128)(2,1)S(1)}, bf16[320,320]{1,0:T(8,128)(2,1)S(1)}, u32[]{:S(2)}, u32[]{:S(2)}) collective-permute-start(bf16[320,320]{1,0:T(8,128)(2,1)S(1)} %shard_map.101), channel_id=1, source_target_pairs={{0,4},{4,8},{8,12},{12,16},{16,20},{20,24},{24,28},{28,32},{32,36}... | collective-permute-start | bytes 614408 | tf_op jit(solution)/shard_map/ppermute | solution.py:348
  38.9 11.6 %collective-permute-start.1 = (bf16[16,25728]{1,0:T(8,128)(2,1)S(1)}, bf16[16,25728]{1,0:T(8,128)(2,1)S(1)}, u32[]{:S(2)}, u32[]{:S(2)}) collective-permute-start(bf16[16,25728]{1,0:T(8,128)(2,1)S(1)} %get-tuple-element.20), channel_id=1, source_target_pairs={{0,4},{4,0},{1,5},{5,1},{2,6},{6,2},{3,7},{7,3},{8,12},{12,8},{9,1... | collective-permute-start | bytes 2469896 | tf_op jit(solution)/shard_map/ppermute | solution.py:374
  73.6 11.7 %collective-permute-start.2 = (bf16[16,1792]{1,0:T(8,128)(2,1)S(1)}, bf16[16,1792]{1,0:T(8,128)(2,1)S(1)}, u32[]{:S(2)}, u32[]{:S(2)}) collective-permute-start(bf16[16,1792]{1,0:T(8,128)(2,1)S(1)} %shard_map.106.own_ref), channel_id=1, source_target_pairs={{0,128},{128,0},{256,384},{384,256},{1,129},{129,1},{257,385},{385... | collective-permute-start | bytes 172040 | tf_op jit(solution)/shard_map/ppermute | solution.py:394
  85.3 8.9 %collective-permute-start.3 = (bf16[16,1792]{1,0:T(8,128)(2,1)S(1)}, bf16[16,1792]{1,0:T(8,128)(2,1)S(1)}, u32[]{:S(2)}, u32[]{:S(2)}) collective-permute-start(bf16[16,1792]{1,0:T(8,128)(2,1)S(1)} %shard_map.108.own_ref), channel_id=1, source_target_pairs={{128,256},{256,128},{384,0},{0,384},{129,257},{257,129},{385,1},{1... | collective-permute-start | bytes 172040 | tf_op jit(solution)/shard_map/ppermute | solution.py:396
  94.2 10.8 %collective-permute-start.5 = (bf16[16,1664]{1,0:T(8,128)(2,1)S(1)}, bf16[16,1664]{1,0:T(8,128)(2,1)S(1)}, u32[]{:S(2)}, u32[]{:S(2)}) collective-permute-start(bf16[16,1664]{1,0:T(8,128)(2,1)S(1)} %get-tuple-element.29.own_ref), channel_id=1, source_target_pairs={{0,96},{96,0},{32,64},{64,32},{1,97},{97,1},{33,65},{65,33},{2,98}... | collective-permute-start | bytes 159752 | tf_op jit(solution)/shard_map/ppermute | solution.py:398
  100.7 31.7 %all-to-all-start.2 = ((bf16[4,656,384]{2,1,0:T(8,128)(2,1)}), bf16[4,656,384]{2,1,0:T(8,128)(2,1)S(1)}, u32[]{:S(2)}, u32[]{:S(2)}) async-start(bf16[4,656,384]{2,1,0:T(8,128)(2,1)} %shard_map.110), calls=%async_computation.2 | async-start | bytes 4030464 | tf_op jit(solution)/shard_map/all_to_all | solution.py:407
  105.0 27.4 %copy-start.2 = (bf16[384,320]{0,1:T(8,128)(2,1)S(1)}, bf16[384,320]{0,1:T(8,128)(2,1)}, u32[]{:S(2)}) copy-start(bf16[384,320]{0,1:T(8,128)(2,1)} %param.6) | copy-start | bytes 737284
  105.0 5.6 %collective-permute-start.6 = (bf16[2,16,1664]{2,1,0:T(8,128)(2,1)S(1)}, bf16[2,16,1664]{2,1,0:T(8,128)(2,1)S(1)}, u32[]{:S(2)}, u32[]{:S(2)}) collective-permute-start(bf16[2,16,1664]{2,1,0:T(8,128)(2,1)S(1)} %shard_map.113.own_ref), channel_id=1, source_target_pairs={{0,32},{32,0},{64,96},{96,64},{1,33},{33,1},{65,97},{97,65},{2,34}... | collective-permute-start | bytes 319496 | tf_op jit(solution)/shard_map/ppermute | solution.py:409
  122.9 17.9 %copy-start.5 = (s32[128]{0:T(128)S(1)}, s32[128]{0:T(128)}, u32[]{:S(2)}) copy-start(s32[128]{0:T(128)} %param.11) | copy-start | bytes 1540
  122.9 12.3 %collective-permute-start.7 = (bf16[4,16,6400]{2,1,0:T(8,128)(2,1)S(1)}, bf16[4,16,6400]{2,1,0:T(8,128)(2,1)}, u32[]{:S(2)}, u32[]{:S(2)}) collective-permute-start(bf16[4,16,6400]{2,1,0:T(8,128)(2,1)S(1)} %bitcast.9), channel_id=1, source_target_pairs={{0,4},{4,0},{1,5},{5,1},{2,6},{6,2},{3,7},{7,3},{8,12},{12,8},{9,1... | collective-permute-start | bytes 2457608 | tf_op jit(solution)/shard_map/ppermute | solution.py:412
  133.3 7.5 %collective-permute-start.4 = (bf16[320,320]{1,0:T(8,128)(2,1)S(1)}, bf16[320,320]{1,0:T(8,128)(2,1)S(1)}, u32[]{:S(2)}, u32[]{:S(2)}) collective-permute-start(bf16[320,320]{1,0:T(8,128)(2,1)S(1)} %get-tuple-element.27), channel_id=1, source_target_pairs={{4,0},{8,4},{12,8},{16,12},{20,16},{24,20},{28,24},{32,28},{36,32}... | collective-permute-start | bytes 614408 | tf_op jit(solution)/shard_map/ppermute | solution.py:434

commit v4 on v3

--- a/solution.py
+++ b/solution.py
@@ -71,29 +71,23 @@
     return lax.dot_general(a, b, ((dims[:1], dims[1:]), ((), ())), preferred_element_type=F32)
 
 
-def enter(counts_hbm, cot_hbm, send_ref, counts, cot, sems):
-    copies = [
-        pltpu.make_async_copy(counts_hbm, counts, sems.at[0]),
-        pltpu.make_async_copy(cot_hbm, cot, sems.at[1]),
-    ]
+def route_in(counts_hbm, gain_hbm, cot_hbm, got_hbm, out_ref, counts_ref, gain_ref, cot_ref, got_ref, sems):
+    pairs_in = ((counts_hbm, counts_ref), (gain_hbm, gain_ref), (cot_hbm.at[:, pl.ds(0, ROWS)], cot_ref), (got_hbm, got_ref))
+    copies = [pltpu.make_async_copy(a, b, sems.at[n]) for n, (a, b) in enumerate(pairs_in)]
     for copy in copies:
         copy.start()
     for copy in copies:
         copy.wait()
-    drift = drift_of(counts[...], lax.axis_index(DP))
-    pick = one_hot(SLOTS, PASS, (W_DEV - drift) * WIN)
-    send_ref[...] = dot(cot[...], pick, (1, 0)).astype(BF16)
-
-
-def route_in(counts_ref, gain_ref, cot_ref, got_ref, out_ref):
-    drift = drift_of(counts_ref[...], lax.axis_index(DP)) * WIN
-    own = dot(cot_ref[:, :ROWS], one_hot(ROWS, ROWS, -drift), (1, 0))
-    col = lax.broadcasted_iota(jnp.int32, (PASS, ROWS), 1)
-    row = lax.broadcasted_iota(jnp.int32, (PASS, ROWS), 0)
-    near = jnp.where((row == col) & (col < drift), 1.0, 0.0).astype(BF16)
+    rank = lax.axis_index(DP)
+    drift = drift_of(counts_ref[...], rank) * WIN
+    drift_before = drift_of(counts_ref[...], rank - 1) * WIN
+    own = dot(cot_ref[...], one_hot(ROWS, ROWS, -drift), (1, 0))
+    col = lax.broadcasted_iota(jnp.int32, (SLOTS, ROWS), 1)
+    row = lax.broadcasted_iota(jnp.int32, (SLOTS, ROWS), 0)
+    near = jnp.where((row == col + (W_DEV * WIN - drift_before)) & (col < drift), 1.0, 0.0).astype(BF16)
     out_ref[:FX, :] = (own + dot(got_ref[...], near, (1, 0))).astype(BF16)
     out_ref[FX:, :] = jnp.zeros((GROWS - FX, ROWS), BF16)
-    out_ref[FX:, :FX] = jnp.broadcast_to(gain_ref[...], (GROWS - FX, FX))
+    out_ref[FX:, :FX] = jnp.broadcast_to(gain_ref[...].reshape(1, FX), (GROWS - FX, FX))
 
 
 def x_rows(x_ref, i):
@@ -104,7 +98,7 @@
     return [(3 * h + p, h, slice(128 * p, 128 * (p + 1)), 3 * HD * h) for h in range(HEADS) for p in range(3)]
 
 
-def block(x_ref, g_ref, wq_ref, wo_ref, send_ref, keep_ref, gp_ref, mx_ref, gcol_ref, rms_ref, gt, nrm, pk, gm, dsum):
+def block(x_ref, g_ref, wq_ref, wo_ref, send_ref, dsum, tile_ref, gp_ref, mx_ref, gcol_ref, rms_ref, gt, nrm, pk, gm):
     core = lax.axis_index("c")
     r_i = lax.broadcasted_iota(jnp.int32, (FX, ROWS), 0)
     c_i = lax.broadcasted_iota(jnp.int32, (FX, ROWS), 1)
@@ -147,7 +141,6 @@
     dsum[QKV:, :] = dot(mx_ref[...], gt[...], (1, 1))
     for i in range(20):
         c = slice(FEAT * i, FEAT * (i + 1))
-        keep_ref[:, c] = dsum[pl.ds(pl.multiple_of(core * 320 + 16 * i, 16), 16), :]
         send_ref[:, c] = dsum[pl.ds(pl.multiple_of((1 - core) * 320 + 16 * i, 16), 16), :].astype(BF16)
     total = jnp.zeros((8, FEAT), F32)
     for i in range(30):
@@ -160,7 +153,7 @@
         tile = jnp.where(tile_row == i, line[:, TILE * i:TILE * (i + 1)], tile)
     tile = tile.astype(BF16)
     send_ref[:, HALF:] = tile
-    keep_ref[:, HALF:] = tile.astype(F32)
+    tile_ref[...] = tile.astype(F32)
 
 
 def head_shares(gp_ref, mx_ref, x_ref, wq_ref, wo_ref, gcol_ref, rms_ref, heads_ref, part, out, sems):
@@ -188,11 +181,15 @@
         copy.wait()
 
 
-def core_sum(keep_ref, got_ref, out_ref):
-    gain = (keep_ref[:, HALF:] + got_ref[:, HALF:].astype(F32)).astype(BF16)
+def core_sum(dsum_ref, tile_ref, got_ref, out_ref):
+    core = lax.axis_index("c")
+    gain = (tile_ref[...] + got_ref[:, HALF:].astype(F32)).astype(BF16)
+    for i in range(20):
+        b, o = divmod(i, 5)
+        own = dsum_ref[pl.ds(pl.multiple_of(core * 320 + 16 * i, 16), 16), :]
+        got = got_ref[:, FEAT * i:FEAT * (i + 1)].astype(F32)
+        out_ref[b, :, FEAT * o:FEAT * (o + 1)] = (own + got).astype(BF16)
     for b in range(4):
-        s = slice(Y_LANES * b, Y_LANES * (b + 1))
-        out_ref[b, :, :Y_LANES] = (keep_ref[:, s] + got_ref[:, s].astype(F32)).astype(BF16)
         out_ref[b, :, Y_LANES:] = gain
 
 
@@ -339,22 +336,29 @@
     down = [(i + 1, i) for i in range(127)]
     cores = [(0, 1), (1, 0)]
 
-    send = call(
-        enter,
-        struct((FX, PASS), BF16),
-        ins=(HBM, HBM),
-        scratch=(pltpu.VMEM((1, 128), jnp.int32), pltpu.VMEM((FX, SLOTS), BF16), pltpu.SemaphoreType.DMA((2,))),
-    )(counts, cot)
-    got = lax.ppermute(send, DP, up)
+    got = lax.ppermute(cot, DP, up)
     x_full = lax.all_gather(xt, "x", axis=0, tiled=True)
-    cot_work = call(route_in, struct((GROWS, ROWS), BF16))(counts, gain, cot, got)
+    cot_work = call(
+        route_in,
+        struct((GROWS, ROWS), BF16),
+        ins=(HBM, HBM, HBM, HBM),
+        scratch=(
+            pltpu.VMEM((1, 128), jnp.int32),
+            pltpu.VMEM((FX,), BF16),
+            pltpu.VMEM((FX, ROWS), BF16),
+            pltpu.VMEM((FX, SLOTS), BF16),
+            pltpu.SemaphoreType.DMA((4,)),
+        ),
+        vmem_mib=61,
+    )(counts, norm_gain, cot, got)
     g_full = lax.all_gather(cot_work, "x", axis=0)
 
-    send, keep, gp, mx, gcol, rms = call(
+    send, dsum, tile, gp, mx, gcol, rms = call(
         block,
         (
             struct((16, HALF + TILE), BF16),
-            struct((16, HALF + TILE), F32),
+            struct((QKV + ATT, FEAT), F32),
+            struct((16, TILE), F32),
             struct((QKV, ROWS), BF16),
             struct((ATT, ROWS), BF16),
             struct((FEAT, 1), F32),
@@ -365,7 +369,6 @@
             pltpu.VMEM((FEAT, ROWS), BF16),
             pltpu.VMEM((QKV, ROWS), BF16),
             pltpu.VMEM((ATT, ROWS), BF16),
-            pltpu.VMEM((QKV + ATT, FEAT), F32),
         ),
         vmem_mib=40,
         flops=1500000000,
@@ -386,7 +389,7 @@
         flops=700000000,
     )(gp, mx, x_full, wq, w_out, gcol, rms)
 
-    parts = call(core_sum, struct((4, 16, Y_LANES + TILE), BF16))(keep, got)
+    parts = call(core_sum, struct((4, 16, Y_LANES + TILE), BF16))(dsum, tile, got)
     parts = lax.all_to_all(parts, "y", 0, 0)
     parts = call(y_sum, struct((4, 16, Z_LANES + TILE), BF16))(parts)
     parts = lax.all_to_all(parts, "zl", 0, 0)

time: 143 us -> 142 us (level)
  local copies, waits for them, and re-layouts: 2.38 us -> 0.03 us
    unnamed x12, local copies, waits for them, and re-layouts: 1.69 us -> 0.03 us
    pallas_call x4 -> x3, Pallas kernels: 5.58 us -> 6.61 us  [the longest x1 3.86 us: shards(): call(block, (struct((16, HALF + TILE), BF16), struct((QKV + ATT, FEAT), F...]
where the time goes in v4:
time: 142 us; the launch traced here: 141 us
  blocking collectives  60.3 us (42%)
  starting transfers between devices  54 us (38%)
  Pallas kernels  15.6 us (11%)
  waiting for transfers between devices  10.5 us (7%)
    all_to_all x1, blocking collectives, shards(): parts = lax.all_to_all(parts, 'y', 0, 0)  14.7 us
    all_gather x1, blocking collectives, shards(): x_full = lax.all_gather(xt, 'x', axis=0, tiled=True)  13.2 us
    all_gather x1, blocking collectives, shards(): own = lax.all_gather(part, 'y', axis=0)  12.3 us
    all_gather x1, blocking collectives, shards(): g_full = lax.all_gather(cot_work, 'x', axis=0)  11.7 us
    ppermute x1, starting transfers between devices, shards(): got = lax.ppermute(send, 'c', cores)  10.4 us
    ppermute x1, starting transfers between devices, shards(): other = lax.ppermute(own, 'c', cores)  9.37 us
    ppermute x1, starting transfers between devices, shards(): got = lax.ppermute(part, 'zh', [(0, 1), (1, 0), (2, 3), (3, 2)])  8.79 us
    all_to_all x1, blocking collectives, shards(): parts = lax.all_to_all(parts, 'zl', 0, 0)  8.38 us
  transfers between devices with their start and end apart: 9, of which 4 were waited for; matrix products, arithmetic and copies ran while one was open for 0% of the time, Pallas kernels for 5%

profile of v4, /device:TPU:1, one launch (start us, length us, event | category | flops | bytes accessed | tf_op | source)
XLA Modules:
  0.0 141.3 jit_solution(407802818214165468)
XLA Ops:
  0.6 0.0 copy-start.1
  0.6 0.0 copy-start.3
  0.7 4.7 %collective-permute-start = (bf16[320,704]{1,0:T(8,128)(2,1)}, bf16[320,704]{1,0:T(8,128)(2,1)}, u32[]{:S(2)}, u32[]{:S(2)}) collective-permute-start(bf16[320,704]{1,0:T(8,128)(2,1)} %bitcast.19), channel_id=1, source_target_pairs={{0,4},{4,8},{8,12},{12,16},{16,20},{20,24},{24,28},{28,32},{32,36}... | collective-permute-start | bytes 1351688 | tf_op jit(solution)/shard_map/ppermute | solution.py:339
  5.4 13.2 %all_gather.15.x_ref = bf16[1280,384]{1,0:T(8,128)(2,1)S(1)} all-gather(bf16[320,384]{1,0:T(8,128)(2,1)} %bitcast.14), channel_id=1, replica_groups=mesh['zh'=4,'zl'=4,'y'=4,'c'=2,'x'=4] {'x'}, dimensions={0}, use_global_device_ids=true | all-gather | bytes 1228800 | tf_op jit(solution)/shard_map/all_gather | solution.py:340
  18.6 0.0 collective-permute-done.got_hbm
  18.6 2.6 %shard_map.101.cot_ref = bf16[336,384]{1,0:T(8,128)(2,1)} custom-call(s32[1,128]{1,0:T(1,128)} %bitcast.16, bf16[320]{0:T(512)(128)(2,1)} %gain_hbm.1, bf16[320,704]{1,0:T(8,128)(2,1)} %bitcast.20, bf16[320,704]{1,0:T(8,128)(2,1)} %collective-permute-done.got_hbm), custom_call_target="tpu_custom_call" | custom-call | flops 1000000 | bytes 1000000 | tf_op jit(solution)/shard_map/pallas_call | solution.py:341
  21.3 11.7 %all-gather = bf16[1344,384]{1,0:T(8,128)(2,1)S(1)} all-gather(bf16[336,384]{1,0:T(8,128)(2,1)} %shard_map.101.cot_ref), channel_id=2, replica_groups=mesh['zh'=4,'zl'=4,'y'=4,'c'=2,'x'=4] {'x'}, dimensions={0}, use_global_device_ids=true | all-gather | bytes 1290240 | tf_op jit(solution)/shard_map/all_gather | solution.py:354
  33.0 0.0 copy-done.1
  33.0 0.0 copy-done.3
  33.0 3.9 %shard_map.102 = (bf16[16,25728]{1,0:T(8,128)(2,1)S(1)}, f32[640,1280]{1,0:T(8,128)S(1)}, f32[16,128]{1,0:T(8,128)S(1)}, bf16[480,384]{1,0:T(8,128)(2,1)S(1)}, b...) custom-call(bf16[1280,384]{1,0:T(8,128)(2,1)S(1)} %all_gather.15.x_ref, ...), custom_call_target="tpu_custom_call" | custom-call | flops 1500000000 | bytes 1000000 | tf_op jit(solution)/shard_map/pallas_call | solution.py:356
  36.8 10.4 %collective-permute-start.1 = (bf16[16,25728]{1,0:T(8,128)(2,1)S(1)}, bf16[16,25728]{1,0:T(8,128)(2,1)S(1)}, u32[]{:S(2)}, u32[]{:S(2)}) collective-permute-start(bf16[16,25728]{1,0:T(8,128)(2,1)S(1)} %get-tuple-element.22), channel_id=1, source_target_pairs={{0,4},{4,0},{1,5},{5,1},{2,6},{6,2},{3,7},{7,3},{8,12},{12,8},{9,1... | collective-permute-start | bytes 2469896 | tf_op jit(solution)/shard_map/ppermute | solution.py:377
  47.3 1.9 %collective-permute-done.1.got_ref = bf16[16,25728]{1,0:T(8,128)(2,1)S(1)} collective-permute-done((bf16[16,25728]{1,0:T(8,128)(2,1)S(1)}, bf16[16,25728]{1,0:T(8,128)(2,1)S(1)}, u32[]{:S(2)}, u32[]{:S(2)}) %collective-permute-start.1) | collective-permute-done | bytes 823328 | tf_op jit(solution)/shard_map/ppermute | solution.py:377
  49.2 0.1 shard_map.103
  49.4 14.7 %all_to_all.15.got_ref = bf16[4,16,6528]{2,1,0:T(8,128)(2,1)S(1)} all-to-all(bf16[4,16,6528]{2,1,0:T(8,128)(2,1)S(1)} %shard_map.103), channel_id=1, replica_groups=mesh['zh'=4,'zl'=4,'y'=4,'c'=2,'x'=4] {'y'}, dimensions={0} | all-to-all | bytes 1671168 | tf_op jit(solution)/shard_map/all_to_all | solution.py:393
  64.0 0.1 shard_map.104
  64.2 8.4 %all_to_all.16.got_ref = bf16[4,16,1792]{2,1,0:T(8,128)(2,1)S(1)} all-to-all(bf16[4,16,1792]{2,1,0:T(8,128)(2,1)S(1)} %shard_map.104), channel_id=1, replica_groups=mesh['zh'=4,'zl'=4,'y'=4,'c'=2,'x'=4] {'zl'}, dimensions={0} | all-to-all | bytes 458752 | tf_op jit(solution)/shard_map/all_to_all | solution.py:395
  72.6 8.8 %collective-permute-start.2 = (bf16[16,1792]{1,0:T(8,128)(2,1)S(1)}, bf16[16,1792]{1,0:T(8,128)(2,1)S(1)}, u32[]{:S(2)}, u32[]{:S(2)}) collective-permute-start(bf16[16,1792]{1,0:T(8,128)(2,1)S(1)} %shard_map.105.own_ref), channel_id=1, source_target_pairs={{0,128},{128,0},{256,384},{384,256},{1,129},{129,1},{257,385},{385... | collective-permute-start | bytes 172040 | tf_op jit(solution)/shard_map/ppermute | solution.py:397
  81.4 3.0 %shard_map.106.heads_ref.heads_in = bf16[4,656,384]{2,1,0:T(8,128)(2,1)} custom-call(bf16[480,384]{1,0:T(8,128)(2,1)S(1)} %get-tuple-element.23.gp_ref, bf16[160,384]{1,0:T(8,128)(2,1)S(1)} %get-tuple-element.24.mx_ref, bf16[1280,384]{1,0:T(8,128)(2,1)S(1)} %all_gather.15.x_ref, bf16[480,1280]{1,0:T(8,128)(2,1)S(1)} %bitcast.12, ...), custom_call_target="tpu_custom_call" | custom-call | flops 700000000 | bytes 1000000 | tf_op jit(solution)/shard_map/pallas_call | solution.py:379
  84.3 0.0 collective-permute-done.2.got_ref
  84.4 6.7 %collective-permute-start.3 = (bf16[16,1792]{1,0:T(8,128)(2,1)S(1)}, bf16[16,1792]{1,0:T(8,128)(2,1)S(1)}, u32[]{:S(2)}, u32[]{:S(2)}) collective-permute-start(bf16[16,1792]{1,0:T(8,128)(2,1)S(1)} %shard_map.107.own_ref), channel_id=1, source_target_pairs={{128,256},{256,128},{384,0},{0,384},{129,257},{257,129},{385,1},{1... | collective-permute-start | bytes 172040 | tf_op jit(solution)/shard_map/ppermute | solution.py:399
  91.0 2.2 %collective-permute-done.3.got_ref = bf16[16,1792]{1,0:T(8,128)(2,1)S(1)} collective-permute-done((bf16[16,1792]{1,0:T(8,128)(2,1)S(1)}, bf16[16,1792]{1,0:T(8,128)(2,1)S(1)}, u32[]{:S(2)}, u32[]{:S(2)}) %collective-permute-start.3) | collective-permute-done | bytes 57376 | tf_op jit(solution)/shard_map/ppermute | solution.py:399
  93.3 5.7 %collective-permute-start.5 = (bf16[16,1664]{1,0:T(8,128)(2,1)S(1)}, bf16[16,1664]{1,0:T(8,128)(2,1)S(1)}, u32[]{:S(2)}, u32[]{:S(2)}) collective-permute-start(bf16[16,1664]{1,0:T(8,128)(2,1)S(1)} %get-tuple-element.31.own_ref), channel_id=1, source_target_pairs={{0,96},{96,0},{32,64},{64,32},{1,97},{97,1},{33,65},{65,33},{2,98}... | collective-permute-start | bytes 159752 | tf_op jit(solution)/shard_map/ppermute | solution.py:401
  99.0 0.7 shard_map.109
  99.8 4.3 %all-to-all-start.2 = ((bf16[4,656,384]{2,1,0:T(8,128)(2,1)}), bf16[4,656,384]{2,1,0:T(8,128)(2,1)S(1)}, u32[]{:S(2)}, u32[]{:S(2)}) async-start(bf16[4,656,384]{2,1,0:T(8,128)(2,1)} %shard_map.109), calls=%async_computation.2 | async-start | bytes 4030464 | tf_op jit(solution)/shard_map/all_to_all | solution.py:410
  104.1 0.0 copy-start.5
  104.1 0.0 copy-start
  104.1 0.0 copy-start.2
  104.1 0.0 collective-permute-done.5.got_ref
  104.1 2.1 %collective-permute-start.6 = (bf16[2,16,1664]{2,1,0:T(8,128)(2,1)S(1)}, bf16[2,16,1664]{2,1,0:T(8,128)(2,1)S(1)}, u32[]{:S(2)}, u32[]{:S(2)}) collective-permute-start(bf16[2,16,1664]{2,1,0:T(8,128)(2,1)S(1)} %shard_map.112.own_ref), channel_id=1, source_target_pairs={{0,32},{32,0},{64,96},{96,64},{1,33},{33,1},{65,97},{97,65},{2,34}... | collective-permute-start | bytes 319496 | tf_op jit(solution)/shard_map/ppermute | solution.py:412
  106.2 3.5 %collective-permute-done.6.got_ref = bf16[2,16,1664]{2,1,0:T(8,128)(2,1)S(1)} collective-permute-done((bf16[2,16,1664]{2,1,0:T(8,128)(2,1)S(1)}, bf16[2,16,1664]{2,1,0:T(8,128)(2,1)S(1)}, u32[]{:S(2)}, u32[]{:S(2)}) %collective-permute-start.6) | collective-permute-done | bytes 106528 | tf_op jit(solution)/shard_map/ppermute | solution.py:412
  109.7 12.3 %all-gather.1 = bf16[64,6400]{1,0:T(8,128)(2,1)S(1)} all-gather(bf16[16,6400]{1,0:T(8,128)(2,1)S(1)} %shard_map.113), channel_id=3, replica_groups=mesh['zh'=4,'zl'=4,'y'=4,'c'=2,'x'=4] {'y'}, dimensions={0}, use_global_device_ids=true | all-gather | bytes 1024000 | tf_op jit(solution)/shard_map/all_gather | solution.py:414
  122.0 9.4 %collective-permute-start.7 = (bf16[4,16,6400]{2,1,0:T(8,128)(2,1)S(1)}, bf16[4,16,6400]{2,1,0:T(8,128)(2,1)}, u32[]{:S(2)}, u32[]{:S(2)}) collective-permute-start(bf16[4,16,6400]{2,1,0:T(8,128)(2,1)S(1)} %bitcast.9), channel_id=1, source_target_pairs={{0,4},{4,0},{1,5},{5,1},{2,6},{6,2},{3,7},{7,3},{8,12},{12,8},{9,1... | collective-permute-start | bytes 2457608 | tf_op jit(solution)/shard_map/ppermute | solution.py:415
  131.4 0.0 copy-done.5
  131.4 0.0 copy-start.4
  131.4 0.0 all-to-all-done.2.got_ref
  131.4 0.0 copy-done
  131.4 0.0 copy-done.2
  131.4 0.9 shard_map.110
  132.3 1.9 %collective-permute-start.4 = (bf16[320,320]{1,0:T(8,128)(2,1)S(1)}, bf16[320,320]{1,0:T(8,128)(2,1)S(1)}, u32[]{:S(2)}, u32[]{:S(2)}) collective-permute-start(bf16[320,320]{1,0:T(8,128)(2,1)S(1)} %get-tuple-element.29), channel_id=1, source_target_pairs={{4,0},{8,4},{12,8},{16,12},{20,16},{24,20},{28,24},{32,28},{36,32}... | collective-permute-start | bytes 614408 | tf_op jit(solution)/shard_map/ppermute | solution.py:437
  134.2 0.0 collective-permute-done.7.other_any
  134.2 2.7 %shard_map.114 = (f32[480,1280]{1,0:T(8,128)}, f32[160,1280]{1,0:T(8,128)}) custom-call(bf16[4,16,6400]{2,1,0:T(8,128)(2,1)S(1)} %bitcast.10, bf16[4,16,6400]{2,1,0:T(8,128)(2,1)} %collective-permute-done.7.other_any), custom_call_target="tpu_custom_call" | custom-call | flops 1000000 | bytes 1000000 | tf_op jit(solution)/shard_map/pallas_call | solution.py:416
  137.0 2.8 %collective-permute-done.4.got_ref = bf16[320,320]{1,0:T(8,128)(2,1)S(1)} collective-permute-done((bf16[320,320]{1,0:T(8,128)(2,1)S(1)}, bf16[320,320]{1,0:T(8,128)(2,1)S(1)}, u32[]{:S(2)}, u32[]{:S(2)}) %collective-permute-start.4) | collective-permute-done | bytes 204832 | tf_op jit(solution)/shard_map/ppermute | solution.py:437
  139.8 0.0 copy-done.4
  139.8 1.5 %shard_map.111 = bf16[320,704]{1,0:T(8,128)(2,1)} custom-call(s32[1,128]{1,0:T(1,128)S(1)} %bitcast.17, bf16[320,384]{1,0:T(8,128)(2,1)S(1)} %get-tuple-element.28.y_ref, bf16[320,320]{1,0:T(8,128)(2,1)S(1)} %collective-permute-done.4.got_ref), custom_call_target="tpu_custom_call" | custom-call | flops 1000000 | bytes 1000000 | tf_op jit(solution)/shard_map/pallas_call | solution.py:438
  (6 shorter events, 0.1 us)
Async XLA Ops:
  0.6 32.3 %copy-start.1 = (bf16[1280,480]{0,1:T(8,128)(2,1)S(1)}, bf16[1280,480]{0,1:T(8,128)(2,1)}, u32[]{:S(2)}) copy-start(bf16[1280,480]{0,1:T(8,128)(2,1)} %param.8) | copy-start | bytes 3686404
  0.6 32.3 %copy-start.3 = (bf16[160,1280]{1,0:T(8,128)(2,1)S(1)}, bf16[160,1280]{1,0:T(8,128)(2,1)}, u32[]{:S(2)}) copy-start(bf16[160,1280]{1,0:T(8,128)(2,1)} %wo_ref.3) | copy-start | bytes 1228804
  0.7 18.0 %collective-permute-start = (bf16[320,704]{1,0:T(8,128)(2,1)}, bf16[320,704]{1,0:T(8,128)(2,1)}, u32[]{:S(2)}, u32[]{:S(2)}) collective-permute-start(bf16[320,704]{1,0:T(8,128)(2,1)} %bitcast.19), channel_id=1, source_target_pairs={{0,4},{4,8},{8,12},{12,16},{16,20},{20,24},{24,28},{28,32},{32,36}... | collective-permute-start | bytes 1351688 | tf_op jit(solution)/shard_map/ppermute | solution.py:339
  36.8 12.4 %collective-permute-start.1 = (bf16[16,25728]{1,0:T(8,128)(2,1)S(1)}, bf16[16,25728]{1,0:T(8,128)(2,1)S(1)}, u32[]{:S(2)}, u32[]{:S(2)}) collective-permute-start(bf16[16,25728]{1,0:T(8,128)(2,1)S(1)} %get-tuple-element.22), channel_id=1, source_target_pairs={{0,4},{4,0},{1,5},{5,1},{2,6},{6,2},{3,7},{7,3},{8,12},{12,8},{9,1... | collective-permute-start | bytes 2469896 | tf_op jit(solution)/shard_map/ppermute | solution.py:377
  72.6 11.8 %collective-permute-start.2 = (bf16[16,1792]{1,0:T(8,128)(2,1)S(1)}, bf16[16,1792]{1,0:T(8,128)(2,1)S(1)}, u32[]{:S(2)}, u32[]{:S(2)}) collective-permute-start(bf16[16,1792]{1,0:T(8,128)(2,1)S(1)} %shard_map.105.own_ref), channel_id=1, source_target_pairs={{0,128},{128,0},{256,384},{384,256},{1,129},{129,1},{257,385},{385... | collective-permute-start | bytes 172040 | tf_op jit(solution)/shard_map/ppermute | solution.py:397
  84.4 8.9 %collective-permute-start.3 = (bf16[16,1792]{1,0:T(8,128)(2,1)S(1)}, bf16[16,1792]{1,0:T(8,128)(2,1)S(1)}, u32[]{:S(2)}, u32[]{:S(2)}) collective-permute-start(bf16[16,1792]{1,0:T(8,128)(2,1)S(1)} %shard_map.107.own_ref), channel_id=1, source_target_pairs={{128,256},{256,128},{384,0},{0,384},{129,257},{257,129},{385,1},{1... | collective-permute-start | bytes 172040 | tf_op jit(solution)/shard_map/ppermute | solution.py:399
  93.3 10.8 %collective-permute-start.5 = (bf16[16,1664]{1,0:T(8,128)(2,1)S(1)}, bf16[16,1664]{1,0:T(8,128)(2,1)S(1)}, u32[]{:S(2)}, u32[]{:S(2)}) collective-permute-start(bf16[16,1664]{1,0:T(8,128)(2,1)S(1)} %get-tuple-element.31.own_ref), channel_id=1, source_target_pairs={{0,96},{96,0},{32,64},{64,32},{1,97},{97,1},{33,65},{65,33},{2,98}... | collective-permute-start | bytes 159752 | tf_op jit(solution)/shard_map/ppermute | solution.py:401
  99.8 31.6 %all-to-all-start.2 = ((bf16[4,656,384]{2,1,0:T(8,128)(2,1)}), bf16[4,656,384]{2,1,0:T(8,128)(2,1)S(1)}, u32[]{:S(2)}, u32[]{:S(2)}) async-start(bf16[4,656,384]{2,1,0:T(8,128)(2,1)} %shard_map.109), calls=%async_computation.2 | async-start | bytes 4030464 | tf_op jit(solution)/shard_map/all_to_all | solution.py:410
  104.1 27.3 %copy-start.5 = (bf16[320]{0:T(512)(128)(2,1)S(1)}, bf16[320]{0:T(512)(128)(2,1)}, u32[]{:S(2)}) copy-start(bf16[320]{0:T(512)(128)(2,1)} %gain_hbm.1) | copy-start | bytes 1924
  104.1 27.3 %copy-start = (bf16[336,384]{1,0:T(8,128)(2,1)S(1)}, bf16[336,384]{1,0:T(8,128)(2,1)}, u32[]{:S(2)}) copy-start(bf16[336,384]{1,0:T(8,128)(2,1)} %shard_map.101.cot_ref) | copy-start | bytes 774148
  104.1 27.3 %copy-start.2 = (bf16[384,320]{0,1:T(8,128)(2,1)S(1)}, bf16[384,320]{0,1:T(8,128)(2,1)}, u32[]{:S(2)}) copy-start(bf16[384,320]{0,1:T(8,128)(2,1)} %param.6) | copy-start | bytes 737284
  104.1 5.6 %collective-permute-start.6 = (bf16[2,16,1664]{2,1,0:T(8,128)(2,1)S(1)}, bf16[2,16,1664]{2,1,0:T(8,128)(2,1)S(1)}, u32[]{:S(2)}, u32[]{:S(2)}) collective-permute-start(bf16[2,16,1664]{2,1,0:T(8,128)(2,1)S(1)} %shard_map.112.own_ref), channel_id=1, source_target_pairs={{0,32},{32,0},{64,96},{96,64},{1,33},{33,1},{65,97},{97,65},{2,34}... | collective-permute-start | bytes 319496 | tf_op jit(solution)/shard_map/ppermute | solution.py:412
  122.0 12.2 %collective-permute-start.7 = (bf16[4,16,6400]{2,1,0:T(8,128)(2,1)S(1)}, bf16[4,16,6400]{2,1,0:T(8,128)(2,1)}, u32[]{:S(2)}, u32[]{:S(2)}) collective-permute-start(bf16[4,16,6400]{2,1,0:T(8,128)(2,1)S(1)} %bitcast.9), channel_id=1, source_target_pairs={{0,4},{4,0},{1,5},{5,1},{2,6},{6,2},{3,7},{7,3},{8,12},{12,8},{9,1... | collective-permute-start | bytes 2457608 | tf_op jit(solution)/shard_map/ppermute | solution.py:415
  131.4 8.4 %copy-start.4 = (s32[128]{0:T(128)S(1)}, s32[128]{0:T(128)}, u32[]{:S(2)}) copy-start(s32[128]{0:T(128)} %param.11) | copy-start | bytes 1540
  132.3 7.5 %collective-permute-start.4 = (bf16[320,320]{1,0:T(8,128)(2,1)S(1)}, bf16[320,320]{1,0:T(8,128)(2,1)S(1)}, u32[]{:S(2)}, u32[]{:S(2)}) collective-permute-start(bf16[320,320]{1,0:T(8,128)(2,1)S(1)} %get-tuple-element.29), channel_id=1, source_target_pairs={{4,0},{8,4},{12,8},{16,12},{20,16},{24,20},{28,24},{32,28},{36,32}... | collective-permute-start | bytes 614408 | tf_op jit(solution)/shard_map/ppermute | solution.py:437

commit v5 on v4

--- a/solution.py
+++ b/solution.py
@@ -71,23 +71,34 @@
     return lax.dot_general(a, b, ((dims[:1], dims[1:]), ((), ())), preferred_element_type=F32)
 
 
-def route_in(counts_hbm, gain_hbm, cot_hbm, got_hbm, out_ref, counts_ref, gain_ref, cot_ref, got_ref, sems):
-    pairs_in = ((counts_hbm, counts_ref), (gain_hbm, gain_ref), (cot_hbm.at[:, pl.ds(0, ROWS)], cot_ref), (got_hbm, got_ref))
-    copies = [pltpu.make_async_copy(a, b, sems.at[n]) for n, (a, b) in enumerate(pairs_in)]
-    for copy in copies:
-        copy.start()
-    for copy in copies:
-        copy.wait()
+def route_in(counts_hbm, gain_hbm, cot_hbm, got_hbm, out_hbm, counts, gain, cot, got, out, sems):
+    loads = ((counts_hbm, counts), (gain_hbm, gain), (cot_hbm.at[:, pl.ds(0, ROWS)], cot), (got_hbm, got))
+    loads = [pltpu.make_async_copy(a, b, sems.at[n]) for n, (a, b) in enumerate(loads)]
+    for load in loads:
+        load.start()
+    loads[0].wait()
     rank = lax.axis_index(DP)
-    drift = drift_of(counts_ref[...], rank) * WIN
-    drift_before = drift_of(counts_ref[...], rank - 1) * WIN
-    own = dot(cot_ref[...], one_hot(ROWS, ROWS, -drift), (1, 0))
+    drift = drift_of(counts[...], rank) * WIN
+    drift_before = drift_of(counts[...], rank - 1) * WIN
+    own = one_hot(ROWS, ROWS, -drift)
     col = lax.broadcasted_iota(jnp.int32, (SLOTS, ROWS), 1)
     row = lax.broadcasted_iota(jnp.int32, (SLOTS, ROWS), 0)
     near = jnp.where((row == col + (W_DEV * WIN - drift_before)) & (col < drift), 1.0, 0.0).astype(BF16)
-    out_ref[:FX, :] = (own + dot(got_ref[...], near, (1, 0))).astype(BF16)
-    out_ref[FX:, :] = jnp.zeros((GROWS - FX, ROWS), BF16)
-    out_ref[FX:, :FX] = jnp.broadcast_to(gain_ref[...].reshape(1, FX), (GROWS - FX, FX))
+    loads[1].wait()
+    out[FX:, :] = jnp.zeros((GROWS - FX, ROWS), BF16)
+    out[FX:, :FX] = jnp.broadcast_to(gain[...].reshape(1, FX), (GROWS - FX, FX))
+    loads[2].wait()
+    loads[3].wait()
+    stores = []
+    for n, (lo, hi) in enumerate(((0, 160), (160, FX))):
+        block_rows = dot(cot[lo:hi, :], own, (1, 0)) + dot(got[lo:hi, :], near, (1, 0))
+        out[lo:hi, :] = block_rows.astype(BF16)
+        end = hi if n == 0 else GROWS
+        rows = pl.ds(lo, end - lo)
+        stores.append(pltpu.make_async_copy(out.at[rows], out_hbm.at[rows], sems.at[4 + n]))
+        stores[n].start()
+    for store in stores:
+        store.wait()
 
 
 def x_rows(x_ref, i):
@@ -313,7 +324,7 @@
     gain_grad_ref[...] = (line[:, :FX] / gain_ref[...].astype(F32)).reshape(FX)
 
 
-def route_out(counts_ref, y_ref, got_ref, out_ref):
+def route_own(counts_ref, y_ref, out_ref, far_ref):
     rank = lax.axis_index(DP)
     counts = counts_ref[...]
     owners = lax.broadcasted_iota(jnp.int32, counts.shape, 1)
@@ -323,9 +334,13 @@
     r = lax.broadcasted_iota(jnp.int32, (ROWS, SLOTS), 0)
     c = lax.broadcasted_iota(jnp.int32, (ROWS, SLOTS), 1)
     own = jnp.where((r == c + drift) & (c < live), 1.0, 0.0).astype(BF16)
+    out_ref[...] = dot(y_ref[...], own, (1, 0)).astype(BF16)
     r, c = r[:PASS], c[:PASS]
-    far = jnp.where((r == c - kept) & (c < live), 1.0, 0.0).astype(BF16)
-    out_ref[...] = (dot(y_ref[...], own, (1, 0)) + dot(got_ref[...], far, (1, 0))).astype(BF16)
+    far_ref[...] = jnp.where((r == c - kept) & (c < live), 1.0, 0.0).astype(BF16)
+
+
+def route_far(own_ref, far_ref, got_ref, out_ref):
+    out_ref[...] = (own_ref[...].astype(F32) + dot(got_ref[...], far_ref[...], (1, 0))).astype(BF16)
 
 
 def shards(x_work, norm_gain, w_qkv, w_out, cot_owned, counts):
@@ -342,12 +357,14 @@
         route_in,
         struct((GROWS, ROWS), BF16),
         ins=(HBM, HBM, HBM, HBM),
+        outs=HBM,
         scratch=(
             pltpu.VMEM((1, 128), jnp.int32),
             pltpu.VMEM((FX,), BF16),
             pltpu.VMEM((FX, ROWS), BF16),
             pltpu.VMEM((FX, SLOTS), BF16),
-            pltpu.SemaphoreType.DMA((4,)),
+            pltpu.VMEM((GROWS, ROWS), BF16),
+            pltpu.SemaphoreType.DMA((6,)),
         ),
         vmem_mib=61,
     )(counts, norm_gain, cot, got)
@@ -435,7 +452,12 @@
         ),
     )(heads, xt, cot_work, gain)
     got = lax.ppermute(send, DP, down)
-    y_owned = call(route_out, struct((FX, SLOTS), BF16))(counts, y_work, got)
+    own_slots, far = call(
+        route_own,
+        (struct((FX, SLOTS), BF16), struct((PASS, SLOTS), BF16)),
+        flops=500000000,
+    )(counts, y_work)
+    y_owned = call(route_far, struct((FX, SLOTS), BF16))(own_slots, far, got)
     return (y_owned.T, x_grad.T, qkv_grad.T, out_grad, gain_grad)
 
 

time: 142 us -> 141 us (level)
    pallas_call x2 -> x3, Pallas kernels: 4.14 us -> 4.26 us  [the longest x1 2.46 us: shards(): call(route_in, struct((GROWS, ROWS), BF16), ins=(HBM, HBM, HBM, HBM), out...]
  transfers between devices with their start and end apart: 9 -> 9, of which waited for: 4 -> 4; matrix products, arithmetic and copies ran while one was open for 0% -> 0% of each run, Pallas kernels for 5% -> 6%
where the time goes in v5:
time: 141 us
  blocking collectives  60.2 us (43%)
  starting transfers between devices  54 us (38%)
  Pallas kernels  15.8 us (11%)
  waiting for transfers between devices  9.95 us (7%)
    all_to_all x1, blocking collectives, shards(): parts = lax.all_to_all(parts, 'y', 0, 0)  14.7 us
    all_gather x1, blocking collectives, shards(): x_full = lax.all_gather(xt, 'x', axis=0, tiled=True)  13.2 us
    all_gather x1, blocking collectives, shards(): own = lax.all_gather(part, 'y', axis=0)  12.3 us
    all_gather x1, blocking collectives, shards(): g_full = lax.all_gather(cot_work, 'x', axis=0)  11.7 us
    ppermute x1, starting transfers between devices, shards(): got = lax.ppermute(send, 'c', cores)  10.4 us
    ppermute x1, starting transfers between devices, shards(): other = lax.ppermute(own, 'c', cores)  9.37 us
    ppermute x1, starting transfers between devices, shards(): got = lax.ppermute(part, 'zh', [(0, 1), (1, 0), (2, 3), (3, 2)])  8.81 us
    all_to_all x1, blocking collectives, shards(): parts = lax.all_to_all(parts, 'zl', 0, 0)  8.37 us
  transfers between devices with their start and end apart: 9, of which 4 were waited for; matrix products, arithmetic and copies ran while one was open for 0% of the time, Pallas kernels for 6%

profile of v5, /device:TPU:1, one launch (start us, length us, event | category | flops | bytes accessed | tf_op | source)
XLA Modules:
  0.0 140.8 jit_solution(3566163197871912613)
XLA Ops:
  0.6 0.0 copy-start.1
  0.6 0.0 copy-start.3
  0.7 4.7 %collective-permute-start = (bf16[320,704]{1,0:T(8,128)(2,1)}, bf16[320,704]{1,0:T(8,128)(2,1)}, u32[]{:S(2)}, u32[]{:S(2)}) collective-permute-start(bf16[320,704]{1,0:T(8,128)(2,1)} %bitcast.18), channel_id=1, source_target_pairs={{0,4},{4,8},{8,12},{12,16},{16,20},{20,24},{24,28},{28,32},{32,36}... | collective-permute-start | bytes 1351688 | tf_op jit(solution)/shard_map/ppermute | solution.py:354
  5.4 13.2 %all_gather.15.x_ref = bf16[1280,384]{1,0:T(8,128)(2,1)S(1)} all-gather(bf16[320,384]{1,0:T(8,128)(2,1)} %bitcast.14), channel_id=1, replica_groups=mesh['zh'=4,'zl'=4,'y'=4,'c'=2,'x'=4] {'x'}, dimensions={0}, use_global_device_ids=true | all-gather | bytes 1228800 | tf_op jit(solution)/shard_map/all_gather | solution.py:355
  18.6 0.0 collective-permute-done.got_hbm
  18.6 2.5 %shard_map.101.cot_ref = bf16[336,384]{1,0:T(8,128)(2,1)} custom-call(s32[1,128]{1,0:T(1,128)} %bitcast.16, bf16[320]{0:T(512)(128)(2,1)} %gain_hbm.1, bf16[320,704]{1,0:T(8,128)(2,1)} %bitcast.19, bf16[320,704]{1,0:T(8,128)(2,1)} %collective-permute-done.got_hbm), custom_call_target="tpu_custom_call" | custom-call | flops 1000000 | bytes 1000000 | tf_op jit(solution)/shard_map/pallas_call | solution.py:356
  21.1 11.7 %all-gather = bf16[1344,384]{1,0:T(8,128)(2,1)S(1)} all-gather(bf16[336,384]{1,0:T(8,128)(2,1)} %shard_map.101.cot_ref), channel_id=2, replica_groups=mesh['zh'=4,'zl'=4,'y'=4,'c'=2,'x'=4] {'x'}, dimensions={0}, use_global_device_ids=true | all-gather | bytes 1290240 | tf_op jit(solution)/shard_map/all_gather | solution.py:371
  32.8 0.0 copy-done.1
  32.8 0.0 copy-done.3
  32.8 3.9 %shard_map.102 = (bf16[16,25728]{1,0:T(8,128)(2,1)S(1)}, f32[640,1280]{1,0:T(8,128)S(1)}, f32[16,128]{1,0:T(8,128)S(1)}, bf16[480,384]{1,0:T(8,128)(2,1)S(1)}, b...) custom-call(bf16[1280,384]{1,0:T(8,128)(2,1)S(1)} %all_gather.15.x_ref, ...), custom_call_target="tpu_custom_call" | custom-call | flops 1500000000 | bytes 1000000 | tf_op jit(solution)/shard_map/pallas_call | solution.py:373
  36.7 10.4 %collective-permute-start.1 = (bf16[16,25728]{1,0:T(8,128)(2,1)S(1)}, bf16[16,25728]{1,0:T(8,128)(2,1)S(1)}, u32[]{:S(2)}, u32[]{:S(2)}) collective-permute-start(bf16[16,25728]{1,0:T(8,128)(2,1)S(1)} %get-tuple-element.24), channel_id=1, source_target_pairs={{0,4},{4,0},{1,5},{5,1},{2,6},{6,2},{3,7},{7,3},{8,12},{12,8},{9,1... | collective-permute-start | bytes 2469896 | tf_op jit(solution)/shard_map/ppermute | solution.py:394
  47.1 1.9 %collective-permute-done.1.got_ref = bf16[16,25728]{1,0:T(8,128)(2,1)S(1)} collective-permute-done((bf16[16,25728]{1,0:T(8,128)(2,1)S(1)}, bf16[16,25728]{1,0:T(8,128)(2,1)S(1)}, u32[]{:S(2)}, u32[]{:S(2)}) %collective-permute-start.1) | collective-permute-done | bytes 823328 | tf_op jit(solution)/shard_map/ppermute | solution.py:394
  49.1 0.1 shard_map.103
  49.2 14.7 %all_to_all.15.got_ref = bf16[4,16,6528]{2,1,0:T(8,128)(2,1)S(1)} all-to-all(bf16[4,16,6528]{2,1,0:T(8,128)(2,1)S(1)} %shard_map.103), channel_id=1, replica_groups=mesh['zh'=4,'zl'=4,'y'=4,'c'=2,'x'=4] {'y'}, dimensions={0} | all-to-all | bytes 1671168 | tf_op jit(solution)/shard_map/all_to_all | solution.py:410
  63.9 0.1 shard_map.104
  64.0 8.4 %all_to_all.16.got_ref = bf16[4,16,1792]{2,1,0:T(8,128)(2,1)S(1)} all-to-all(bf16[4,16,1792]{2,1,0:T(8,128)(2,1)S(1)} %shard_map.104), channel_id=1, replica_groups=mesh['zh'=4,'zl'=4,'y'=4,'c'=2,'x'=4] {'zl'}, dimensions={0} | all-to-all | bytes 458752 | tf_op jit(solution)/shard_map/all_to_all | solution.py:412
  72.4 8.8 %collective-permute-start.2 = (bf16[16,1792]{1,0:T(8,128)(2,1)S(1)}, bf16[16,1792]{1,0:T(8,128)(2,1)S(1)}, u32[]{:S(2)}, u32[]{:S(2)}) collective-permute-start(bf16[16,1792]{1,0:T(8,128)(2,1)S(1)} %shard_map.105.own_ref), channel_id=1, source_target_pairs={{0,128},{128,0},{256,384},{384,256},{1,129},{129,1},{257,385},{385... | collective-permute-start | bytes 172040 | tf_op jit(solution)/shard_map/ppermute | solution.py:414
  81.2 3.0 %shard_map.106.heads_ref.heads_in = bf16[4,656,384]{2,1,0:T(8,128)(2,1)} custom-call(bf16[480,384]{1,0:T(8,128)(2,1)S(1)} %get-tuple-element.25.gp_ref, bf16[160,384]{1,0:T(8,128)(2,1)S(1)} %get-tuple-element.26.mx_ref, bf16[1280,384]{1,0:T(8,128)(2,1)S(1)} %all_gather.15.x_ref, bf16[480,1280]{1,0:T(8,128)(2,1)S(1)} %bitcast.12, ...), custom_call_target="tpu_custom_call" | custom-call | flops 700000000 | bytes 1000000 | tf_op jit(solution)/shard_map/pallas_call | solution.py:396
  84.2 0.0 collective-permute-done.2.got_ref
  84.2 6.6 %collective-permute-start.3 = (bf16[16,1792]{1,0:T(8,128)(2,1)S(1)}, bf16[16,1792]{1,0:T(8,128)(2,1)S(1)}, u32[]{:S(2)}, u32[]{:S(2)}) collective-permute-start(bf16[16,1792]{1,0:T(8,128)(2,1)S(1)} %shard_map.107.own_ref), channel_id=1, source_target_pairs={{128,256},{256,128},{384,0},{0,384},{129,257},{257,129},{385,1},{1... | collective-permute-start | bytes 172040 | tf_op jit(solution)/shard_map/ppermute | solution.py:416
  90.9 2.3 %collective-permute-done.3.got_ref = bf16[16,1792]{1,0:T(8,128)(2,1)S(1)} collective-permute-done((bf16[16,1792]{1,0:T(8,128)(2,1)S(1)}, bf16[16,1792]{1,0:T(8,128)(2,1)S(1)}, u32[]{:S(2)}, u32[]{:S(2)}) %collective-permute-start.3) | collective-permute-done | bytes 57376 | tf_op jit(solution)/shard_map/ppermute | solution.py:416
  93.2 5.7 %collective-permute-start.5 = (bf16[16,1664]{1,0:T(8,128)(2,1)S(1)}, bf16[16,1664]{1,0:T(8,128)(2,1)S(1)}, u32[]{:S(2)}, u32[]{:S(2)}) collective-permute-start(bf16[16,1664]{1,0:T(8,128)(2,1)S(1)} %get-tuple-element.35.own_ref), channel_id=1, source_target_pairs={{0,96},{96,0},{32,64},{64,32},{1,97},{97,1},{33,65},{65,33},{2,98}... | collective-permute-start | bytes 159752 | tf_op jit(solution)/shard_map/ppermute | solution.py:418
  98.9 0.7 shard_map.109
  99.6 4.3 %all-to-all-start.2 = ((bf16[4,656,384]{2,1,0:T(8,128)(2,1)}), bf16[4,656,384]{2,1,0:T(8,128)(2,1)S(1)}, u32[]{:S(2)}, u32[]{:S(2)}) async-start(bf16[4,656,384]{2,1,0:T(8,128)(2,1)} %shard_map.109), calls=%async_computation.2 | async-start | bytes 4030464 | tf_op jit(solution)/shard_map/all_to_all | solution.py:427
  103.9 0.0 copy-start.5
  103.9 0.0 copy-start
  103.9 0.0 copy-start.2
  103.9 0.0 collective-permute-done.5.got_ref
  104.0 2.1 %collective-permute-start.6 = (bf16[2,16,1664]{2,1,0:T(8,128)(2,1)S(1)}, bf16[2,16,1664]{2,1,0:T(8,128)(2,1)S(1)}, u32[]{:S(2)}, u32[]{:S(2)}) collective-permute-start(bf16[2,16,1664]{2,1,0:T(8,128)(2,1)S(1)} %shard_map.113.own_ref), channel_id=1, source_target_pairs={{0,32},{32,0},{64,96},{96,64},{1,33},{33,1},{65,97},{97,65},{2,34}... | collective-permute-start | bytes 319496 | tf_op jit(solution)/shard_map/ppermute | solution.py:429
  106.0 3.5 %collective-permute-done.6.got_ref = bf16[2,16,1664]{2,1,0:T(8,128)(2,1)S(1)} collective-permute-done((bf16[2,16,1664]{2,1,0:T(8,128)(2,1)S(1)}, bf16[2,16,1664]{2,1,0:T(8,128)(2,1)S(1)}, u32[]{:S(2)}, u32[]{:S(2)}) %collective-permute-start.6) | collective-permute-done | bytes 106528 | tf_op jit(solution)/shard_map/ppermute | solution.py:429
  109.6 12.3 %all-gather.1 = bf16[64,6400]{1,0:T(8,128)(2,1)S(1)} all-gather(bf16[16,6400]{1,0:T(8,128)(2,1)S(1)} %shard_map.114), channel_id=3, replica_groups=mesh['zh'=4,'zl'=4,'y'=4,'c'=2,'x'=4] {'y'}, dimensions={0}, use_global_device_ids=true | all-gather | bytes 1024000 | tf_op jit(solution)/shard_map/all_gather | solution.py:431
  121.8 9.4 %collective-permute-start.7 = (bf16[4,16,6400]{2,1,0:T(8,128)(2,1)S(1)}, bf16[4,16,6400]{2,1,0:T(8,128)(2,1)}, u32[]{:S(2)}, u32[]{:S(2)}) collective-permute-start(bf16[4,16,6400]{2,1,0:T(8,128)(2,1)S(1)} %bitcast.9), channel_id=1, source_target_pairs={{0,4},{4,0},{1,5},{5,1},{2,6},{6,2},{3,7},{7,3},{8,12},{12,8},{9,1... | collective-permute-start | bytes 2457608 | tf_op jit(solution)/shard_map/ppermute | solution.py:432
  131.2 0.0 copy-done.5
  131.2 0.0 copy-start.4
  131.3 0.0 all-to-all-done.2.got_ref
  131.3 0.0 copy-done
  131.3 0.0 copy-done.2
  131.3 0.9 shard_map.110
  132.1 1.9 %collective-permute-start.4 = (bf16[320,320]{1,0:T(8,128)(2,1)S(1)}, bf16[320,320]{1,0:T(8,128)(2,1)S(1)}, u32[]{:S(2)}, u32[]{:S(2)}) collective-permute-start(bf16[320,320]{1,0:T(8,128)(2,1)S(1)} %get-tuple-element.33), channel_id=1, source_target_pairs={{4,0},{8,4},{12,8},{16,12},{20,16},{24,20},{28,24},{32,28},{36,32}... | collective-permute-start | bytes 614408 | tf_op jit(solution)/shard_map/ppermute | solution.py:454
  134.1 0.0 collective-permute-done.7.other_any
  134.1 2.7 %shard_map.115 = (f32[480,1280]{1,0:T(8,128)}, f32[160,1280]{1,0:T(8,128)}) custom-call(bf16[4,16,6400]{2,1,0:T(8,128)(2,1)S(1)} %bitcast.10, bf16[4,16,6400]{2,1,0:T(8,128)(2,1)} %collective-permute-done.7.other_any), custom_call_target="tpu_custom_call" | custom-call | flops 1000000 | bytes 1000000 | tf_op jit(solution)/shard_map/pallas_call | solution.py:433
  136.8 0.0 copy-done.4
  136.8 0.6 shard_map.111
  137.4 2.2 %collective-permute-done.4.got_ref = bf16[320,320]{1,0:T(8,128)(2,1)S(1)} collective-permute-done((bf16[320,320]{1,0:T(8,128)(2,1)S(1)}, bf16[320,320]{1,0:T(8,128)(2,1)S(1)}, u32[]{:S(2)}, u32[]{:S(2)}) %collective-permute-start.4) | collective-permute-done | bytes 204832 | tf_op jit(solution)/shard_map/ppermute | solution.py:454
  139.7 1.2 shard_map.112
  (6 shorter events, 0.1 us)
Async XLA Ops:
  0.6 32.2 %copy-start.1 = (bf16[1280,480]{0,1:T(8,128)(2,1)S(1)}, bf16[1280,480]{0,1:T(8,128)(2,1)}, u32[]{:S(2)}) copy-start(bf16[1280,480]{0,1:T(8,128)(2,1)} %param.8) | copy-start | bytes 3686404
  0.6 32.2 %copy-start.3 = (bf16[160,1280]{1,0:T(8,128)(2,1)S(1)}, bf16[160,1280]{1,0:T(8,128)(2,1)}, u32[]{:S(2)}) copy-start(bf16[160,1280]{1,0:T(8,128)(2,1)} %wo_ref.3) | copy-start | bytes 1228804
  0.7 18.0 %collective-permute-start = (bf16[320,704]{1,0:T(8,128)(2,1)}, bf16[320,704]{1,0:T(8,128)(2,1)}, u32[]{:S(2)}, u32[]{:S(2)}) collective-permute-start(bf16[320,704]{1,0:T(8,128)(2,1)} %bitcast.18), channel_id=1, source_target_pairs={{0,4},{4,8},{8,12},{12,16},{16,20},{20,24},{24,28},{28,32},{32,36}... | collective-permute-start | bytes 1351688 | tf_op jit(solution)/shard_map/ppermute | solution.py:354
  36.7 12.4 %collective-permute-start.1 = (bf16[16,25728]{1,0:T(8,128)(2,1)S(1)}, bf16[16,25728]{1,0:T(8,128)(2,1)S(1)}, u32[]{:S(2)}, u32[]{:S(2)}) collective-permute-start(bf16[16,25728]{1,0:T(8,128)(2,1)S(1)} %get-tuple-element.24), channel_id=1, source_target_pairs={{0,4},{4,0},{1,5},{5,1},{2,6},{6,2},{3,7},{7,3},{8,12},{12,8},{9,1... | collective-permute-start | bytes 2469896 | tf_op jit(solution)/shard_map/ppermute | solution.py:394
  72.4 11.8 %collective-permute-start.2 = (bf16[16,1792]{1,0:T(8,128)(2,1)S(1)}, bf16[16,1792]{1,0:T(8,128)(2,1)S(1)}, u32[]{:S(2)}, u32[]{:S(2)}) collective-permute-start(bf16[16,1792]{1,0:T(8,128)(2,1)S(1)} %shard_map.105.own_ref), channel_id=1, source_target_pairs={{0,128},{128,0},{256,384},{384,256},{1,129},{129,1},{257,385},{385... | collective-permute-start | bytes 172040 | tf_op jit(solution)/shard_map/ppermute | solution.py:414
  84.2 8.9 %collective-permute-start.3 = (bf16[16,1792]{1,0:T(8,128)(2,1)S(1)}, bf16[16,1792]{1,0:T(8,128)(2,1)S(1)}, u32[]{:S(2)}, u32[]{:S(2)}) collective-permute-start(bf16[16,1792]{1,0:T(8,128)(2,1)S(1)} %shard_map.107.own_ref), channel_id=1, source_target_pairs={{128,256},{256,128},{384,0},{0,384},{129,257},{257,129},{385,1},{1... | collective-permute-start | bytes 172040 | tf_op jit(solution)/shard_map/ppermute | solution.py:416
  93.2 10.8 %collective-permute-start.5 = (bf16[16,1664]{1,0:T(8,128)(2,1)S(1)}, bf16[16,1664]{1,0:T(8,128)(2,1)S(1)}, u32[]{:S(2)}, u32[]{:S(2)}) collective-permute-start(bf16[16,1664]{1,0:T(8,128)(2,1)S(1)} %get-tuple-element.35.own_ref), channel_id=1, source_target_pairs={{0,96},{96,0},{32,64},{64,32},{1,97},{97,1},{33,65},{65,33},{2,98}... | collective-permute-start | bytes 159752 | tf_op jit(solution)/shard_map/ppermute | solution.py:418
  99.6 31.6 %all-to-all-start.2 = ((bf16[4,656,384]{2,1,0:T(8,128)(2,1)}), bf16[4,656,384]{2,1,0:T(8,128)(2,1)S(1)}, u32[]{:S(2)}, u32[]{:S(2)}) async-start(bf16[4,656,384]{2,1,0:T(8,128)(2,1)} %shard_map.109), calls=%async_computation.2 | async-start | bytes 4030464 | tf_op jit(solution)/shard_map/all_to_all | solution.py:427
  103.9 27.3 %copy-start.5 = (bf16[320]{0:T(512)(128)(2,1)S(1)}, bf16[320]{0:T(512)(128)(2,1)}, u32[]{:S(2)}) copy-start(bf16[320]{0:T(512)(128)(2,1)} %gain_hbm.1) | copy-start | bytes 1924
  103.9 27.3 %copy-start = (bf16[336,384]{1,0:T(8,128)(2,1)S(1)}, bf16[336,384]{1,0:T(8,128)(2,1)}, u32[]{:S(2)}) copy-start(bf16[336,384]{1,0:T(8,128)(2,1)} %shard_map.101.cot_ref) | copy-start | bytes 774148
  103.9 27.3 %copy-start.2 = (bf16[384,320]{0,1:T(8,128)(2,1)S(1)}, bf16[384,320]{0,1:T(8,128)(2,1)}, u32[]{:S(2)}) copy-start(bf16[384,320]{0,1:T(8,128)(2,1)} %param.6) | copy-start | bytes 737284
  104.0 5.6 %collective-permute-start.6 = (bf16[2,16,1664]{2,1,0:T(8,128)(2,1)S(1)}, bf16[2,16,1664]{2,1,0:T(8,128)(2,1)S(1)}, u32[]{:S(2)}, u32[]{:S(2)}) collective-permute-start(bf16[2,16,1664]{2,1,0:T(8,128)(2,1)S(1)} %shard_map.113.own_ref), channel_id=1, source_target_pairs={{0,32},{32,0},{64,96},{96,64},{1,33},{33,1},{65,97},{97,65},{2,34}... | collective-permute-start | bytes 319496 | tf_op jit(solution)/shard_map/ppermute | solution.py:429
  121.8 12.2 %collective-permute-start.7 = (bf16[4,16,6400]{2,1,0:T(8,128)(2,1)S(1)}, bf16[4,16,6400]{2,1,0:T(8,128)(2,1)}, u32[]{:S(2)}, u32[]{:S(2)}) collective-permute-start(bf16[4,16,6400]{2,1,0:T(8,128)(2,1)S(1)} %bitcast.9), channel_id=1, source_target_pairs={{0,4},{4,0},{1,5},{5,1},{2,6},{6,2},{3,7},{7,3},{8,12},{12,8},{9,1... | collective-permute-start | bytes 2457608 | tf_op jit(solution)/shard_map/ppermute | solution.py:432
  131.2 5.6 %copy-start.4 = (s32[128]{0:T(128)S(1)}, s32[128]{0:T(128)}, u32[]{:S(2)}) copy-start(s32[128]{0:T(128)} %param.11) | copy-start | bytes 1540
  132.1 7.5 %collective-permute-start.4 = (bf16[320,320]{1,0:T(8,128)(2,1)S(1)}, bf16[320,320]{1,0:T(8,128)(2,1)S(1)}, u32[]{:S(2)}, u32[]{:S(2)}) collective-permute-start(bf16[320,320]{1,0:T(8,128)(2,1)S(1)} %get-tuple-element.33), channel_id=1, source_target_pairs={{4,0},{8,4},{12,8},{16,12},{20,16},{24,20},{28,24},{32,28},{36,32}... | collective-permute-start | bytes 614408 | tf_op jit(solution)/shard_map/ppermute | solution.py:454

commit v6 on v5

--- a/solution.py
+++ b/solution.py
@@ -309,15 +309,19 @@
         pltpu.make_async_copy(buf.at[pl.ds(80 * n, 80)], qkv_ref.at[pl.ds(0, 80)], sems.at[n]).wait()
 
 
-def heads_sum(got_ref, x_ref, cot_ref, gain_ref, y_ref, send_ref, grad_ref, gain_grad_ref):
+def y_heads(got_ref, x_ref, y_ref, send_ref):
     for i in range(5):
         s = slice(64 * i, 64 * (i + 1))
-        t = slice(FX + 64 * i, FX + 64 * (i + 1))
         a, b, c, d = (got_ref[j, s, :].astype(F32) for j in range(4))
         y = (x_ref[s, :].astype(F32) + ((a + b) + (c + d))).astype(BF16)
         y_ref[s, :] = y
         send_ref[s, :] = y[:, :PASS]
-        a, b, c, d = (got_ref[j, t, :].astype(F32) for j in range(4))
+
+
+def x_heads(got_ref, cot_ref, gain_ref, grad_ref, gain_grad_ref):
+    for i in range(5):
+        s = slice(64 * i, 64 * (i + 1))
+        a, b, c, d = (got_ref[j, FX + 64 * i:FX + 64 * (i + 1), :].astype(F32) for j in range(4))
         grad_ref[s, :] = (cot_ref[s, :].astype(F32) + ((a + b) + (c + d))).astype(BF16)
     a, b, c, d = (got_ref[j, 2 * FX:, :].astype(F32) for j in range(4))
     line = jnp.sum((a + b) + (c + d), axis=0, keepdims=True)
@@ -442,16 +446,13 @@
         ),
     )(own, other)
 
-    y_work, send, x_grad, gain_grad = call(
-        heads_sum,
-        (
-            struct((FX, ROWS), BF16),
-            struct((FX, PASS), BF16),
-            struct((FX, ROWS), BF16),
-            struct((FX,), F32),
-        ),
-    )(heads, xt, cot_work, gain)
+    y_work, send = call(y_heads, (struct((FX, ROWS), BF16), struct((FX, PASS), BF16)))(heads, xt)
     got = lax.ppermute(send, DP, down)
+    x_grad, gain_grad = call(
+        x_heads,
+        (struct((FX, ROWS), BF16), struct((FX,), F32)),
+        flops=500000000,
+    )(heads, cot_work, gain)
     own_slots, far = call(
         route_own,
         (struct((FX, SLOTS), BF16), struct((PASS, SLOTS), BF16)),

time: 141 us -> 141 us (level)
  no operation moved by 1% of the time
where the time goes in v6:
time: 141 us; the launch traced here: 140 us
  blocking collectives  60.2 us (43%)
  starting transfers between devices  54.3 us (39%)
  Pallas kernels  15.9 us (11%)
  waiting for transfers between devices  9.05 us (6%)
    all_to_all x1, blocking collectives, shards(): parts = lax.all_to_all(parts, 'y', 0, 0)  14.7 us
    all_gather x1, blocking collectives, shards(): x_full = lax.all_gather(xt, 'x', axis=0, tiled=True)  13.2 us
    all_gather x1, blocking collectives, shards(): own = lax.all_gather(part, 'y', axis=0)  12.3 us
    all_gather x1, blocking collectives, shards(): g_full = lax.all_gather(cot_work, 'x', axis=0)  11.7 us
    ppermute x1, starting transfers between devices, shards(): got = lax.ppermute(send, 'c', cores)  10.4 us
    ppermute x1, starting transfers between devices, shards(): other = lax.ppermute(own, 'c', cores)  9.51 us
    ppermute x1, starting transfers between devices, shards(): got = lax.ppermute(part, 'zh', [(0, 1), (1, 0), (2, 3), (3, 2)])  8.81 us
    all_to_all x1, blocking collectives, shards(): parts = lax.all_to_all(parts, 'zl', 0, 0)  8.37 us
  transfers between devices with their start and end apart: 9, of which 4 were waited for; matrix products, arithmetic and copies ran while one was open for 0% of the time, Pallas kernels for 6%

profile of v6, /device:TPU:1, one launch (start us, length us, event | category | flops | bytes accessed | tf_op | source)
XLA Modules:
  0.0 140.4 jit_solution(13470113257209933881)
XLA Ops:
  0.6 0.0 copy-start.1
  0.6 0.0 copy-start.3
  0.7 4.7 %collective-permute-start = (bf16[320,704]{1,0:T(8,128)(2,1)}, bf16[320,704]{1,0:T(8,128)(2,1)}, u32[]{:S(2)}, u32[]{:S(2)}) collective-permute-start(bf16[320,704]{1,0:T(8,128)(2,1)} %bitcast.18), channel_id=1, source_target_pairs={{0,4},{4,8},{8,12},{12,16},{16,20},{20,24},{24,28},{28,32},{32,36}... | collective-permute-start | bytes 1351688 | tf_op jit(solution)/shard_map/ppermute | solution.py:358
  5.4 13.2 %all_gather.15.x_ref = bf16[1280,384]{1,0:T(8,128)(2,1)S(1)} all-gather(bf16[320,384]{1,0:T(8,128)(2,1)} %bitcast.14), channel_id=1, replica_groups=mesh['zh'=4,'zl'=4,'y'=4,'c'=2,'x'=4] {'x'}, dimensions={0}, use_global_device_ids=true | all-gather | bytes 1228800 | tf_op jit(solution)/shard_map/all_gather | solution.py:359
  18.6 0.0 collective-permute-done.got_hbm
  18.6 2.5 %shard_map.101.cot_ref = bf16[336,384]{1,0:T(8,128)(2,1)} custom-call(s32[1,128]{1,0:T(1,128)} %bitcast.16, bf16[320]{0:T(512)(128)(2,1)} %gain_hbm.1, bf16[320,704]{1,0:T(8,128)(2,1)} %bitcast.19, bf16[320,704]{1,0:T(8,128)(2,1)} %collective-permute-done.got_hbm), custom_call_target="tpu_custom_call" | custom-call | flops 1000000 | bytes 1000000 | tf_op jit(solution)/shard_map/pallas_call | solution.py:360
  21.1 11.7 %all-gather = bf16[1344,384]{1,0:T(8,128)(2,1)S(1)} all-gather(bf16[336,384]{1,0:T(8,128)(2,1)} %shard_map.101.cot_ref), channel_id=2, replica_groups=mesh['zh'=4,'zl'=4,'y'=4,'c'=2,'x'=4] {'x'}, dimensions={0}, use_global_device_ids=true | all-gather | bytes 1290240 | tf_op jit(solution)/shard_map/all_gather | solution.py:375
  32.8 0.0 copy-done.1
  32.8 0.0 copy-done.3
  32.8 3.9 %shard_map.102 = (bf16[16,25728]{1,0:T(8,128)(2,1)S(1)}, f32[640,1280]{1,0:T(8,128)S(1)}, f32[16,128]{1,0:T(8,128)S(1)}, bf16[480,384]{1,0:T(8,128)(2,1)S(1)}, b...) custom-call(bf16[1280,384]{1,0:T(8,128)(2,1)S(1)} %all_gather.15.x_ref, ...), custom_call_target="tpu_custom_call" | custom-call | flops 1500000000 | bytes 1000000 | tf_op jit(solution)/shard_map/pallas_call | solution.py:377
  36.7 10.4 %collective-permute-start.1 = (bf16[16,25728]{1,0:T(8,128)(2,1)S(1)}, bf16[16,25728]{1,0:T(8,128)(2,1)S(1)}, u32[]{:S(2)}, u32[]{:S(2)}) collective-permute-start(bf16[16,25728]{1,0:T(8,128)(2,1)S(1)} %get-tuple-element.24), channel_id=1, source_target_pairs={{0,4},{4,0},{1,5},{5,1},{2,6},{6,2},{3,7},{7,3},{8,12},{12,8},{9,1... | collective-permute-start | bytes 2469896 | tf_op jit(solution)/shard_map/ppermute | solution.py:398
  47.1 1.9 %collective-permute-done.1.got_ref = bf16[16,25728]{1,0:T(8,128)(2,1)S(1)} collective-permute-done((bf16[16,25728]{1,0:T(8,128)(2,1)S(1)}, bf16[16,25728]{1,0:T(8,128)(2,1)S(1)}, u32[]{:S(2)}, u32[]{:S(2)}) %collective-permute-start.1) | collective-permute-done | bytes 823328 | tf_op jit(solution)/shard_map/ppermute | solution.py:398
  49.1 0.1 shard_map.103
  49.2 14.7 %all_to_all.15.got_ref = bf16[4,16,6528]{2,1,0:T(8,128)(2,1)S(1)} all-to-all(bf16[4,16,6528]{2,1,0:T(8,128)(2,1)S(1)} %shard_map.103), channel_id=1, replica_groups=mesh['zh'=4,'zl'=4,'y'=4,'c'=2,'x'=4] {'y'}, dimensions={0} | all-to-all | bytes 1671168 | tf_op jit(solution)/shard_map/all_to_all | solution.py:414
  63.9 0.1 shard_map.104
  64.0 8.4 %all_to_all.16.got_ref = bf16[4,16,1792]{2,1,0:T(8,128)(2,1)S(1)} all-to-all(bf16[4,16,1792]{2,1,0:T(8,128)(2,1)S(1)} %shard_map.104), channel_id=1, replica_groups=mesh['zh'=4,'zl'=4,'y'=4,'c'=2,'x'=4] {'zl'}, dimensions={0} | all-to-all | bytes 458752 | tf_op jit(solution)/shard_map/all_to_all | solution.py:416
  72.4 8.8 %collective-permute-start.2 = (bf16[16,1792]{1,0:T(8,128)(2,1)S(1)}, bf16[16,1792]{1,0:T(8,128)(2,1)S(1)}, u32[]{:S(2)}, u32[]{:S(2)}) collective-permute-start(bf16[16,1792]{1,0:T(8,128)(2,1)S(1)} %shard_map.105.own_ref), channel_id=1, source_target_pairs={{0,128},{128,0},{256,384},{384,256},{1,129},{129,1},{257,385},{385... | collective-permute-start | bytes 172040 | tf_op jit(solution)/shard_map/ppermute | solution.py:418
  81.2 3.0 %shard_map.106.heads_ref.heads_in = bf16[4,656,384]{2,1,0:T(8,128)(2,1)} custom-call(bf16[480,384]{1,0:T(8,128)(2,1)S(1)} %get-tuple-element.25.gp_ref, bf16[160,384]{1,0:T(8,128)(2,1)S(1)} %get-tuple-element.26.mx_ref, bf16[1280,384]{1,0:T(8,128)(2,1)S(1)} %all_gather.15.x_ref, bf16[480,1280]{1,0:T(8,128)(2,1)S(1)} %bitcast.12, ...), custom_call_target="tpu_custom_call" | custom-call | flops 700000000 | bytes 1000000 | tf_op jit(solution)/shard_map/pallas_call | solution.py:400
  84.2 0.0 collective-permute-done.2.got_ref
  84.2 6.6 %collective-permute-start.3 = (bf16[16,1792]{1,0:T(8,128)(2,1)S(1)}, bf16[16,1792]{1,0:T(8,128)(2,1)S(1)}, u32[]{:S(2)}, u32[]{:S(2)}) collective-permute-start(bf16[16,1792]{1,0:T(8,128)(2,1)S(1)} %shard_map.107.own_ref), channel_id=1, source_target_pairs={{128,256},{256,128},{384,0},{0,384},{129,257},{257,129},{385,1},{1... | collective-permute-start | bytes 172040 | tf_op jit(solution)/shard_map/ppermute | solution.py:420
  90.9 2.3 %collective-permute-done.3.got_ref = bf16[16,1792]{1,0:T(8,128)(2,1)S(1)} collective-permute-done((bf16[16,1792]{1,0:T(8,128)(2,1)S(1)}, bf16[16,1792]{1,0:T(8,128)(2,1)S(1)}, u32[]{:S(2)}, u32[]{:S(2)}) %collective-permute-start.3) | collective-permute-done | bytes 57376 | tf_op jit(solution)/shard_map/ppermute | solution.py:420
  93.2 5.7 %collective-permute-start.5 = (bf16[16,1664]{1,0:T(8,128)(2,1)S(1)}, bf16[16,1664]{1,0:T(8,128)(2,1)S(1)}, u32[]{:S(2)}, u32[]{:S(2)}) collective-permute-start(bf16[16,1664]{1,0:T(8,128)(2,1)S(1)} %get-tuple-element.35.own_ref), channel_id=1, source_target_pairs={{0,96},{96,0},{32,64},{64,32},{1,97},{97,1},{33,65},{65,33},{2,98}... | collective-permute-start | bytes 159752 | tf_op jit(solution)/shard_map/ppermute | solution.py:422
  98.9 0.7 shard_map.109
  99.6 4.3 %all-to-all-start.2 = ((bf16[4,656,384]{2,1,0:T(8,128)(2,1)}), bf16[4,656,384]{2,1,0:T(8,128)(2,1)S(1)}, u32[]{:S(2)}, u32[]{:S(2)}) async-start(bf16[4,656,384]{2,1,0:T(8,128)(2,1)} %shard_map.109), calls=%async_computation.2 | async-start | bytes 4030464 | tf_op jit(solution)/shard_map/all_to_all | solution.py:431
  103.9 0.0 copy-start.2
  103.9 0.0 collective-permute-done.5.got_ref
  104.0 0.0 copy-start.5
  104.0 2.1 %collective-permute-start.6 = (bf16[2,16,1664]{2,1,0:T(8,128)(2,1)S(1)}, bf16[2,16,1664]{2,1,0:T(8,128)(2,1)S(1)}, u32[]{:S(2)}, u32[]{:S(2)}) collective-permute-start(bf16[2,16,1664]{2,1,0:T(8,128)(2,1)S(1)} %shard_map.114.own_ref), channel_id=1, source_target_pairs={{0,32},{32,0},{64,96},{96,64},{1,33},{33,1},{65,97},{97,65},{2,34}... | collective-permute-start | bytes 319496 | tf_op jit(solution)/shard_map/ppermute | solution.py:433
  106.0 3.5 %collective-permute-done.6.got_ref = bf16[2,16,1664]{2,1,0:T(8,128)(2,1)S(1)} collective-permute-done((bf16[2,16,1664]{2,1,0:T(8,128)(2,1)S(1)}, bf16[2,16,1664]{2,1,0:T(8,128)(2,1)S(1)}, u32[]{:S(2)}, u32[]{:S(2)}) %collective-permute-start.6) | collective-permute-done | bytes 106528 | tf_op jit(solution)/shard_map/ppermute | solution.py:433
  109.6 12.3 %all-gather.1 = bf16[64,6400]{1,0:T(8,128)(2,1)S(1)} all-gather(bf16[16,6400]{1,0:T(8,128)(2,1)S(1)} %shard_map.115), channel_id=3, replica_groups=mesh['zh'=4,'zl'=4,'y'=4,'c'=2,'x'=4] {'y'}, dimensions={0}, use_global_device_ids=true | all-gather | bytes 1024000 | tf_op jit(solution)/shard_map/all_gather | solution.py:435
  121.8 0.0 copy-start.4
  121.8 9.5 %collective-permute-start.7 = (bf16[4,16,6400]{2,1,0:T(8,128)(2,1)S(1)}, bf16[4,16,6400]{2,1,0:T(8,128)(2,1)}, u32[]{:S(2)}, u32[]{:S(2)}) collective-permute-start(bf16[4,16,6400]{2,1,0:T(8,128)(2,1)S(1)} %bitcast.9), channel_id=1, source_target_pairs={{0,4},{4,0},{1,5},{5,1},{2,6},{6,2},{3,7},{7,3},{8,12},{12,8},{9,1... | collective-permute-start | bytes 2457608 | tf_op jit(solution)/shard_map/ppermute | solution.py:436
  131.4 0.0 all-to-all-done.2.got_ref
  131.4 0.0 copy-done.2
  131.4 0.2 shard_map.110
  131.5 0.0 copy-start
  131.6 2.1 %collective-permute-start.4 = (bf16[320,320]{1,0:T(8,128)(2,1)S(1)}, bf16[320,320]{1,0:T(8,128)(2,1)S(1)}, u32[]{:S(2)}, u32[]{:S(2)}) collective-permute-start(bf16[320,320]{1,0:T(8,128)(2,1)S(1)} %get-tuple-element.33), channel_id=1, source_target_pairs={{4,0},{8,4},{12,8},{16,12},{20,16},{24,20},{28,24},{32,28},{36,32}... | collective-permute-start | bytes 614408 | tf_op jit(solution)/shard_map/ppermute | solution.py:450
  133.6 0.0 copy-done.5
  133.6 0.0 collective-permute-done.7.other_any
  133.6 2.7 %shard_map.116 = (f32[480,1280]{1,0:T(8,128)}, f32[160,1280]{1,0:T(8,128)}) custom-call(bf16[4,16,6400]{2,1,0:T(8,128)(2,1)S(1)} %bitcast.10, bf16[4,16,6400]{2,1,0:T(8,128)(2,1)} %collective-permute-done.7.other_any), custom_call_target="tpu_custom_call" | custom-call | flops 1000000 | bytes 1000000 | tf_op jit(solution)/shard_map/pallas_call | solution.py:437
  136.4 0.0 copy-done.4
  136.4 0.6 shard_map.111
  137.0 0.0 copy-done
  137.0 0.9 shard_map.113
  137.9 1.3 collective-permute-done.4.got_ref
  139.2 1.2 shard_map.112
  (6 shorter events, 0.1 us)
Async XLA Ops:
  0.6 32.2 %copy-start.1 = (bf16[1280,480]{0,1:T(8,128)(2,1)S(1)}, bf16[1280,480]{0,1:T(8,128)(2,1)}, u32[]{:S(2)}) copy-start(bf16[1280,480]{0,1:T(8,128)(2,1)} %param.8) | copy-start | bytes 3686404
  0.6 32.2 %copy-start.3 = (bf16[160,1280]{1,0:T(8,128)(2,1)S(1)}, bf16[160,1280]{1,0:T(8,128)(2,1)}, u32[]{:S(2)}) copy-start(bf16[160,1280]{1,0:T(8,128)(2,1)} %wo_ref.3) | copy-start | bytes 1228804
  0.7 18.0 %collective-permute-start = (bf16[320,704]{1,0:T(8,128)(2,1)}, bf16[320,704]{1,0:T(8,128)(2,1)}, u32[]{:S(2)}, u32[]{:S(2)}) collective-permute-start(bf16[320,704]{1,0:T(8,128)(2,1)} %bitcast.18), channel_id=1, source_target_pairs={{0,4},{4,8},{8,12},{12,16},{16,20},{20,24},{24,28},{28,32},{32,36}... | collective-permute-start | bytes 1351688 | tf_op jit(solution)/shard_map/ppermute | solution.py:358
  36.7 12.4 %collective-permute-start.1 = (bf16[16,25728]{1,0:T(8,128)(2,1)S(1)}, bf16[16,25728]{1,0:T(8,128)(2,1)S(1)}, u32[]{:S(2)}, u32[]{:S(2)}) collective-permute-start(bf16[16,25728]{1,0:T(8,128)(2,1)S(1)} %get-tuple-element.24), channel_id=1, source_target_pairs={{0,4},{4,0},{1,5},{5,1},{2,6},{6,2},{3,7},{7,3},{8,12},{12,8},{9,1... | collective-permute-start | bytes 2469896 | tf_op jit(solution)/shard_map/ppermute | solution.py:398
  72.4 11.8 %collective-permute-start.2 = (bf16[16,1792]{1,0:T(8,128)(2,1)S(1)}, bf16[16,1792]{1,0:T(8,128)(2,1)S(1)}, u32[]{:S(2)}, u32[]{:S(2)}) collective-permute-start(bf16[16,1792]{1,0:T(8,128)(2,1)S(1)} %shard_map.105.own_ref), channel_id=1, source_target_pairs={{0,128},{128,0},{256,384},{384,256},{1,129},{129,1},{257,385},{385... | collective-permute-start | bytes 172040 | tf_op jit(solution)/shard_map/ppermute | solution.py:418
  84.2 8.9 %collective-permute-start.3 = (bf16[16,1792]{1,0:T(8,128)(2,1)S(1)}, bf16[16,1792]{1,0:T(8,128)(2,1)S(1)}, u32[]{:S(2)}, u32[]{:S(2)}) collective-permute-start(bf16[16,1792]{1,0:T(8,128)(2,1)S(1)} %shard_map.107.own_ref), channel_id=1, source_target_pairs={{128,256},{256,128},{384,0},{0,384},{129,257},{257,129},{385,1},{1... | collective-permute-start | bytes 172040 | tf_op jit(solution)/shard_map/ppermute | solution.py:420
  93.2 10.8 %collective-permute-start.5 = (bf16[16,1664]{1,0:T(8,128)(2,1)S(1)}, bf16[16,1664]{1,0:T(8,128)(2,1)S(1)}, u32[]{:S(2)}, u32[]{:S(2)}) collective-permute-start(bf16[16,1664]{1,0:T(8,128)(2,1)S(1)} %get-tuple-element.35.own_ref), channel_id=1, source_target_pairs={{0,96},{96,0},{32,64},{64,32},{1,97},{97,1},{33,65},{65,33},{2,98}... | collective-permute-start | bytes 159752 | tf_op jit(solution)/shard_map/ppermute | solution.py:422
  99.6 31.7 %all-to-all-start.2 = ((bf16[4,656,384]{2,1,0:T(8,128)(2,1)}), bf16[4,656,384]{2,1,0:T(8,128)(2,1)S(1)}, u32[]{:S(2)}, u32[]{:S(2)}) async-start(bf16[4,656,384]{2,1,0:T(8,128)(2,1)} %shard_map.109), calls=%async_computation.2 | async-start | bytes 4030464 | tf_op jit(solution)/shard_map/all_to_all | solution.py:431
  103.9 27.4 %copy-start.2 = (bf16[384,320]{0,1:T(8,128)(2,1)S(1)}, bf16[384,320]{0,1:T(8,128)(2,1)}, u32[]{:S(2)}) copy-start(bf16[384,320]{0,1:T(8,128)(2,1)} %param.6) | copy-start | bytes 737284
  104.0 29.6 %copy-start.5 = (bf16[320]{0:T(512)(128)(2,1)S(1)}, bf16[320]{0:T(512)(128)(2,1)}, u32[]{:S(2)}) copy-start(bf16[320]{0:T(512)(128)(2,1)} %gain_hbm.1) | copy-start | bytes 1924
  104.0 5.6 %collective-permute-start.6 = (bf16[2,16,1664]{2,1,0:T(8,128)(2,1)S(1)}, bf16[2,16,1664]{2,1,0:T(8,128)(2,1)S(1)}, u32[]{:S(2)}, u32[]{:S(2)}) collective-permute-start(bf16[2,16,1664]{2,1,0:T(8,128)(2,1)S(1)} %shard_map.114.own_ref), channel_id=1, source_target_pairs={{0,32},{32,0},{64,96},{96,64},{1,33},{33,1},{65,97},{97,65},{2,34}... | collective-permute-start | bytes 319496 | tf_op jit(solution)/shard_map/ppermute | solution.py:433
  121.8 14.6 %copy-start.4 = (s32[128]{0:T(128)S(1)}, s32[128]{0:T(128)}, u32[]{:S(2)}) copy-start(s32[128]{0:T(128)} %param.11) | copy-start | bytes 1540
  121.8 11.8 %collective-permute-start.7 = (bf16[4,16,6400]{2,1,0:T(8,128)(2,1)S(1)}, bf16[4,16,6400]{2,1,0:T(8,128)(2,1)}, u32[]{:S(2)}, u32[]{:S(2)}) collective-permute-start(bf16[4,16,6400]{2,1,0:T(8,128)(2,1)S(1)} %bitcast.9), channel_id=1, source_target_pairs={{0,4},{4,0},{1,5},{5,1},{2,6},{6,2},{3,7},{7,3},{8,12},{12,8},{9,1... | collective-permute-start | bytes 2457608 | tf_op jit(solution)/shard_map/ppermute | solution.py:436
  131.5 5.5 %copy-start = (bf16[336,384]{1,0:T(8,128)(2,1)S(1)}, bf16[336,384]{1,0:T(8,128)(2,1)}, u32[]{:S(2)}) copy-start(bf16[336,384]{1,0:T(8,128)(2,1)} %shard_map.101.cot_ref) | copy-start | bytes 774148
  131.6 7.6 %collective-permute-start.4 = (bf16[320,320]{1,0:T(8,128)(2,1)S(1)}, bf16[320,320]{1,0:T(8,128)(2,1)S(1)}, u32[]{:S(2)}, u32[]{:S(2)}) collective-permute-start(bf16[320,320]{1,0:T(8,128)(2,1)S(1)} %get-tuple-element.33), channel_id=1, source_target_pairs={{4,0},{8,4},{12,8},{16,12},{20,16},{24,20},{28,24},{32,28},{36,32}... | collective-permute-start | bytes 614408 | tf_op jit(solution)/shard_map/ppermute | solution.py:450
